TPU v7x, 32 devices: a whole 2x2x4 slice. The times are simulated.
32 devices in a mesh: grp: 8 (over y, x, core), blk: 4 (over z).
Axes of the slice: x: 2, y: 2, z: 4, core: 2. Of those that a mesh axis runs over, the one named last changes fastest.
Arguments:
- tiles_near: bfloat16 [1024, 256, 256], P(('grp', 'blk')), may hold values from -0.09375 to 0.09375
- near_cols: int32 [32, 32], P(('grp', 'blk')), may hold values from 0 to 3
- tiles_far: bfloat16 [768, 256, 256], P(('grp', 'blk')), may hold values from -0.09375 to 0.09375
- far_groups: int32 [32, 24], P(('grp', 'blk')), may hold values from 0 to 7, as said below
- need_blocks: int32 [32, 8], P(('grp', 'blk')), may hold values from -1 to 3, as said below
- start_vectors: bfloat16 [32768, 128], P(('grp', 'blk')), may hold values from -6 to 6
Outputs:
- vectors: float32 [32768, 128], P(('grp', 'blk'))
Inputs may be any that keep to these rules, and one draw needn't show every extreme that they name: need_blocks[d, h] is -1 for d's own group and for groups d reads nothing from, else a row block index below 4 of the device of group h at d's position along blk; every device reads from at least one other group. far_groups[d, t] is a group h with need_blocks[d, h] >= 0.
All inputs are finite; a program needn't handle non-finite values.
Results may differ from a plain program's by a relative error of at most 0.0029.
Values may be sent and summed in bfloat16 or wider, within the bound.
No kernel may reach another device: no remote copies, remote signals or barrier semaphores. Data moves between devices by JAX's collectives and lax.ppermute only.
A program may use at most 128 MiB of HBM per device.

v0:
```python
import jax
import jax.numpy as jnp
from jax import lax
from jax.sharding import PartitionSpec as P

ITERS = 2


def per_device(tiles_near, near_cols, tiles_far, far_groups, need_blocks, start_vectors):
    tile_size = tiles_near.shape[1]
    vec_width = start_vectors.shape[1]
    blocks = start_vectors.shape[0] // tile_size
    group_size = lax.axis_size("blk")
    group_count = lax.axis_size("grp")
    per_source = tiles_near.shape[0] // (blocks * group_size)
    far_each = tiles_far.shape[0] // blocks
    near_tiles = tiles_near.reshape(blocks, group_size, per_source, tile_size, tile_size)
    near_index = near_cols.reshape(blocks, group_size, per_source)
    far_tiles = tiles_far.reshape(blocks, far_each, tile_size, tile_size)
    far_index = far_groups.reshape(blocks, far_each)
    wanted = need_blocks.reshape(group_count)
    total_rows = blocks * tile_size * group_size * group_count
    current = start_vectors
    vectors = start_vectors.astype(jnp.float32)
    for iteration in range(ITERS):
        local_rows = current.reshape(blocks, tile_size, vec_width)
        group_table = lax.all_gather(local_rows, "blk", axis=0, tiled=True)
        source_ids = jnp.arange(group_size, dtype=jnp.int32)[None, :, None]
        chosen = group_table[source_ids * blocks + near_index]
        near_part = jnp.einsum(
            "rmnij,rmnjk->rik", near_tiles, chosen, preferred_element_type=jnp.float32
        )
        everything = lax.all_gather(local_rows, "grp", axis=0, tiled=True)
        far_rows = everything[far_index * blocks + wanted[far_index]]
        far_part = jnp.einsum(
            "rnij,rnjk->rik", far_tiles, far_rows, preferred_element_type=jnp.float32
        )
        product = near_part + far_part
        flat_rows = product.reshape(blocks * tile_size, vec_width)
        local_gram = jnp.dot(
            flat_rows.T,
            flat_rows,
            precision=lax.Precision.HIGHEST,
            preferred_element_type=jnp.float32,
        )
        gram = lax.psum(local_gram, ("grp", "blk")) / total_rows
        factor = jnp.linalg.cholesky(gram)
        identity_matrix = jnp.eye(vec_width, dtype=jnp.float32)
        inverse = lax.linalg.triangular_solve(factor, identity_matrix, left_side=True, lower=True).T
        vectors = jnp.dot(
            flat_rows, inverse, precision=lax.Precision.HIGHEST, preferred_element_type=jnp.float32
        )
        current = vectors.astype(jnp.bfloat16)
    return vectors


def solution(mesh):
    in_specs = (
        P(("grp", "blk"), None, None),
        P(("grp", "blk"), None),
        P(("grp", "blk"), None, None),
        P(("grp", "blk"), None),
        P(("grp", "blk"), None),
        P(("grp", "blk"), None),
    )
    out_specs = P(("grp", "blk"), None)
    return jax.shard_map(
        per_device, mesh=mesh, in_specs=in_specs, out_specs=out_specs, check_vma=False
    )
```

profile of v0, /device:TPU:0, one launch (start us, length us, event | category | flops | bytes accessed | tf_op | source)
XLA Modules:
  0.0 444.7 jit_solution(17189978610640001608)
XLA Ops:
  8.6 1.3 reduce.10
  10.1 1.4 gather_fusion.1
  12.6 27.0 %all-gather.5.cloned.1.call-done = bf16[16,256,128]{2,1,0:T(8,128)(2,1)} async-done(((bf16[4,256,128]{2,1,0:T(8,128)(2,1)}), bf16[16,256,128]{2,1,0:T(8,128)(2,1)}) %all-gather.5.cloned.1.call-update) | async-done | bytes 1048592 | tf_op jit(solution)/shard_map/all_gather | solution.py:27
  39.6 3.4 gather_fusion
  43.0 25.9 %all-gather.7.cloned.1.call-done = bf16[32,256,128]{2,1,0:T(8,128)(2,1)} async-done(((bf16[4,256,128]{2,1,0:T(8,128)(2,1)}), bf16[32,256,128]{2,1,0:T(8,128)(2,1)}) %all-gather.7.cloned.1.call-update) | async-done | bytes 2097168 | tf_op jit(solution)/shard_map/all_gather | solution.py:33
  68.9 3.6 gather_fusion.2
  72.5 2.7 convolution_bitcast_fusion.1
  75.8 1.5 fusion.31
  79.4 2.0 copy.32
  81.4 115.6 %all-reduce.3.cloned.1.call-done = f32[128,128]{0,1:T(8,128)} async-done(((f32[128,128]{0,1:T(8,128)}), f32[128,128]{0,1:T(8,128)}) %all-reduce.3.cloned.1.call-update) | async-done | bytes 65552 | tf_op jit(solution)/shard_map/psum | solution.py:46
  198.8 11.7 %cholesky.44 = f32[128,128]{1,0:T(8,128)S(1)} custom-call(f32[128,128]{1,0:T(8,128)S(1)} %fusion.45), custom_call_target="Cholesky" | custom-call | tf_op jit(solution)/shard_map/jit(cholesky)/cholesky | solution.py:47
  211.9 9.8 %custom-call.6 = f32[1,128,128]{1,2,0:T(8,128)S(1)} custom-call(f32[1,128,128]{2,1,0:T(8,128)S(1)} %fusion.40), custom_call_target="InvertDiagBlocksLowerTriangular" | custom-call | tf_op jit(solution)/shard_map/triangular_solve/custom-call.0 | solution.py:49
  222.0 2.3 convolution_convert_fusion
  225.1 28.1 %all-gather.9.cloned.1.call-done = bf16[16,256,128]{2,1,0:T(8,128)(2,1)} async-done(((bf16[4,256,128]{2,1,0:T(8,128)(2,1)}), bf16[16,256,128]{2,1,0:T(8,128)(2,1)}) %all-gather.9.cloned.1.call-update) | async-done | bytes 1048592 | tf_op jit(solution)/shard_map/all_gather | solution.py:27
  253.2 3.4 gather_fusion.3
  256.6 25.8 %all-gather.11.cloned.1.call-done = bf16[32,256,128]{2,1,0:T(8,128)(2,1)} async-done(((bf16[4,256,128]{2,1,0:T(8,128)(2,1)}), bf16[32,256,128]{2,1,0:T(8,128)(2,1)}) %all-gather.11.cloned.1.call-update) | async-done | bytes 2097168 | tf_op jit(solution)/shard_map/all_gather | solution.py:33
  282.4 3.6 gather_fusion.4
  286.0 2.7 convolution_bitcast_fusion
  289.3 1.5 fusion.21
  292.8 2.0 copy.39
  294.9 115.6 %all-reduce.5.cloned.1.call-done = f32[128,128]{0,1:T(8,128)} async-done(((f32[128,128]{0,1:T(8,128)}), f32[128,128]{0,1:T(8,128)}) %all-reduce.5.cloned.1.call-update) | async-done | bytes 65552 | tf_op jit(solution)/shard_map/psum | solution.py:46
  412.3 11.7 %cholesky.55 = f32[128,128]{1,0:T(8,128)S(1)} custom-call(f32[128,128]{1,0:T(8,128)S(1)} %fusion.43), custom_call_target="Cholesky" | custom-call | tf_op jit(solution)/shard_map/jit(cholesky)/cholesky | solution.py:47
  425.4 9.8 %custom-call.7 = f32[1,128,128]{1,2,0:T(8,128)S(1)} custom-call(f32[1,128,128]{2,1,0:T(8,128)S(1)} %fusion.41), custom_call_target="InvertDiagBlocksLowerTriangular" | custom-call | tf_op jit(solution)/shard_map/triangular_solve/custom-call.0 | solution.py:49
  435.5 2.4 fusion.46
  (59 shorter events, 16.1 us)
Async XLA Ops:
  6.5 66.0 %copy-start = (bf16[24,256,256]{2,1,0:T(8,128)(2,1)S(1)}, bf16[24,256,256]{2,1,0:T(8,128)(2,1)}, u32[]{:S(2)}) copy-start(bf16[24,256,256]{2,1,0:T(8,128)(2,1)} %param.11) | copy-start | bytes 9437188
  6.5 5.1 %copy-start.7 = (s32[1,32]{1,0:T(1,128)S(1)}, s32[1,32]{1,0:T(1,128)}, u32[]{:S(2)}) copy-start(s32[1,32]{1,0:T(1,128)} %param.10) | copy-start | bytes 388
  6.5 33.1 %all-gather.5.cloned.1.call-start = ((), (), s32[]{:S(2)}) async-start(), calls=%async_computation | async-start | bytes 1310720 | tf_op jit(solution)/shard_map/all_gather | solution.py:27
  7.3 61.6 %all-gather.7.cloned.1.call-start = ((), (), s32[]{:S(2)}) async-start(), calls=%async_computation.1 | async-start | bytes 2359296 | tf_op jit(solution)/shard_map/all_gather | solution.py:33
  8.0 189.0 %all-reduce.3.cloned.1.call-start = ((), (), s32[]{:S(2)}) async-start(), calls=%async_computation.2 | async-start | bytes 131072 | tf_op jit(solution)/shard_map/psum | solution.py:46
  72.5 2.7 copy-start.4
  72.5 3.3 copy-start.5
  77.3 0.8 copy-start.1
  79.3 173.9 %all-gather.9.cloned.1.call-start = ((), (), s32[]{:S(2)}) async-start(), calls=%async_computation.3 | async-start | bytes 1310720 | tf_op jit(solution)/shard_map/all_gather | solution.py:27
  224.3 58.1 %all-gather.11.cloned.1.call-start = ((), (), s32[]{:S(2)}) async-start(), calls=%async_computation.4 | async-start | bytes 2359296 | tf_op jit(solution)/shard_map/all_gather | solution.py:33
  224.9 185.6 %all-reduce.5.cloned.1.call-start = ((), (), s32[]{:S(2)}) async-start(), calls=%async_computation.5 | async-start | bytes 131072 | tf_op jit(solution)/shard_map/psum | solution.py:46
  286.0 2.7 copy-start.3
  286.0 3.3 copy-start.6
  290.8 0.8 copy-start.2
Sparse Core Ops, SparseCore 0:
  8.9 30.6 all-gather.4
  41.5 27.3 all-gather.6
  79.5 117.5 all-reduce.2
  224.5 28.7 all-gather.8
  255.0 27.3 all-gather.10
  292.9 117.5 all-reduce.4
where the time goes:
time: 447 us; the launch traced here: 445 us
  waiting for transfers between devices  340 us (76%)
  other arithmetic  51.2 us (11%)
  local copies, waits for them, and re-layouts  23.3 us (5%)
  matrix products  16.2 us (4%)
  between operations  13.6 us (3%)
    psum x2, waiting for transfers between devices, per_device(): gram = lax.psum(local_gram, ('grp', 'blk')) / total_rows  231 us
    all_gather x2, waiting for transfers between devices, per_device(): group_table = lax.all_gather(local_rows, 'blk', axis=0, tiled=True)  55.1 us
    all_gather x2, waiting for transfers between devices, per_device(): everything = lax.all_gather(local_rows, 'grp', axis=0, tiled=True)  51.7 us
    another operation x6, other arithmetic, per_device(): factor = jnp.linalg.cholesky(gram)  24.8 us
    another operation x4, other arithmetic, per_device(): lax.linalg.triangular_solve(factor, identity_matrix, left_side=True, lowe...  20.9 us
  transfers between devices with their start and end apart: 6, of which 6 were waited for; matrix products, arithmetic and copies ran while one was open for 3% of the time, Pallas kernels for 0%

commit v1 on v0

v1 whole, which is shorter than its diff:
```python
import functools

import jax
import jax.numpy as jnp
from jax import lax
from jax.experimental import pallas as pl
from jax.experimental.pallas import tpu as pltpu
from jax.sharding import PartitionSpec as P

ITERS = 2
AXES = ("grp", "blk")
HIGHEST = lax.Precision.HIGHEST
INFLATION_MAX = 1.05
CORRECTION_MAX = 4e-6
VMEM = pl.BlockSpec(memory_space=pltpu.VMEM)
SMEM = pl.BlockSpec(memory_space=pltpu.SMEM)
F32 = jnp.float32
BF16 = jnp.bfloat16


def mm(a, b):
    return jnp.dot(a, b, precision=HIGHEST, preferred_element_type=F32)


def mm_nt(a, b):
    return lax.dot_general(a, b, (((1,), (1,)), ((), ())), precision=HIGHEST, preferred_element_type=F32)


def mm_tn(a, b):
    return lax.dot_general(a, b, (((0,), (0,)), ((), ())), precision=HIGHEST, preferred_element_type=F32)


def cost(flops, nbytes):
    return pl.CostEstimate(flops=flops, bytes_accessed=nbytes, transcendentals=0)


def inverse_factor(gram, work):
    n = gram.shape[0]
    rows = lax.broadcasted_iota(jnp.int32, (n, n), 0)
    cols = lax.broadcasted_iota(jnp.int32, (n, n), 1)
    on_diag = rows == cols
    eye = on_diag.astype(F32)
    weight = jnp.where(rows > cols, 1.0, jnp.where(on_diag, 0.5, 0.0)).astype(F32)
    on_diag_values = jnp.where(on_diag, gram, 0.0)
    scale_row = lax.rsqrt(jnp.sum(on_diag_values, axis=0, keepdims=True))
    scale_col = lax.rsqrt(jnp.sum(on_diag_values, axis=1, keepdims=True))
    base = gram * scale_col * scale_row - eye
    low = weight * base
    size = jnp.float32(0)
    for _ in range(2):
        moved = mm(low, base)
        crossed = mm_nt(low + moved - base, low)
        error = base - low - moved + crossed - low * eye
        step = weight * error
        size = jnp.sum(step * step)
        low = low + step - mm(step, low)
    work[0] = eye - low

    @pl.when(jnp.logical_not(size <= CORRECTION_MAX))
    def _():
        work[0] = eye
        work[1] = base + eye

        def eliminate(j, carry):
            left = work[1]
            pivot_row = work[1, pl.ds(j, 1), :]
            pivot = jnp.sum(jnp.where(cols[:1] == j, pivot_row, 0.0), axis=1, keepdims=True)
            column = jnp.sum(jnp.where(cols == j, left, 0.0), axis=1, keepdims=True)
            factor = jnp.where(rows[:, :1] > j, column / pivot, 0.0)
            right_row = work[0, pl.ds(j, 1), :]
            work[1] = left - factor * pivot_row
            work[0] = work[0] - factor * right_row
            work[0, pl.ds(j, 1), :] = right_row * lax.rsqrt(pivot)
            return carry

        lax.fori_loop(0, n, eliminate, 0)

    inverse = work[0]
    inflation = jnp.sum(inverse * inverse) / n
    return inverse * scale_row, inflation


def factor_kernel(total_rows, gram_ref, inverse_ref, fine_ref, work):
    inverse, inflation = inverse_factor(gram_ref[...] / total_rows, work)
    inverse_ref[...] = inverse
    fine_ref[0] = (inflation <= INFLATION_MAX).astype(jnp.int32)


def factor(gram, total_rows):
    n = gram.shape[0]
    return pl.pallas_call(
        functools.partial(factor_kernel, total_rows),
        out_shape=(jax.ShapeDtypeStruct((n, n), F32), jax.ShapeDtypeStruct((1,), jnp.int32)),
        in_specs=[VMEM],
        out_specs=(VMEM, SMEM),
        scratch_shapes=[pltpu.VMEM((2, n, n), F32)],
        cost_estimate=cost(2 * 6 * 6 * n**3, 8 * n * n),
        name="factor",
    )(gram)


def finish_kernel(total_rows, gram_ref, product_ref, out_ref, work):
    inverse, _ = inverse_factor(gram_ref[...] / total_rows, work)
    out_ref[...] = mm_nt(product_ref[...], inverse)


def finish(gram, product, total_rows):
    n = gram.shape[0]
    return pl.pallas_call(
        functools.partial(finish_kernel, total_rows),
        out_shape=jax.ShapeDtypeStruct(product.shape, F32),
        in_specs=[VMEM, VMEM],
        out_specs=VMEM,
        scratch_shapes=[pltpu.VMEM((2, n, n), F32)],
        cost_estimate=cost(2 * 6 * 6 * n**3 + 12 * product.shape[0] * n * n, 8 * product.size),
        name="finish",
    )(gram, product)


def near_terms(shape, place, near_cols, tiles, near):
    blocks, sources, per_source, tile = shape

    def add(r, acc):
        for k, ref in near:
            first = (r * sources + (place[0] ^ k)) * per_source
            for n in range(per_source):
                start = pl.multiple_of(near_cols[first + n] * tile, tile)
                part = jnp.dot(tiles[first + n], ref[pl.ds(start, tile), :], preferred_element_type=F32)
                acc = part if acc is None else acc + part
        return acc

    return add


def early_kernel(shape, n_near, groups, place, near_cols, far_groups, need, *refs):
    blocks, sources, per_source, tile = shape
    near = list(enumerate_sources(sources))[:n_near]
    near = list(zip(near, refs[:n_near]))
    far = refs[n_near : n_near + groups - 1]
    tiles_near, tiles_far, out_ref, table = refs[n_near + groups - 1 :]
    far_each = tiles_far.shape[0] // blocks
    for k in range(1, groups):
        h = place[1] ^ k
        start = pl.multiple_of(jnp.maximum(need[h], 0) * tile, tile)
        table[h] = far[k - 1][pl.ds(start, tile), :]
    add = near_terms(shape, place, near_cols, tiles_near, near)
    for r in range(blocks):
        acc = add(r, None)
        for t in range(r * far_each, (r + 1) * far_each):
            acc = acc + jnp.dot(tiles_far[t], table[far_groups[t]], preferred_element_type=F32)
        out_ref[pl.ds(r * tile, tile), :] = acc


def enumerate_sources(sources):
    order = [0]
    step = sources // 2
    while step:
        order += [k | step for k in order]
        step //= 2
    return order


def early(shape, groups, scalars, near, far, tiles_near, tiles_far):
    blocks, sources, per_source, tile = shape
    width = near[0].shape[1]
    count = len(near) * blocks * per_source + tiles_far.shape[0]
    return pl.pallas_call(
        functools.partial(early_kernel, shape, len(near), groups),
        out_shape=jax.ShapeDtypeStruct((blocks * tile, width), F32),
        in_specs=[SMEM] * 4 + [VMEM] * (len(near) + len(far) + 2),
        out_specs=VMEM,
        scratch_shapes=[pltpu.VMEM((groups, tile, width), BF16)],
        cost_estimate=cost(2 * count * tile * tile * width, 2 * count * tile * tile),
        compiler_params=pltpu.CompilerParams(vmem_limit_bytes=40 << 20),
        name="early",
    )(*scalars, *near, *far, tiles_near, tiles_far)


def late_rows(shape, place, near_cols, partial, late, tiles, r):
    blocks, sources, per_source, tile = shape
    order = enumerate_sources(sources)
    near = list(zip(order[len(order) - len(late) :], late))
    return near_terms(shape, place, near_cols, tiles, near)(r, partial[pl.ds(r * tile, tile), :])


def late_kernel(shape, n_late, place, near_cols, partial, *refs):
    late, (tiles, product_ref, rounded_ref, gram_ref) = refs[:n_late], refs[n_late:]
    blocks, _, _, tile = shape
    gram = None
    for r in range(blocks):
        acc = late_rows(shape, place, near_cols, partial, late, tiles, r)
        product_ref[pl.ds(r * tile, tile), :] = acc
        rounded_ref[pl.ds(r * tile, tile), :] = acc.astype(BF16)
        part = mm_tn(acc, acc)
        gram = part if gram is None else gram + part
    gram_ref[...] = gram


def late_scaled_kernel(shape, n_late, place, near_cols, partial, *refs):
    late, (tiles, inverse_ref, product_ref, gram_ref) = refs[:n_late], refs[n_late:]
    blocks, _, _, tile = shape
    gram = None
    for r in range(blocks):
        acc = late_rows(shape, place, near_cols, partial, late, tiles, r)
        acc = mm_nt(acc, inverse_ref[...])
        product_ref[pl.ds(r * tile, tile), :] = acc
        part = mm_tn(acc, acc)
        gram = part if gram is None else gram + part
    gram_ref[...] = gram


def late(shape, scalars, partial, rows, tiles, inverse=None):
    blocks, sources, per_source, tile = shape
    width = partial.shape[1]
    count = len(rows) * blocks * per_source
    wide = jax.ShapeDtypeStruct(partial.shape, F32)
    gram = jax.ShapeDtypeStruct((width, width), F32)
    if inverse is None:
        body, outs, more = late_kernel, (wide, jax.ShapeDtypeStruct(partial.shape, BF16), gram), ()
    else:
        body, outs, more = late_scaled_kernel, (wide, gram), (inverse,)
    return pl.pallas_call(
        functools.partial(body, shape, len(rows)),
        out_shape=outs,
        in_specs=[SMEM] * 2 + [VMEM] * (len(rows) + 2 + len(more)),
        out_specs=(VMEM,) * len(outs),
        cost_estimate=cost(2 * count * tile * tile * width + 12 * partial.size * width, 2 * count * tile * tile),
        compiler_params=pltpu.CompilerParams(vmem_limit_bytes=40 << 20),
        name="late",
    )(*scalars[:2], partial, *rows, tiles, *more)


def swap(x, axis, mask):
    size = lax.axis_size(axis)
    return lax.ppermute(x, axis, [(i, i ^ mask) for i in range(size)])


def near_rows(rows):
    held = [rows]
    step = lax.axis_size("blk") // 2
    while step:
        held += [swap(x, "blk", step) for x in held]
        step //= 2
    return held


def far_rows(rows):
    held = {0: rows}
    size = lax.axis_size("grp")
    for k in range(2, size, 2):
        held[k] = swap(rows, "grp", k)
    for k in range(1, size, 2):
        held[k] = swap(held[k - 1], "grp", 1)
    return [held[k] for k in range(1, size)]


def pair_sum(parts):
    while len(parts) > 1:
        parts = [a + b for a, b in zip(parts[::2], parts[1::2])]
    return parts[0]


def everywhere(x):
    x = x + swap(x, "grp", 1)
    x = pair_sum([x] + [swap(x, "grp", k) for k in range(2, lax.axis_size("grp"), 2)])
    return pair_sum([x] + [swap(x, "blk", k) for k in range(1, lax.axis_size("blk"))])


def per_device(tiles_near, near_cols, tiles_far, far_groups, need_blocks, start_vectors):
    tile = tiles_near.shape[1]
    blocks = start_vectors.shape[0] // tile
    sources = lax.axis_size("blk")
    groups = lax.axis_size("grp")
    shape = (blocks, sources, tiles_near.shape[0] // (blocks * sources), tile)
    total_rows = start_vectors.shape[0] * sources * groups
    place = jnp.stack([lax.axis_index("blk"), lax.axis_index("grp")]).astype(jnp.int32)
    scalars = (place, near_cols.reshape(-1), far_groups.reshape(-1), need_blocks.reshape(-1))
    split = 3 * sources // 4

    def gathered(rows):
        near, far = near_rows(rows), far_rows(rows)
        return early(shape, groups, scalars, near[:split], far, tiles_near, tiles_far), near[split:]

    partial, rest = gathered(start_vectors)
    product, rounded, gram = late(shape, scalars, partial, rest, tiles_near)
    for _ in range(ITERS - 1):
        inverse, fine = factor(everywhere(gram), total_rows)

        partial, rest = gathered(rounded)

        def quick(product, inverse, partial, rest):
            return late(shape, scalars, partial, rest, tiles_near, inverse)

        def plain(product, inverse, partial, rest):
            current = lax.dot_general(
                product, inverse, (((1,), (1,)), ((), ())), precision=HIGHEST, preferred_element_type=F32
            ).astype(BF16)
            partial, rest = gathered(current)
            product, _, gram = late(shape, scalars, partial, rest, tiles_near)
            return product, gram

        product, gram = lax.cond(fine[0] > 0, quick, plain, product, inverse, partial, rest)
        rounded = product.astype(BF16)
    return finish(everywhere(gram), product, total_rows)


def solution(mesh):
    in_specs = (
        P(AXES, None, None),
        P(AXES, None),
        P(AXES, None, None),
        P(AXES, None),
        P(AXES, None),
        P(AXES, None),
    )
    return jax.shard_map(
        per_device, mesh=mesh, in_specs=in_specs, out_specs=P(AXES, None), check_vma=False
    )
```

time: 447 us -> 138 us (0.31)
  waiting for transfers between devices: 340 us -> 52.6 us
  other arithmetic: 51.2 us -> 1.43 us
  starting transfers between devices: 0.38 us -> 43.9 us
  Pallas kernels: 0 us -> 37.5 us
  local copies, waits for them, and re-layouts: 23.3 us -> 1.09 us
  matrix products: 16.2 us -> 0.58 us
  between operations: 13.6 us -> 0.88 us
    psum x2 -> x0, waiting for transfers between devices: 231 us -> none  [per_device(): gram = lax.psum(local_gram, ('grp', 'blk')) / total_rows]
    all_gather x4 -> x0, waiting for transfers between devices: 107 us -> none  [the longest x2 55.1 us: per_device(): group_table = lax.all_gather(local_rows, 'blk', axis=0, tiled=True)]
    ppermute x0 -> x44, waiting for transfers between devices: none -> 52.6 us  [swap(): return lax.ppermute(x, axis, [(i, i ^ mask) for i in range(size)])]
    another operation x10 -> x1, other arithmetic: 45.7 us -> 0.07 us  [per_device(): jnp.stack([lax.axis_index('blk'), lax.axis_index('grp')]).astype(jnp.int32)]
    ppermute x0 -> x44, starting transfers between devices: none -> 43.9 us  [swap(): return lax.ppermute(x, axis, [(i, i ^ mask) for i in range(size)])]
    pallas_call x0 -> x7, Pallas kernels: none -> 37.5 us  [the longest x1 16.3 us: factor(): pl.pallas_call(functools.partial(factor_kernel, total_rows), out_shape=(j...]
    gather x6 -> x0, local copies, waits for them, and re-layouts: 15.4 us -> none  [the longest x4 8.61 us: per_device(): far_rows = everything[far_index * blocks + wanted[far_index]]]
    dot_general x8 -> x1, matrix products: 15.6 us -> 0.58 us  [plain(): lax.dot_general(product, inverse, (((1,), (1,)), ((), ())), precision=HIG...]
  transfers between devices with their start and end apart: 6 -> 44, of which waited for: 6 -> 27; matrix products, arithmetic and copies ran while one was open for 3% -> 1% of each run, Pallas kernels for 0% -> 21%
where the time goes in v1:
time: 138 us
  waiting for transfers between devices  52.6 us (38%)
  starting transfers between devices  43.9 us (32%)
  Pallas kernels  37.5 us (27%)
  other arithmetic  1.43 us (1%)
    ppermute x44, waiting for transfers between devices, swap(): return lax.ppermute(x, axis, [(i, i ^ mask) for i in range(size)])  52.6 us
    ppermute x44, starting transfers between devices, swap(): return lax.ppermute(x, axis, [(i, i ^ mask) for i in range(size)])  43.9 us
    pallas_call x1, Pallas kernels, factor(): pl.pallas_call(functools.partial(factor_kernel, total_rows), out_shape=(j...  16.3 us
    pallas_call x3, Pallas kernels, early(): pl.pallas_call(functools.partial(early_kernel, shape, len(near), groups),...  12.6 us
    pallas_call x2, Pallas kernels, late(): pl.pallas_call(functools.partial(body, shape, len(rows)), out_shape=outs,...  4.77 us
    pallas_call x1, Pallas kernels, finish(): pl.pallas_call(functools.partial(finish_kernel, total_rows), out_shape=ja...  3.77 us
  transfers between devices with their start and end apart: 44, of which 27 were waited for; matrix products, arithmetic and copies ran while one was open for 1% of the time, Pallas kernels for 21%

profile of v1, /device:TPU:0, one launch (start us, length us, event | category | flops | bytes accessed | tf_op | source)
XLA Modules:
  0.0 138.1 jit_solution(16127693810337121587)
XLA Ops:
  0.0 3.0 %collective-permute-start.15 = (bf16[1024,128]{1,0:T(8,128)(2,1)}, bf16[1024,128]{1,0:T(8,128)(2,1)S(1)}, u32[]{:S(2)}, u32[]{:S(2)}) collective-permute-start(bf16[1024,128]{1,0:T(8,128)(2,1)} %refs_0_.1), channel_id=1, source_target_pairs={{0,16},{4,20},{8,24},{12,28},{16,0},{20,4},{24,8},{28,12},{1,17},{... | collective-permute-start | bytes 786440 | tf_op jit(solution)/shard_map/ppermute | solution.py:235
  4.5 3.1 %collective-permute-start.10 = (bf16[1024,128]{1,0:T(8,128)(2,1)}, bf16[1024,128]{1,0:T(8,128)(2,1)S(1)}, u32[]{:S(2)}, u32[]{:S(2)}) collective-permute-start(bf16[1024,128]{1,0:T(8,128)(2,1)} %refs_0_.1), channel_id=1, source_target_pairs={{0,2},{1,3},{2,0},{3,1},{4,6},{5,7},{6,4},{7,5},{8,10},{9,11},{10,... | collective-permute-start | bytes 786440 | tf_op jit(solution)/shard_map/ppermute | solution.py:235
  9.5 2.1 %collective-permute-start.11 = (bf16[1024,128]{1,0:T(8,128)(2,1)}, bf16[1024,128]{1,0:T(8,128)(2,1)S(1)}, u32[]{:S(2)}, u32[]{:S(2)}) collective-permute-start(bf16[1024,128]{1,0:T(8,128)(2,1)} %refs_0_.1), channel_id=1, source_target_pairs={{0,1},{1,0},{2,3},{3,2},{4,5},{5,4},{6,7},{7,6},{8,9},{9,8},{10,11... | collective-permute-start | bytes 786440 | tf_op jit(solution)/shard_map/ppermute | solution.py:235
  12.9 3.4 %collective-permute-done.17.refs_8_ = bf16[1024,128]{1,0:T(8,128)(2,1)S(1)} collective-permute-done((bf16[1024,128]{1,0:T(8,128)(2,1)}, bf16[1024,128]{1,0:T(8,128)(2,1)S(1)}, u32[]{:S(2)}, u32[]{:S(2)}) %collective-permute-start.17) | collective-permute-done | bytes 262176 | tf_op jit(solution)/shard_map/ppermute | solution.py:235
  16.3 3.9 %collective-permute-done.10.refs_1_ = bf16[1024,128]{1,0:T(8,128)(2,1)S(1)} collective-permute-done((bf16[1024,128]{1,0:T(8,128)(2,1)}, bf16[1024,128]{1,0:T(8,128)(2,1)S(1)}, u32[]{:S(2)}, u32[]{:S(2)}) %collective-permute-start.10) | collective-permute-done | bytes 262176 | tf_op jit(solution)/shard_map/ppermute | solution.py:235
  22.6 5.1 %early.4.partial = f32[1024,128]{1,0:T(8,128)S(1)} custom-call(s32[2]{0:T(128)S(1)} %pad_add_fusion.place, s32[32]{0:T(128)} %bitcast.8, s32[24]{0:T(128)} %bitcast.13, s32[8]{0:T(128)} %bitcast.16, bf16[1024,128]{1,0:T(8,128)(2,1)S(1)} %copy-done, bf16[1024,128]{1,0:T(8,128)(2,1)S(1)} %collective-permute-done.10.refs_1_, ...), custom_call_target="tpu_custom_call" | custom-call | flops 805306368 | bytes 6291456 | tf_op jit(solution)/shard_map/early/pallas_call | solution.py:167
  28.1 2.4 %late.5 = (f32[1024,128]{1,0:T(8,128)}, bf16[1024,128]{1,0:T(8,128)(2,1)S(1)}, f32[128,128]{1,0:T(8,128)S(1)}) custom-call(s32[2]{0:T(128)S(1)} %pad_add_fusion.place, s32[32]{0:T(128)S(1)} %bitcast.9, f32[1024,128]{1,0:T(8,128)S(1)} %early.4.partial, bf16[1024,128]{1,0:T(8,128)(2,1)S(1)} %collective-permute-done.19.refs_0_, bf16[32,256,256]{2,1,0:T(8,128)(2,1)S(1)} %copy-done.1), custom_call_target="tpu_custom_call" | custom-call | flops 335544320 | bytes 1048576 | tf_op jit(solution)/shard_map/late/pallas_call | solution.py:222
  31.8 2.3 %collective-permute-start.23 = (f32[128,128]{1,0:T(8,128)S(1)}, f32[128,128]{1,0:T(8,128)S(1)}, u32[]{:S(2)}, u32[]{:S(2)}) collective-permute-start(f32[128,128]{1,0:T(8,128)S(1)} %add.42), channel_id=1, source_target_pairs={{0,24},{4,28},{8,16},{12,20},{16,8},{20,12},{24,0},{28,4},{1,25},{... | collective-permute-start | bytes 196616 | tf_op jit(solution)/shard_map/ppermute | solution.py:235
  38.8 4.6 %collective-permute-start.26 = (f32[128,128]{1,0:T(8,128)S(1)}, f32[128,128]{1,0:T(8,128)S(1)}, u32[]{:S(2)}, u32[]{:S(2)}) collective-permute-start(f32[128,128]{1,0:T(8,128)S(1)} %add_add_fusion.3), channel_id=1, source_target_pairs={{0,3},{1,2},{2,1},{3,0},{4,7},{5,6},{6,5},{7,4},{8,11},{9,10},{10,... | collective-permute-start | bytes 196616 | tf_op jit(solution)/shard_map/ppermute | solution.py:235
  50.6 3.4 %collective-permute-done.34.refs_8_ = bf16[1024,128]{1,0:T(8,128)(2,1)S(1)} collective-permute-done((bf16[1024,128]{1,0:T(8,128)(2,1)S(1)}, bf16[1024,128]{1,0:T(8,128)(2,1)S(1)}, u32[]{:S(2)}, u32[]{:S(2)}) %collective-permute-start.34) | collective-permute-done | bytes 262176 | tf_op jit(solution)/shard_map/ppermute | solution.py:235
  58.0 5.9 %collective-permute-done.27.refs_1_ = bf16[1024,128]{1,0:T(8,128)(2,1)S(1)} collective-permute-done((bf16[1024,128]{1,0:T(8,128)(2,1)S(1)}, bf16[1024,128]{1,0:T(8,128)(2,1)S(1)}, u32[]{:S(2)}, u32[]{:S(2)}) %collective-permute-start.27) | collective-permute-done | bytes 262176 | tf_op jit(solution)/shard_map/ppermute | solution.py:235
  64.6 16.3 %factor.1 = (f32[128,128]{1,0:T(8,128)S(1)}, s32[1]{0:T(128)}) custom-call(f32[128,128]{1,0:T(8,128)} %add_add_fusion.2.gram_ref), custom_call_target="tpu_custom_call" | custom-call | flops 150994944 | bytes 131072 | tf_op jit(solution)/shard_map/factor/pallas_call | solution.py:91
  81.7 5.1 %early.5 = f32[1024,128]{1,0:T(8,128)S(1)} custom-call(s32[2]{0:T(128)S(1)} %pad_add_fusion.place, s32[32]{0:T(128)S(1)} %bitcast.10, s32[24]{0:T(128)S(1)} %bitcast.14, s32[8]{0:T(128)S(1)} %bitcast.17, bf16[1024,128]{1,0:T(8,128)(2,1)S(1)} %get-tuple-element.60.refs_0_, bf16[1024,128]{1,0:T(8,128)(2,1)S(1)} %collective-permute-done.27.refs_1_, ...), custom_call_target="tpu_custom_call" | custom-call | flops 805306368 | bytes 6291456 | tf_op jit(solution)/shard_map/early/pallas_call | solution.py:167
  87.0 30.0 %conditional.1 = ((f32[1024,128]{1,0:T(8,128)S(1)}, f32[128,128]{1,0:T(8,128)S(1)})) conditional(s32[]{:T(128)} %bitcast.5, (f32[1024,128]{1,0:T(8,128)S(1)}, f32[128,128]{1,0:T(8,128)S(1)}, s32[2]{0:T(128)S(1)}, s32[32]{0:T(128)S(1)}, s32[24]{0:T(128)S(1)}, /*index=5*/s32[8]{0:T(128)S(1)}, bf16[32,256,256]{2,1,0:T(8,128)(2,1)S(1)}, ...), branch_computations={%region_0.0_spmd, %region_1.0_spmd} | conditional | flops 1342308352 | bytes 18678184 | solution.py:302
  91.2 2.7 %collective-permute-start = (bf16[1024,128]{1,0:T(8,128)(2,1)S(1)}, bf16[1024,128]{1,0:T(8,128)(2,1)S(1)}, u32[]{:S(2)}, u32[]{:S(2)}) collective-permute-start(bf16[1024,128]{1,0:T(8,128)(2,1)S(1)} %convolution_convert_fusion.refs_0_), channel_id=1, source_target_pairs={{0,2},{1,3},{2,0},{3,1},{4,6},{5,7},{6,4},{7,5},{8,10},{9,11},{10,... | collective-permute-start | bytes 786440 | tf_op jit(solution)/shard_map/cond/branch_0_fun/ppermute | solution.py:235
  93.9 3.9 %collective-permute-done.7.refs_8_ = bf16[1024,128]{1,0:T(8,128)(2,1)S(1)} collective-permute-done((bf16[1024,128]{1,0:T(8,128)(2,1)S(1)}, bf16[1024,128]{1,0:T(8,128)(2,1)S(1)}, u32[]{:S(2)}, u32[]{:S(2)}) %collective-permute-start.7) | collective-permute-done | bytes 262176 | tf_op jit(solution)/shard_map/cond/branch_0_fun/ppermute | solution.py:235
  99.9 2.4 %collective-permute-done.5.refs_6_ = bf16[1024,128]{1,0:T(8,128)(2,1)S(1)} collective-permute-done((bf16[1024,128]{1,0:T(8,128)(2,1)S(1)}, bf16[1024,128]{1,0:T(8,128)(2,1)S(1)}, u32[]{:S(2)}, u32[]{:S(2)}) %collective-permute-start.5) | collective-permute-done | bytes 262176 | tf_op jit(solution)/shard_map/cond/branch_0_fun/ppermute | solution.py:235
  103.1 3.6 %collective-permute-done.refs_1_ = bf16[1024,128]{1,0:T(8,128)(2,1)S(1)} collective-permute-done((bf16[1024,128]{1,0:T(8,128)(2,1)S(1)}, bf16[1024,128]{1,0:T(8,128)(2,1)S(1)}, u32[]{:S(2)}, u32[]{:S(2)}) %collective-permute-start) | collective-permute-done | bytes 262176 | tf_op jit(solution)/shard_map/cond/branch_0_fun/ppermute | solution.py:235
  108.4 2.4 %early.3.partial = f32[1024,128]{1,0:T(8,128)S(1)} custom-call(s32[2]{0:T(128)S(1)} %get-tuple-element.33.place, s32[32]{0:T(128)S(1)} %get-tuple-element.34.near_cols, s32[24]{0:T(128)S(1)} %get-tuple-element.35.far_groups, s32[8]{0:T(128)S(1)} %get-tuple-element.36.need, bf16[1024,128]{1,0:T(8,128)(2,1)S(1)} %convolution_convert_fusion.refs_0_, ...), custom_call_target="tpu_custom_call" | custom-call | flops 805306368 | bytes 6291456 | tf_op jit(solution)/shard_map/cond/branch_0_fun/early/pallas_call | solution.py:167
  110.8 3.8 %collective-permute-done.9.refs_0_ = bf16[1024,128]{1,0:T(8,128)(2,1)S(1)} collective-permute-done((bf16[1024,128]{1,0:T(8,128)(2,1)S(1)}, bf16[1024,128]{1,0:T(8,128)(2,1)S(1)}, u32[]{:S(2)}, u32[]{:S(2)}) %collective-permute-start.9) | collective-permute-done | bytes 262176 | tf_op jit(solution)/shard_map/cond/branch_0_fun/ppermute | solution.py:235
  114.6 2.3 %late.3 = (f32[1024,128]{1,0:T(8,128)S(1)}, bf16[1024,128]{1,0:T(8,128)(2,1)}, f32[128,128]{1,0:T(8,128)S(1)}) custom-call(s32[2]{0:T(128)S(1)} %get-tuple-element.33.place, s32[32]{0:T(128)S(1)} %get-tuple-element.34.near_cols, f32[1024,128]{1,0:T(8,128)S(1)} %early.3.partial, bf16[1024,128]{1,0:T(8,128)(2,1)S(1)} %collective-permute-done.9.refs_0_, ...), custom_call_target="tpu_custom_call" | custom-call | flops 335544320 | bytes 1048576 | tf_op jit(solution)/shard_map/cond/branch_0_fun/late/pallas_call | solution.py:222
  127.4 2.5 %collective-permute-start.41 = (f32[128,128]{1,0:T(8,128)S(1)}, f32[128,128]{1,0:T(8,128)S(1)}, u32[]{:S(2)}, u32[]{:S(2)}) collective-permute-start(f32[128,128]{1,0:T(8,128)S(1)} %add_add_fusion.1), channel_id=1, source_target_pairs={{0,1},{1,0},{2,3},{3,2},{4,5},{5,4},{6,7},{7,6},{8,9},{9,8},{10,11... | collective-permute-start | bytes 196616 | tf_op jit(solution)/shard_map/ppermute | solution.py:235
  129.9 2.2 %collective-permute-done.43 = f32[128,128]{1,0:T(8,128)S(1)} collective-permute-done((f32[128,128]{1,0:T(8,128)S(1)}, f32[128,128]{1,0:T(8,128)S(1)}, u32[]{:S(2)}, u32[]{:S(2)}) %collective-permute-start.43) | collective-permute-done | bytes 65568 | tf_op jit(solution)/shard_map/ppermute | solution.py:235
  134.3 3.8 %finish.1 = f32[1024,128]{1,0:T(8,128)} custom-call(f32[128,128]{1,0:T(8,128)} %add_add_fusion.gram_ref, f32[1024,128]{1,0:T(8,128)S(1)} %get-tuple-element.62.product_ref), custom_call_target="tpu_custom_call" | custom-call | flops 352321536 | bytes 1048576 | tf_op jit(solution)/shard_map/finish/pallas_call | solution.py:109
  (96 shorter events, 47.0 us)
Async XLA Ops:
  0.0 9.5 %collective-permute-start.15 = (bf16[1024,128]{1,0:T(8,128)(2,1)}, bf16[1024,128]{1,0:T(8,128)(2,1)S(1)}, u32[]{:S(2)}, u32[]{:S(2)}) collective-permute-start(bf16[1024,128]{1,0:T(8,128)(2,1)} %refs_0_.1), channel_id=1, source_target_pairs={{0,16},{4,20},{8,24},{12,28},{16,0},{20,4},{24,8},{28,12},{1,17},{... | collective-permute-start | bytes 786440 | tf_op jit(solution)/shard_map/ppermute | solution.py:235
  3.0 9.4 %collective-permute-start.13 = (bf16[1024,128]{1,0:T(8,128)(2,1)}, bf16[1024,128]{1,0:T(8,128)(2,1)S(1)}, u32[]{:S(2)}, u32[]{:S(2)}) collective-permute-start(bf16[1024,128]{1,0:T(8,128)(2,1)} %refs_0_.1), channel_id=1, source_target_pairs={{0,8},{4,12},{8,0},{12,4},{16,24},{20,28},{24,16},{28,20},{1,9},{5... | collective-permute-start | bytes 786440 | tf_op jit(solution)/shard_map/ppermute | solution.py:235
  4.5 11.8 %collective-permute-start.17 = (bf16[1024,128]{1,0:T(8,128)(2,1)}, bf16[1024,128]{1,0:T(8,128)(2,1)S(1)}, u32[]{:S(2)}, u32[]{:S(2)}) collective-permute-start(bf16[1024,128]{1,0:T(8,128)(2,1)} %refs_0_.1), channel_id=1, source_target_pairs={{0,24},{4,28},{8,16},{12,20},{16,8},{20,12},{24,0},{28,4},{1,25},{... | collective-permute-start | bytes 786440 | tf_op jit(solution)/shard_map/ppermute | solution.py:235
  4.5 15.7 %collective-permute-start.10 = (bf16[1024,128]{1,0:T(8,128)(2,1)}, bf16[1024,128]{1,0:T(8,128)(2,1)S(1)}, u32[]{:S(2)}, u32[]{:S(2)}) collective-permute-start(bf16[1024,128]{1,0:T(8,128)(2,1)} %refs_0_.1), channel_id=1, source_target_pairs={{0,2},{1,3},{2,0},{3,1},{4,6},{5,7},{6,4},{7,5},{8,10},{9,11},{10,... | collective-permute-start | bytes 786440 | tf_op jit(solution)/shard_map/ppermute | solution.py:235
  9.5 12.2 %collective-permute-start.11 = (bf16[1024,128]{1,0:T(8,128)(2,1)}, bf16[1024,128]{1,0:T(8,128)(2,1)S(1)}, u32[]{:S(2)}, u32[]{:S(2)}) collective-permute-start(bf16[1024,128]{1,0:T(8,128)(2,1)} %refs_0_.1), channel_id=1, source_target_pairs={{0,1},{1,0},{2,3},{3,2},{4,5},{5,4},{6,7},{7,6},{8,9},{9,8},{10,11... | collective-permute-start | bytes 786440 | tf_op jit(solution)/shard_map/ppermute | solution.py:235
  12.4 9.2 %collective-permute-start.16 = (bf16[1024,128]{1,0:T(8,128)(2,1)S(1)}, bf16[1024,128]{1,0:T(8,128)(2,1)S(1)}, u32[]{:S(2)}, u32[]{:S(2)}) collective-permute-start(bf16[1024,128]{1,0:T(8,128)(2,1)S(1)} %collective-permute-done.15.refs_6_), channel_id=1, source_target_pairs={{0,4},{4,0},{8,12},{12,8},{16,20},{20,16},{24,28},{28,24},{1,5},{5... | collective-permute-start | bytes 786440 | tf_op jit(solution)/shard_map/ppermute | solution.py:235
  12.4 9.2 %collective-permute-start.14 = (bf16[1024,128]{1,0:T(8,128)(2,1)S(1)}, bf16[1024,128]{1,0:T(8,128)(2,1)S(1)}, u32[]{:S(2)}, u32[]{:S(2)}) collective-permute-start(bf16[1024,128]{1,0:T(8,128)(2,1)S(1)} %collective-permute-done.13.refs_4_), channel_id=1, source_target_pairs={{0,4},{4,0},{8,12},{12,8},{16,20},{20,16},{24,28},{28,24},{1,5},{5... | collective-permute-start | bytes 786440 | tf_op jit(solution)/shard_map/ppermute | solution.py:235
  44.1 10.0 %collective-permute-start.34 = (bf16[1024,128]{1,0:T(8,128)(2,1)S(1)}, bf16[1024,128]{1,0:T(8,128)(2,1)S(1)}, u32[]{:S(2)}, u32[]{:S(2)}) collective-permute-start(bf16[1024,128]{1,0:T(8,128)(2,1)S(1)} %get-tuple-element.60.refs_0_), channel_id=1, source_target_pairs={{0,24},{4,28},{8,16},{12,20},{16,8},{20,12},{24,0},{28,4},{1,25},{... | collective-permute-start | bytes 786440 | tf_op jit(solution)/shard_map/ppermute | solution.py:235
  45.6 11.2 %collective-permute-start.32 = (bf16[1024,128]{1,0:T(8,128)(2,1)S(1)}, bf16[1024,128]{1,0:T(8,128)(2,1)S(1)}, u32[]{:S(2)}, u32[]{:S(2)}) collective-permute-start(bf16[1024,128]{1,0:T(8,128)(2,1)S(1)} %get-tuple-element.60.refs_0_), channel_id=1, source_target_pairs={{0,16},{4,20},{8,24},{12,28},{16,0},{20,4},{24,8},{28,12},{1,17},{... | collective-permute-start | bytes 786440 | tf_op jit(solution)/shard_map/ppermute | solution.py:235
  46.3 11.2 %collective-permute-start.30 = (bf16[1024,128]{1,0:T(8,128)(2,1)S(1)}, bf16[1024,128]{1,0:T(8,128)(2,1)S(1)}, u32[]{:S(2)}, u32[]{:S(2)}) collective-permute-start(bf16[1024,128]{1,0:T(8,128)(2,1)S(1)} %get-tuple-element.60.refs_0_), channel_id=1, source_target_pairs={{0,8},{4,12},{8,0},{12,4},{16,24},{20,28},{24,16},{28,20},{1,9},{5... | collective-permute-start | bytes 786440 | tf_op jit(solution)/shard_map/ppermute | solution.py:235
  48.6 8.9 %collective-permute-start.29 = (bf16[1024,128]{1,0:T(8,128)(2,1)S(1)}, bf16[1024,128]{1,0:T(8,128)(2,1)S(1)}, u32[]{:S(2)}, u32[]{:S(2)}) collective-permute-start(bf16[1024,128]{1,0:T(8,128)(2,1)S(1)} %get-tuple-element.60.refs_0_), channel_id=1, source_target_pairs={{0,4},{4,0},{8,12},{12,8},{16,20},{20,16},{24,28},{28,24},{1,5},{5... | collective-permute-start | bytes 786440 | tf_op jit(solution)/shard_map/ppermute | solution.py:235
  48.6 15.3 %collective-permute-start.27 = (bf16[1024,128]{1,0:T(8,128)(2,1)S(1)}, bf16[1024,128]{1,0:T(8,128)(2,1)S(1)}, u32[]{:S(2)}, u32[]{:S(2)}) collective-permute-start(bf16[1024,128]{1,0:T(8,128)(2,1)S(1)} %get-tuple-element.60.refs_0_), channel_id=1, source_target_pairs={{0,2},{1,3},{2,0},{3,1},{4,6},{5,7},{6,4},{7,5},{8,10},{9,11},{10,... | collective-permute-start | bytes 786440 | tf_op jit(solution)/shard_map/ppermute | solution.py:235
  54.0 27.6 %collective-permute-start.28 = (bf16[1024,128]{1,0:T(8,128)(2,1)S(1)}, bf16[1024,128]{1,0:T(8,128)(2,1)S(1)}, u32[]{:S(2)}, u32[]{:S(2)}) collective-permute-start(bf16[1024,128]{1,0:T(8,128)(2,1)S(1)} %get-tuple-element.60.refs_0_), channel_id=1, source_target_pairs={{0,1},{1,0},{2,3},{3,2},{4,5},{5,4},{6,7},{7,6},{8,9},{9,8},{10,11... | collective-permute-start | bytes 786440 | tf_op jit(solution)/shard_map/ppermute | solution.py:235
  56.8 24.9 %collective-permute-start.35 = (bf16[1024,128]{1,0:T(8,128)(2,1)S(1)}, bf16[1024,128]{1,0:T(8,128)(2,1)S(1)}, u32[]{:S(2)}, u32[]{:S(2)}) collective-permute-start(bf16[1024,128]{1,0:T(8,128)(2,1)S(1)} %collective-permute-done.34.refs_8_), channel_id=1, source_target_pairs={{0,4},{4,0},{8,12},{12,8},{16,20},{20,16},{24,28},{28,24},{1,5},{5... | collective-permute-start | bytes 786440 | tf_op jit(solution)/shard_map/ppermute | solution.py:235
  57.5 24.2 %collective-permute-start.33 = (bf16[1024,128]{1,0:T(8,128)(2,1)S(1)}, bf16[1024,128]{1,0:T(8,128)(2,1)S(1)}, u32[]{:S(2)}, u32[]{:S(2)}) collective-permute-start(bf16[1024,128]{1,0:T(8,128)(2,1)S(1)} %collective-permute-done.32.refs_6_), channel_id=1, source_target_pairs={{0,4},{4,0},{8,12},{12,8},{16,20},{20,16},{24,28},{28,24},{1,5},{5... | collective-permute-start | bytes 786440 | tf_op jit(solution)/shard_map/ppermute | solution.py:235
  57.5 24.2 %collective-permute-start.31 = (bf16[1024,128]{1,0:T(8,128)(2,1)S(1)}, bf16[1024,128]{1,0:T(8,128)(2,1)S(1)}, u32[]{:S(2)}, u32[]{:S(2)}) collective-permute-start(bf16[1024,128]{1,0:T(8,128)(2,1)S(1)} %collective-permute-done.30.refs_4_), channel_id=1, source_target_pairs={{0,4},{4,0},{8,12},{12,8},{16,20},{20,16},{24,28},{28,24},{1,5},{5... | collective-permute-start | bytes 786440 | tf_op jit(solution)/shard_map/ppermute | solution.py:235
  63.9 22.9 %collective-permute-start.36 = (bf16[1024,128]{1,0:T(8,128)(2,1)S(1)}, bf16[1024,128]{1,0:T(8,128)(2,1)S(1)}, u32[]{:S(2)}, u32[]{:S(2)}) collective-permute-start(bf16[1024,128]{1,0:T(8,128)(2,1)S(1)} %collective-permute-done.27.refs_1_), channel_id=1, source_target_pairs={{0,1},{1,0},{2,3},{3,2},{4,5},{5,4},{6,7},{7,6},{8,9},{9,8},{10,11... | collective-permute-start | bytes 786440 | tf_op jit(solution)/shard_map/ppermute | solution.py:235
  87.7 10.2 %collective-permute-start.7 = (bf16[1024,128]{1,0:T(8,128)(2,1)S(1)}, bf16[1024,128]{1,0:T(8,128)(2,1)S(1)}, u32[]{:S(2)}, u32[]{:S(2)}) collective-permute-start(bf16[1024,128]{1,0:T(8,128)(2,1)S(1)} %convolution_convert_fusion.refs_0_), channel_id=1, source_target_pairs={{0,24},{4,28},{8,16},{12,20},{16,8},{20,12},{24,0},{28,4},{1,25},{... | collective-permute-start | bytes 786440 | tf_op jit(solution)/shard_map/cond/branch_0_fun/ppermute | solution.py:235
  89.2 13.1 %collective-permute-start.5 = (bf16[1024,128]{1,0:T(8,128)(2,1)S(1)}, bf16[1024,128]{1,0:T(8,128)(2,1)S(1)}, u32[]{:S(2)}, u32[]{:S(2)}) collective-permute-start(bf16[1024,128]{1,0:T(8,128)(2,1)S(1)} %convolution_convert_fusion.refs_0_), channel_id=1, source_target_pairs={{0,16},{4,20},{8,24},{12,28},{16,0},{20,4},{24,8},{28,12},{1,17},{... | collective-permute-start | bytes 786440 | tf_op jit(solution)/shard_map/cond/branch_0_fun/ppermute | solution.py:235
  90.0 12.5 %collective-permute-start.3 = (bf16[1024,128]{1,0:T(8,128)(2,1)S(1)}, bf16[1024,128]{1,0:T(8,128)(2,1)S(1)}, u32[]{:S(2)}, u32[]{:S(2)}) collective-permute-start(bf16[1024,128]{1,0:T(8,128)(2,1)S(1)} %convolution_convert_fusion.refs_0_), channel_id=1, source_target_pairs={{0,8},{4,12},{8,0},{12,4},{16,24},{20,28},{24,16},{28,20},{1,9},{5... | collective-permute-start | bytes 786440 | tf_op jit(solution)/shard_map/cond/branch_0_fun/ppermute | solution.py:235
  91.2 11.6 %collective-permute-start.2 = (bf16[1024,128]{1,0:T(8,128)(2,1)S(1)}, bf16[1024,128]{1,0:T(8,128)(2,1)S(1)}, u32[]{:S(2)}, u32[]{:S(2)}) collective-permute-start(bf16[1024,128]{1,0:T(8,128)(2,1)S(1)} %convolution_convert_fusion.refs_0_), channel_id=1, source_target_pairs={{0,4},{4,0},{8,12},{12,8},{16,20},{20,16},{24,28},{28,24},{1,5},{5... | collective-permute-start | bytes 786440 | tf_op jit(solution)/shard_map/cond/branch_0_fun/ppermute | solution.py:235
  91.2 15.4 %collective-permute-start = (bf16[1024,128]{1,0:T(8,128)(2,1)S(1)}, bf16[1024,128]{1,0:T(8,128)(2,1)S(1)}, u32[]{:S(2)}, u32[]{:S(2)}) collective-permute-start(bf16[1024,128]{1,0:T(8,128)(2,1)S(1)} %convolution_convert_fusion.refs_0_), channel_id=1, source_target_pairs={{0,2},{1,3},{2,0},{3,1},{4,6},{5,7},{6,4},{7,5},{8,10},{9,11},{10,... | collective-permute-start | bytes 786440 | tf_op jit(solution)/shard_map/cond/branch_0_fun/ppermute | solution.py:235
  97.9 10.5 %collective-permute-start.1 = (bf16[1024,128]{1,0:T(8,128)(2,1)S(1)}, bf16[1024,128]{1,0:T(8,128)(2,1)S(1)}, u32[]{:S(2)}, u32[]{:S(2)}) collective-permute-start(bf16[1024,128]{1,0:T(8,128)(2,1)S(1)} %convolution_convert_fusion.refs_0_), channel_id=1, source_target_pairs={{0,1},{1,0},{2,3},{3,2},{4,5},{5,4},{6,7},{7,6},{8,9},{9,8},{10,11... | collective-permute-start | bytes 786440 | tf_op jit(solution)/shard_map/cond/branch_0_fun/ppermute | solution.py:235
  106.6 8.0 %collective-permute-start.9 = (bf16[1024,128]{1,0:T(8,128)(2,1)S(1)}, bf16[1024,128]{1,0:T(8,128)(2,1)S(1)}, u32[]{:S(2)}, u32[]{:S(2)}) collective-permute-start(bf16[1024,128]{1,0:T(8,128)(2,1)S(1)} %collective-permute-done.refs_1_), channel_id=1, source_target_pairs={{0,1},{1,0},{2,3},{3,2},{4,5},{5,4},{6,7},{7,6},{8,9},{9,8},{10,11... | collective-permute-start | bytes 786440 | tf_op jit(solution)/shard_map/cond/branch_0_fun/ppermute | solution.py:235
  (28 other events, 242.5 us)

commit v2 on v0

v2 whole, which is shorter than its diff:
```python
import functools

import jax
import jax.numpy as jnp
from jax import lax
from jax.experimental import pallas as pl
from jax.experimental.pallas import tpu as pltpu
from jax.sharding import PartitionSpec as P

AXES = ("grp", "blk")
HIGHEST = lax.Precision.HIGHEST
INFLATION_MAX = 1.05
CORRECTION_MAX = 4e-6
VMEM = pl.BlockSpec(memory_space=pltpu.VMEM)
SMEM = pl.BlockSpec(memory_space=pltpu.SMEM)
ANY = pl.BlockSpec(memory_space=pl.ANY)
F32 = jnp.float32
NEED_ROWS = 16
DIAGONAL_ROWS = 8
BF16 = jnp.bfloat16
NN = (((1,), (0,)), ((), ()))
NT = (((1,), (1,)), ((), ()))
TN = (((0,), (0,)), ((), ()))


def cost(flops, nbytes):
    return pl.CostEstimate(flops=int(flops), bytes_accessed=int(nbytes), transcendentals=0)


def vmem(nbytes):
    return pltpu.CompilerParams(vmem_limit_bytes=int(nbytes) + (8 << 20))


def parts(x):
    high = x.astype(BF16)
    return high, (x - high.astype(F32)).astype(BF16)


def dot1(a, b, dims=NN):
    return lax.dot_general(a.astype(BF16), b.astype(BF16), dims, preferred_element_type=F32)


def dot3(a, b, dims=NN):
    a_high, a_low = parts(a)
    b_high, b_low = parts(b)
    return dot1(a_high, b_high, dims) + (dot1(a_high, b_low, dims) + dot1(a_low, b_high, dims))


def dot6(a, b, dims=NN):
    return lax.dot_general(a, b, dims, precision=HIGHEST, preferred_element_type=F32)


def inverse_factor(gram, work):
    n = gram.shape[0]
    rows = lax.broadcasted_iota(jnp.int32, (n, n), 0)
    cols = lax.broadcasted_iota(jnp.int32, (n, n), 1)
    on_diag = rows == cols
    eye = on_diag.astype(F32)
    weight = jnp.where(rows > cols, 1.0, jnp.where(on_diag, 0.5, 0.0)).astype(F32)
    diag = jnp.where(on_diag, gram, 0.0)
    scale_row = lax.rsqrt(jnp.sum(diag, axis=0, keepdims=True))
    scale_col = lax.rsqrt(jnp.sum(diag, axis=1, keepdims=True))
    base = gram * scale_col * scale_row - eye
    low = weight * base
    for dot in (dot1, dot3):
        moved = dot(low, base)
        crossed = dot(low + moved - base, low, NT)
        step = weight * (base - low - moved + crossed - low * eye)
        low = low + step - dot1(step, low)
    close = jnp.sum(step * step) <= CORRECTION_MAX
    work[0] = low

    @pl.when(jnp.logical_not(close))
    def _():
        work[0] = eye
        work[1] = base + eye

        def eliminate(j, carry):
            left = work[1]
            pivot_row = work[1, pl.ds(j, 1), :]
            pivot = jnp.sum(jnp.where(cols[:1] == j, pivot_row, 0.0), axis=1, keepdims=True)
            column = jnp.sum(jnp.where(cols == j, left, 0.0), axis=1, keepdims=True)
            factor = jnp.where(rows[:, :1] > j, column / pivot, 0.0)
            right_row = work[0, pl.ds(j, 1), :]
            work[1] = left - factor * pivot_row
            work[0] = work[0] - factor * right_row
            work[0, pl.ds(j, 1), :] = right_row * lax.rsqrt(pivot)
            return carry

        lax.fori_loop(0, n, eliminate, 0)
        work[0] = eye - work[0]

    return scale_row, close


def masks(n):
    rows = lax.broadcasted_iota(jnp.int32, (n, n), 0)
    cols = lax.broadcasted_iota(jnp.int32, (n, n), 1)
    return rows > cols, rows == cols


def halved(place, a, b, whole, mine, other):
    n = whole.shape[0]
    half = n // 2
    below, diagonal = masks(n)
    whole[...] = jnp.where(jnp.logical_or(below, diagonal), b, a)
    row = jnp.sum(jnp.where(diagonal, a, 0.0), axis=0, keepdims=True)
    here = pl.multiple_of((place[1] & 1) * half, half)
    for ref, start in ((mine, here), (other, half - here)):
        ref[:half, :] = whole[pl.ds(start, half), :]
        ref[half:, :] = jnp.broadcast_to(row, (DIAGONAL_ROWS, n))


def unhalved(place, mine, other, whole):
    n = whole.shape[0]
    half = n // 2
    here = pl.multiple_of((place[1] & 1) * half, half)
    whole[pl.ds(here, half), :] = mine[:half, :]
    whole[pl.ds(half - here, half), :] = other[:half, :]
    stored = whole[...]
    turned = stored.T
    below, diagonal = masks(n)
    a = jnp.where(diagonal, mine[half : half + 1, :], jnp.where(below, turned, stored))
    return a, jnp.where(jnp.logical_or(below, diagonal), stored, turned)


def scaled(x, scale, low, dot):
    x = x * scale
    return x - dot(x, low, NT)


def factors_kernel(total_rows, place, mine, other, low_ref, scale_ref, both_low_ref, both_scale_ref, flags, whole, work):
    n = whole.shape[0]
    _, on_diag = masks(n)
    first, second = unhalved(place, mine, other, whole)
    scale, close = inverse_factor(first / total_rows, work)
    low = work[0]
    low_ref[...] = low
    scale_ref[...] = scale
    inverse = on_diag.astype(F32) - low
    inflation = jnp.sum(inverse * inverse) / n
    flags[0] = jnp.logical_and(close, inflation <= INFLATION_MAX).astype(jnp.int32)
    scale_col = jnp.sum(jnp.where(on_diag, scale, 0.0), axis=1, keepdims=True)
    raw = second / total_rows * scale * scale_col
    raw = raw - dot3(low, raw)
    raw = raw - dot3(raw, low, NT)
    next_scale, next_close = inverse_factor(raw, work)
    next_low = work[0]
    flags[1] = next_close.astype(jnp.int32)
    next_col = jnp.sum(jnp.where(on_diag, next_scale, 0.0), axis=1, keepdims=True)
    moved = next_col * low
    both_low_ref[...] = moved + next_low * next_scale - dot3(next_low, moved)
    both_scale_ref[...] = next_scale


def factors(place, halves, total_rows):
    n = halves[0].shape[1]
    square, row = jax.ShapeDtypeStruct((n, n), F32), jax.ShapeDtypeStruct((1, n), F32)
    return pl.pallas_call(
        functools.partial(factors_kernel, total_rows),
        out_shape=(square, row, square, row, jax.ShapeDtypeStruct((2,), jnp.int32)),
        in_specs=[SMEM, VMEM, VMEM],
        out_specs=(VMEM, VMEM, VMEM, VMEM, SMEM),
        scratch_shapes=[pltpu.VMEM((n, n), F32), pltpu.VMEM((2, n, n), F32)],
        cost_estimate=cost(60 * n**3, 8 * n * n),
        compiler_params=vmem(0),
        name="factors",
    )(place, *halves)


def finish_kernel(flags, product, scale, low, next_scale, out_ref, done, sems):
    step = product.shape[0] // sems.shape[0]
    copies = []

    def write(dot, here):
        x = product[here, :] * scale[...]
        done[here, :] = x * next_scale[...] - dot(x, low[...], NT)

    for i in range(sems.shape[0]):
        here = pl.ds(i * step, step)
        pl.when(flags[1] > 0)(functools.partial(write, dot3, here))
        pl.when(flags[1] <= 0)(functools.partial(write, dot6, here))
        copies.append(pltpu.make_async_copy(done.at[here, :], out_ref.at[here, :], sems.at[i]))
        copies[-1].start()
    for copy in copies:
        copy.wait()


def finish(flags, product, scale, low, next_scale):
    return pl.pallas_call(
        finish_kernel,
        out_shape=pltpu.HBM(product.shape, F32),
        in_specs=[SMEM] + [VMEM] * 4,
        out_specs=ANY,
        scratch_shapes=[pltpu.VMEM(product.shape, F32), pltpu.SemaphoreType.DMA((4,))],
        cost_estimate=cost(6 * product.size * product.shape[1], 8 * product.size),
        compiler_params=vmem(4 * product.size),
        name="finish",
    )(flags, *held(product, scale, low, next_scale))


def with_tables(near, refs):
    out, used = [], 0
    spare = list(refs[sum(n for _, n in near) :])
    for k, n in near:
        chunks, used = refs[used : used + n], used + n
        table = chunks[0]
        if n > 1:
            table, rows = spare.pop(0), chunks[0].shape[0]
            for i, chunk in enumerate(chunks):
                table[pl.ds(i * rows, rows), :] = chunk[...]
        out.append((k, table))
    return out


def tables(near):
    rows = [sum(c.shape[0] for c in chunks) for _, chunks in near if len(chunks) > 1]
    return [pltpu.VMEM((n, near[0][1][0].shape[1]), BF16) for n in rows]


def counts(near):
    return [(k, len(chunks)) for k, chunks in near]


def flat(near):
    return [chunk for _, chunks in near for chunk in chunks]


def add_near(shape, place, near_cols, tiles, near, r, acc):
    blocks, sources, per_source, tile = shape
    for k, ref in near:
        first = (r * sources + (place[0] ^ k)) * per_source
        for n in range(per_source):
            start = pl.multiple_of(near_cols[first + n] * tile, tile)
            part = jnp.dot(tiles[first + n], ref[pl.ds(start, tile), :], preferred_element_type=F32)
            acc = part if acc is None else acc + part
    return acc


def load_kernel(n, *refs):
    ins, outs, sems = refs[:n], refs[-n - 1 : -1], refs[-1]
    copies = [pltpu.make_async_copy(ins[i], outs[i], sems.at[i]) for i in range(n)]
    for copy in copies:
        copy.start()
    for copy in copies:
        copy.wait()


def load(token, *arrays):
    n = len(arrays)
    return pl.pallas_call(
        functools.partial(load_kernel, n),
        out_shape=tuple(pltpu.VMEM(a.shape, a.dtype) for a in arrays),
        in_specs=[ANY] * (n + 1),
        out_specs=(VMEM,) * n,
        scratch_shapes=[pltpu.SemaphoreType.DMA((n,))],
        cost_estimate=cost(0, sum(a.size * 4 for a in arrays)),
        compiler_params=vmem(0),
        name="load",
    )(*outside(*arrays), token)


def outside(*arrays):
    return [pltpu.with_memory_space_constraint(a, pltpu.HBM) for a in arrays]


def held(*arrays):
    return [pltpu.with_memory_space_constraint(a, pltpu.VMEM) for a in arrays]


def relay_kernel(x_ref, *refs):
    refs[-1][...] = x_ref[...]


def relay(x, *tokens):
    return pl.pallas_call(
        relay_kernel,
        out_shape=pltpu.VMEM(x.shape, x.dtype),
        in_specs=[VMEM] + [ANY] * len(tokens),
        out_specs=VMEM,
        cost_estimate=cost(0, 0),
        compiler_params=vmem(0),
        name="relay",
    )(*held(x), *tokens)


def prepare_kernel(rows, need, out_ref):
    n, width = rows.shape
    out_ref[:n, :] = rows[...]
    lanes = lax.broadcasted_iota(jnp.int32, (NEED_ROWS, width), 1)
    needs = jnp.zeros((NEED_ROWS, width), F32)
    for h in range(need.shape[0]):
        needs = jnp.where(lanes == h, need[h].astype(F32), needs)
    out_ref[n:, :] = needs.astype(BF16)


def prepare(rows, need):
    n, width = rows.shape
    return pl.pallas_call(
        prepare_kernel,
        out_shape=pltpu.VMEM((n + NEED_ROWS, width), BF16),
        in_specs=[VMEM, SMEM],
        out_specs=VMEM,
        cost_estimate=cost(0, 0),
        compiler_params=vmem(4 * rows.size),
        name="prepare",
    )(rows, need)


def pack_kernel(tile, n, place, wanted, *refs):
    out_ref = refs[-1]
    size = tile + NEED_ROWS
    for i, ref in enumerate(refs[:n]):
        start = pl.multiple_of(jnp.maximum(wanted[place[1] ^ (2 * i)], 0) * tile, tile)
        out_ref[i * size : i * size + tile, :] = ref[pl.ds(start, tile), :]
        out_ref[i * size + tile : (i + 1) * size, :] = ref[ref.shape[0] - NEED_ROWS :, :]


def pack(tile, place, wanted, rows, tokens):
    return pl.pallas_call(
        functools.partial(pack_kernel, tile, len(rows)),
        out_shape=pltpu.VMEM((len(rows) * (tile + NEED_ROWS), rows[0].shape[1]), BF16),
        in_specs=[SMEM] * 2 + [VMEM] * len(rows) + [ANY] * len(tokens),
        out_specs=VMEM,
        cost_estimate=cost(0, 0),
        compiler_params=vmem(0),
        name="pack",
    )(place, wanted, *held(*rows), *tokens)


def core_pack_kernel(tile, own, *refs):
    out_ref = refs[-1]
    out_ref[:tile, :] = own[...]
    for i, ref in enumerate(refs[:-1], 1):
        out_ref[i * tile : (i + 1) * tile, :] = ref[tile:, :]


def core_pack(own, received):
    tile, width = own.shape
    n = 1 + len(received)
    return pl.pallas_call(
        functools.partial(core_pack_kernel, tile),
        out_shape=pltpu.VMEM((n * tile, width), BF16),
        in_specs=[VMEM] * n,
        out_specs=VMEM,
        cost_estimate=cost(0, 0),
        compiler_params=vmem(0),
        name="core_pack",
    )(*held(own, *received))


def near_kernel(shape, near, place, near_cols, *refs):
    blocks, _, _, tile = shape
    n = sum(count for _, count in near)
    tiles, out_ref = refs[n : n + 2]
    near_tables = with_tables(near, (*refs[:n], *refs[n + 2 :]))
    for r in range(blocks):
        out_ref[pl.ds(r * tile, tile), :] = add_near(shape, place, near_cols, tiles, near_tables, r, None)


def near_product(shape, scalars, near, tiles):
    blocks, _, _, tile = shape
    rows = flat(near)
    return pl.pallas_call(
        functools.partial(near_kernel, shape, counts(near)),
        out_shape=pltpu.VMEM((blocks * tile, rows[0].shape[1]), F32),
        in_specs=[SMEM] * 2 + [VMEM] * (len(rows) + 1),
        out_specs=VMEM,
        scratch_shapes=tables(near),
        cost_estimate=cost(0, 0),
        compiler_params=vmem(0),
        name="near",
    )(*scalars[:2], *held(*rows, tiles))


def far_table(place, need, far, packed, table):
    tile = table.shape[1]
    size = tile + NEED_ROWS
    for i in range(len(far) + 1):
        h = place[1] ^ (2 * i)
        table[h ^ 1] = packed[i * size : i * size + tile, :]
        if i:
            start = pl.multiple_of(jnp.maximum(need[h], 0) * tile, tile)
            table[h] = far[i - 1][pl.ds(start, tile), :]


def add_far(far_groups, tiles, table, r, blocks, acc):
    each = tiles.shape[0] // blocks
    for t in range(r * each, (r + 1) * each):
        acc = acc + jnp.dot(tiles[t], table[far_groups[t]], preferred_element_type=F32)
    return acc


def gram_of(rows, tile):
    gram = None
    for start in range(0, rows.shape[0], tile):
        both = jnp.concatenate(parts(rows[pl.ds(start, tile), :]), axis=1)
        part = lax.dot_general(both, both, TN, preferred_element_type=F32)
        gram = part if gram is None else gram + part
    n = rows.shape[1]
    crossed = gram[:n, n:]
    return gram[:n, :n] + (crossed + crossed.T) + gram[n:, n:]


def late_kernel(shape, place, far_groups, need, partial, *refs):
    blocks, _, _, tile = shape
    *far, packed, tiles = refs[: need.shape[0] // 2 + 1]
    product_ref, rounded_ref, first_ref, second_ref, table = refs[need.shape[0] // 2 + 1 :]
    far_table(place, need, far, packed, table)
    for r in range(blocks):
        here = pl.ds(r * tile, tile)
        acc = add_far(far_groups, tiles, table, r, blocks, partial[here, :])
        product_ref[here, :] = acc
        rounded_ref[here, :] = acc.astype(BF16)
        half_ref, q = (first_ref, r) if r < blocks // 2 else (second_ref, r - blocks // 2)
        half_ref[pl.ds(q * tile, tile), :] = acc.astype(BF16)


def late(shape, scalars, need, partial, far, tiles):
    n, width = partial.shape
    groups, (blocks, _, _, tile) = need.shape[0], shape
    half = pltpu.VMEM((n // 2, width), BF16)
    return pl.pallas_call(
        functools.partial(late_kernel, shape),
        out_shape=(pltpu.VMEM((n, width), F32), pltpu.VMEM((n, width), BF16), half, half),
        in_specs=[SMEM] * 3 + [VMEM] * (len(far) + 2),
        out_specs=(VMEM,) * 4,
        scratch_shapes=[pltpu.VMEM((groups, tile, width), BF16)],
        cost_estimate=cost(0, 0),
        compiler_params=vmem(0),
        name="late",
    )(scalars[0], scalars[2], need, *held(partial, *far, tiles))


def gram_kernel(tile, product, out_ref):
    out_ref[...] = gram_of(product, tile)


def gram(tile, product):
    width = product.shape[1]
    return pl.pallas_call(
        functools.partial(gram_kernel, tile),
        out_shape=pltpu.VMEM((width, width), F32),
        in_specs=[VMEM],
        out_specs=VMEM,
        cost_estimate=cost(0, 0),
        compiler_params=vmem(0),
        name="gram",
    )(*held(product))


def halves_kernel(place, a, b, mine, other, whole):
    halved(place, a[...], b[...], whole, mine, other)


def halves_of(place, a, b):
    n = a.shape[0]
    half = pltpu.VMEM((n // 2 + DIAGONAL_ROWS, n), F32)
    return pl.pallas_call(
        halves_kernel,
        out_shape=(half, half),
        in_specs=[SMEM] + [VMEM] * 2,
        out_specs=(VMEM,) * 2,
        scratch_shapes=[pltpu.VMEM((n, n), F32)],
        compiler_params=vmem(0),
        name="halves",
    )(place, a, b)


def blocks_kernel(tile, n_far, place, rounded, *refs):
    *far, packed = refs[:n_far]
    own_ref, *outs = refs[n_far + 1 :]
    lane = lax.broadcasted_iota(jnp.int32, (1, rounded.shape[1]), 1) == place[1]
    size = tile + NEED_ROWS

    def wanted_block(k):
        ref, first = (packed, k // 2 * size + tile) if k % 2 else (far[k // 2 - 1], far[0].shape[0] - NEED_ROWS)
        needs = ref[first : first + NEED_ROWS, :].astype(F32)[:1]
        block = jnp.maximum(jnp.sum(jnp.where(lane, needs, 0.0)).astype(jnp.int32), 0)
        return rounded[pl.ds(pl.multiple_of(block * tile, tile), tile), :]

    own_ref[...] = wanted_block(1)
    for i, out_ref in enumerate(outs, 1):
        out_ref[:tile, :] = wanted_block(2 * i)
        out_ref[tile:, :] = wanted_block(2 * i + 1)


def blocks_for_others(tile, place, rounded, far, token):
    width = rounded.shape[1]
    pair = pltpu.VMEM((2 * tile, width), BF16)
    return pl.pallas_call(
        functools.partial(blocks_kernel, tile, len(far)),
        out_shape=(pltpu.VMEM((tile, width), BF16), *(pair,) * (len(far) - 1)),
        in_specs=[SMEM] + [VMEM] * (1 + len(far)) + [ANY],
        out_specs=(VMEM,) * len(far),
        cost_estimate=cost(0, 0),
        compiler_params=vmem(0),
        name="blocks",
    )(place, *held(rounded, *far), token)


def last_kernel(shape, near, n_far, place, near_cols, far_groups, partial, *refs):
    blocks, _, _, tile = shape
    n = sum(count for _, count in near)
    packed, far = refs[n], refs[n + 1 : n + n_far]
    refs = (*refs[:n], *refs[n + n_far :])
    past, tiles_near, tiles_far, product_ref, mine, other, whole, table = refs[n : n + 8]
    near_tables = with_tables(near, (*refs[:n], *refs[n + 8 :]))
    for i in range(len(far) + 1):
        table[place[1] ^ (2 * i + 1)] = packed[i * tile : (i + 1) * tile, :]
        if i:
            table[place[1] ^ (2 * i)] = far[i - 1][:tile, :]
    for r in range(blocks):
        here = pl.ds(r * tile, tile)
        acc = add_near(shape, place, near_cols, tiles_near, near_tables, r, partial[here, :])
        product_ref[here, :] = add_far(far_groups, tiles_far, table, r, blocks, acc)
    halved(place, past[...], gram_of(product_ref, tile), whole, mine, other)


def last(shape, groups, scalars, partial, near, far, tiles_near, tiles_far, past):
    rows = flat(near)
    width = partial.shape[1]
    half = pltpu.VMEM((width // 2 + DIAGONAL_ROWS, width), F32)
    return pl.pallas_call(
        functools.partial(last_kernel, shape, counts(near), len(far)),
        out_shape=(pltpu.VMEM(partial.shape, F32), half, half),
        in_specs=[SMEM] * 3 + [VMEM] * (len(rows) + len(far) + 4),
        out_specs=(VMEM,) * 3,
        scratch_shapes=[
            pltpu.VMEM((width, width), F32),
            pltpu.VMEM((groups, shape[3], width), BF16),
            *tables(near),
        ],
        cost_estimate=cost(0, 0),
        compiler_params=vmem(0),
        name="last",
    )(*scalars, *held(partial, *rows, *far, past, tiles_near, tiles_far))


def swap(x, axis, mask):
    size = lax.axis_size(axis)
    return lax.ppermute(x, axis, [(i, i ^ mask) for i in range(size)])


def near_rows(rows, chunks, tokens):
    step = lax.axis_size("blk") // 2
    here = [(0, [rows]), (step, [swap(x, "blk", step) for x in chunks])]
    while step > 1:
        step //= 2
        direct = swap(rows, "blk", step)
        moved = [(step, [direct])]
        for k, (*before, after) in here[1:]:
            sent = [swap(x, "blk", step) for x in before]
            sent.append(swap(relay(after, direct, *sent, *tokens), "blk", step))
            moved.append((k | step, sent))
        here += moved
    return here


def bits(size, scale):
    return [scale << i for i in range(size.bit_length() - 1)]


def everywhere(mine, other):
    positions = lax.axis_size("blk")
    chips, places = bits(lax.axis_size("grp"), positions)[1:], bits(positions, 1)
    x = mine + swap(other, "grp", 1)
    while chips or places:
        a, b = chips[:1], places[:1]
        chips, places = chips[1:], places[1:]
        if a and b:
            x = (x + swap(x, AXES, a[0])) + (swap(x, AXES, b[0]) + swap(x, AXES, a[0] | b[0]))
        else:
            x = x + swap(x, AXES, (a + b)[0])
    return x, swap(x, "grp", 1)


def per_device(tiles_near, near_cols, tiles_far, far_groups, need_blocks, start_vectors):
    tile = tiles_near.shape[1]
    blocks = start_vectors.shape[0] // tile
    sources = lax.axis_size("blk")
    groups = lax.axis_size("grp")
    shape = (blocks, sources, tiles_near.shape[0] // (blocks * sources), tile)
    total_rows = start_vectors.shape[0] * sources * groups
    place = jnp.stack([lax.axis_index("blk"), lax.axis_index("grp")]).astype(jnp.int32)
    scalars = (place, near_cols.reshape(-1), far_groups.reshape(-1))
    need = need_blocks.reshape(-1)
    wanted = swap(need_blocks, "grp", 1).reshape(-1)
    split = 3 * sources // 4

    def begin(rows):
        below = prepare(rows, need)
        far = [swap(below, "grp", k) for k in range(2, groups, 2)]
        near = near_rows(rows, [rows], ())
        near[0] = (0, [below])
        tiles = load(near[1][1][0], tiles_near, tiles_far)
        far.append(swap(pack(tile, place, wanted, [below, *far], [*near[-1][1], *tiles]), "grp", 1))
        partial = near_product(shape, scalars, near, tiles[0])
        return tiles, far, late(shape, scalars, need, partial, far, tiles[1])

    tiles, far, (product, rounded, first, second) = begin(start_vectors)
    past = gram(tile, product)
    own, *outs = blocks_for_others(tile, place, rounded, far, past)
    near = near_rows(rounded, [first, second], ())
    far = [swap(x, "grp", 2 * i) for i, x in enumerate(outs, 1)]
    far.insert(0, swap(core_pack(own, far), "grp", 1))
    partial = near_product(shape, scalars, near[:split], tiles[0])
    moved, *halves = last(shape, groups, scalars, partial, near[split:], far, *tiles, past)
    low, scale, both_low, next_scale, flags = factors(place, everywhere(*halves), total_rows)

    def quick(start, moved, low, scale, both_low, next_scale, flags):
        return finish(flags, moved, scale, both_low, next_scale)

    def plain(start, moved, low, scale, both_low, next_scale, flags):
        _, _, (product, *_) = begin(start)
        current = scaled(product, scale, low, dot6).astype(BF16)
        _, _, (product, *_) = begin(current)
        unit = jnp.eye(product.shape[1], dtype=F32) * start.shape[0]
        halves = everywhere(*halves_of(place, unit, gram(tile, product)))
        _, scale, both_low, next_scale, flags = factors(place, halves, total_rows)
        return finish(flags, product, scale, both_low, next_scale)

    return lax.cond(flags[0] > 0, quick, plain, start_vectors, moved, low, scale, both_low, next_scale, flags)


def solution(mesh):
    in_specs = (
        P(AXES, None, None),
        P(AXES, None),
        P(AXES, None, None),
        P(AXES, None),
        P(AXES, None),
        P(AXES, None),
    )
    return jax.shard_map(
        per_device, mesh=mesh, in_specs=in_specs, out_specs=P(AXES, None), check_vma=False
    )
```

time: 447 us -> 171 us (0.38)
  waiting for transfers between devices: 340 us -> 58.4 us
  starting transfers between devices: 0.38 us -> 56.4 us
  Pallas kernels: 0 us -> 53.8 us
  other arithmetic: 51.2 us -> 0.14 us
  local copies, waits for them, and re-layouts: 23.3 us -> 0.02 us
  matrix products: 16.2 us -> 0.58 us
  between operations: 13.6 us -> 0.45 us
    psum x2 -> x0, waiting for transfers between devices: 231 us -> none  [per_device(): gram = lax.psum(local_gram, ('grp', 'blk')) / total_rows]
    all_gather x4 -> x0, waiting for transfers between devices: 107 us -> none  [the longest x2 55.1 us: per_device(): group_table = lax.all_gather(local_rows, 'blk', axis=0, tiled=True)]
    ppermute x0 -> x47, waiting for transfers between devices: none -> 58.4 us  [swap(): return lax.ppermute(x, axis, [(i, i ^ mask) for i in range(size)])]
    ppermute x0 -> x47, starting transfers between devices: none -> 56.4 us  [swap(): return lax.ppermute(x, axis, [(i, i ^ mask) for i in range(size)])]
    pallas_call x0 -> x29, Pallas kernels: none -> 53.8 us  [the longest x2 20.6 us: factors(): pl.pallas_call(functools.partial(factors_kernel, total_rows), out_shape=(...]
    another operation x10 -> x1, other arithmetic: 45.7 us -> 0.07 us  [per_device(): jnp.stack([lax.axis_index('blk'), lax.axis_index('grp')]).astype(jnp.int32)]
    gather x6 -> x0, local copies, waits for them, and re-layouts: 15.4 us -> none  [the longest x4 8.61 us: per_device(): far_rows = everything[far_index * blocks + wanted[far_index]]]
    dot_general x8 -> x1, matrix products: 15.6 us -> 0.58 us  [dot6(): lax.dot_general(a, b, dims, precision=HIGHEST, preferred_element_type=F32)]
  transfers between devices with their start and end apart: 6 -> 47, of which waited for: 6 -> 29; matrix products, arithmetic and copies ran while one was open for 3% -> 0% of each run, Pallas kernels for 0% -> 12%
where the time goes in v2:
time: 171 us; the launch traced here: 170 us
  waiting for transfers between devices  58.4 us (34%)
  starting transfers between devices  56.4 us (33%)
  Pallas kernels  53.8 us (31%)
    ppermute x47, waiting for transfers between devices, swap(): return lax.ppermute(x, axis, [(i, i ^ mask) for i in range(size)])  58.4 us
    ppermute x47, starting transfers between devices, swap(): return lax.ppermute(x, axis, [(i, i ^ mask) for i in range(size)])  56.4 us
    pallas_call x2, Pallas kernels, factors(): pl.pallas_call(functools.partial(factors_kernel, total_rows), out_shape=(...  20.6 us
    pallas_call x3, Pallas kernels, load(): pl.pallas_call(functools.partial(load_kernel, n), out_shape=tuple((pltpu....  9.55 us
    pallas_call x4, Pallas kernels, near_product(): pl.pallas_call(functools.partial(near_kernel, shape, counts(near)), out_s...  6.97 us
    pallas_call x3, Pallas kernels, late(): pl.pallas_call(functools.partial(late_kernel, shape), out_shape=(pltpu.VM...  6.27 us
  transfers between devices with their start and end apart: 47, of which 29 were waited for; matrix products, arithmetic and copies ran while one was open for 0% of the time, Pallas kernels for 12%

profile of v2, /device:TPU:0, one launch (start us, length us, event | category | flops | bytes accessed | tf_op | source)
XLA Modules:
  0.0 170.4 jit_solution(4267580708976138854)
XLA Ops:
  0.0 4.0 %collective-permute-start.22 = (bf16[1024,128]{1,0:T(8,128)(2,1)}, bf16[1024,128]{1,0:T(8,128)(2,1)S(1)}, u32[]{:S(2)}, u32[]{:S(2)}) collective-permute-start(bf16[1024,128]{1,0:T(8,128)(2,1)} %rows.1), channel_id=1, source_target_pairs={{0,2},{1,3},{2,0},{3,1},{4,6},{5,7},{6,4},{7,5},{8,10},{9,11},{10,... | collective-permute-start | bytes 786440 | tf_op jit(solution)/shard_map/ppermute | solution.py:542
  10.2 6.1 %collective-permute-done.22.x_ref.refs_2_.refs_1_ = bf16[1024,128]{1,0:T(8,128)(2,1)S(1)} collective-permute-done((bf16[1024,128]{1,0:T(8,128)(2,1)}, bf16[1024,128]{1,0:T(8,128)(2,1)S(1)}, u32[]{:S(2)}, u32[]{:S(2)}) %collective-permute-start.22) | collective-permute-done | bytes 262176 | tf_op jit(solution)/shard_map/ppermute | solution.py:542
  18.1 3.2 %load.5 = (bf16[32,256,256]{2,1,0:T(8,128)(2,1)S(1)}, bf16[24,256,256]{2,1,0:T(8,128)(2,1)S(1)}) custom-call(bf16[32,256,256]{2,1,0:T(8,128)(2,1)} %refs_0_.1, bf16[24,256,256]{2,1,0:T(8,128)(2,1)} %refs_1_.1, bf16[1024,128]{1,0:T(8,128)(2,1)S(1)} %collective-permute-done.22.x_ref.refs_2_.refs_1_), custom_call_target="tpu_custom_call" | custom-call | bytes 14680064 | tf_op jit(solution)/shard_map/load/pallas_call | solution.py:251
  21.4 2.4 %collective-permute-done.24.refs_3_.refs_4_ = bf16[1024,128]{1,0:T(8,128)(2,1)S(1)} collective-permute-done((bf16[1024,128]{1,0:T(8,128)(2,1)S(1)}, bf16[1024,128]{1,0:T(8,128)(2,1)S(1)}, u32[]{:S(2)}, u32[]{:S(2)}) %collective-permute-start.24) | collective-permute-done | bytes 262176 | tf_op jit(solution)/shard_map/ppermute | solution.py:542
  27.9 3.1 %collective-permute-start.30 = (bf16[512,128]{1,0:T(8,128)(2,1)S(1)}, bf16[512,128]{1,0:T(8,128)(2,1)S(1)}, u32[]{:S(2)}, u32[]{:S(2)}) collective-permute-start(bf16[512,128]{1,0:T(8,128)(2,1)S(1)} %get-tuple-element.86), channel_id=1, source_target_pairs={{0,2},{1,3},{2,0},{3,1},{4,6},{5,7},{6,4},{7,5},{8,10},{9,11},{10,... | collective-permute-start | bytes 393224 | tf_op jit(solution)/shard_map/ppermute | solution.py:542
  39.7 2.6 %collective-permute-start.33 = (bf16[512,128]{1,0:T(8,128)(2,1)S(1)}, bf16[512,128]{1,0:T(8,128)(2,1)S(1)}, u32[]{:S(2)}, u32[]{:S(2)}) collective-permute-start(bf16[512,128]{1,0:T(8,128)(2,1)S(1)} %collective-permute-done.30.refs_1_), channel_id=1, source_target_pairs={{0,1},{1,0},{2,3},{3,2},{4,5},{5,4},{6,7},{7,6},{8,9},{9,8},{10,11... | collective-permute-start | bytes 393224 | tf_op jit(solution)/shard_map/ppermute | solution.py:542
  43.4 3.8 %collective-permute-done.31.refs_2_.x_ref = bf16[512,128]{1,0:T(8,128)(2,1)S(1)} collective-permute-done((bf16[512,128]{1,0:T(8,128)(2,1)S(1)}, bf16[512,128]{1,0:T(8,128)(2,1)S(1)}, u32[]{:S(2)}, u32[]{:S(2)}) %collective-permute-start.31) | collective-permute-done | bytes 131104 | tf_op jit(solution)/shard_map/ppermute | solution.py:542
  49.9 2.4 %collective-permute-done.34.refs_1_ = bf16[512,128]{1,0:T(8,128)(2,1)S(1)} collective-permute-done((bf16[512,128]{1,0:T(8,128)(2,1)S(1)}, bf16[512,128]{1,0:T(8,128)(2,1)S(1)}, u32[]{:S(2)}, u32[]{:S(2)}) %collective-permute-start.34) | collective-permute-done | bytes 131104 | tf_op jit(solution)/shard_map/ppermute | solution.py:542
  52.3 2.3 %last.1 = (f32[1024,128]{1,0:T(8,128)S(1)}, f32[72,128]{1,0:T(8,128)S(1)}, f32[72,128]{1,0:T(8,128)S(1)}) custom-call(s32[2]{0:T(128)S(1)} %pad_add_fusion.place, s32[32]{0:T(128)S(1)} %bitcast.16, s32[24]{0:T(128)S(1)} %bitcast.19, f32[1024,128]{1,0:T(8,128)S(1)} %near.7.partial, bf16[512,128]{1,0:T(8,128)(2,1)S(1)} %collective-permute-done.33.refs_1_.refs_0_, ...), custom_call_target="tpu_custom_call" | custom-call | tf_op jit(solution)/shard_map/last/pallas_call | solution.py:524
  67.8 3.1 %collective-permute-done.45 = f32[72,128]{1,0:T(8,128)S(1)} collective-permute-done((f32[72,128]{1,0:T(8,128)S(1)}, f32[72,128]{1,0:T(8,128)S(1)}, u32[]{:S(2)}, u32[]{:S(2)}) %collective-permute-start.45) | collective-permute-done | bytes 36896 | tf_op jit(solution)/shard_map/ppermute | solution.py:542
  72.4 17.0 %factors.3 = (f32[128,128]{1,0:T(8,128)S(1)}, f32[1,128]{1,0:T(1,128)S(1)}, f32[128,128]{1,0:T(8,128)S(1)}, f32[1,128]{1,0:T(1,128)S(1)}, s32[2]{0:T(128)S(1)}) custom-call(s32[2]{0:T(128)S(1)} %pad_add_fusion.place, f32[72,128]{1,0:T(8,128)S(1)} %add_add_fusion.2.mine, f32[72,128]{1,0:T(8,128)S(1)} %collective-permute-done.46.other), custom_call_target="tpu_custom_call" | custom-call | flops 125829120 | bytes 131072 | tf_op jit(solution)/shard_map/factors/pallas_call | solution.py:159
  89.4 80.8 %conditional.1 = (f32[1024,128]{1,0:T(8,128)}) conditional(s32[]{:T(128)} %bitcast.7, (bf16[1024,128]{1,0:T(8,128)(2,1)S(1)}, s32[8]{0:T(128)S(1)}, bf16[32,256,256]{2,1,0:T(8,128)(2,1)}, bf16[24,256,256]{2,1,0:T(8,128)(2,1)}, s32[2]{0:T(128)S(1)}, /*index=5*/s32[32]{0:T(128)S(1)}, s32[8]{0:T(128)S(1)}, s32[24]{0:T(128)S(1)}, f32[1,128]{1,0:T(1,128)S(1)}, ...), branch_computations={%region_0.0_spmd, %region_1.0_spmd} | conditional | flops 428309504 | bytes 48027000 | solution.py:623
  94.8 2.4 %collective-permute-start.5 = (bf16[1040,128]{1,0:T(8,128)(2,1)S(1)}, bf16[1040,128]{1,0:T(8,128)(2,1)S(1)}, u32[]{:S(2)}, u32[]{:S(2)}) collective-permute-start(bf16[1040,128]{1,0:T(8,128)(2,1)S(1)} %prepare.3.refs_0_), channel_id=1, source_target_pairs={{0,24},{4,28},{8,16},{12,20},{16,8},{20,12},{24,0},{28,4},{1,25},{... | collective-permute-start | bytes 798728 | tf_op jit(solution)/shard_map/cond/branch_0_fun/ppermute | solution.py:542
  97.2 7.4 %collective-permute-done.x_ref.refs_2_.refs_1_ = bf16[1024,128]{1,0:T(8,128)(2,1)S(1)} collective-permute-done((bf16[1024,128]{1,0:T(8,128)(2,1)S(1)}, bf16[1024,128]{1,0:T(8,128)(2,1)S(1)}, u32[]{:S(2)}, u32[]{:S(2)}) %collective-permute-start) | collective-permute-done | bytes 262176 | tf_op jit(solution)/shard_map/cond/branch_0_fun/ppermute | solution.py:542
  105.5 3.2 %load.3 = (bf16[32,256,256]{2,1,0:T(8,128)(2,1)S(1)}, bf16[24,256,256]{2,1,0:T(8,128)(2,1)S(1)}) custom-call(bf16[32,256,256]{2,1,0:T(8,128)(2,1)} %get-tuple-element.43.refs_0_, bf16[24,256,256]{2,1,0:T(8,128)(2,1)} %get-tuple-element.44.refs_1_, bf16[1024,128]{1,0:T(8,128)(2,1)S(1)} %collective-permute-done.x_ref.refs_2_.refs_1_), custom_call_target="tpu_custom_call" | custom-call | bytes 14680064 | tf_op jit(solution)/shard_map/cond/branch_0_fun/load/pallas_call | solution.py:251
  108.8 3.5 %collective-permute-done.2.refs_3_.refs_4_ = bf16[1024,128]{1,0:T(8,128)(2,1)S(1)} collective-permute-done((bf16[1024,128]{1,0:T(8,128)(2,1)S(1)}, bf16[1024,128]{1,0:T(8,128)(2,1)S(1)}, u32[]{:S(2)}, u32[]{:S(2)}) %collective-permute-start.2) | collective-permute-done | bytes 262176 | tf_op jit(solution)/shard_map/cond/branch_0_fun/ppermute | solution.py:542
  114.7 2.4 %late.3 = (f32[1024,128]{1,0:T(8,128)S(1)}, bf16[1024,128]{1,0:T(8,128)(2,1)}, bf16[512,128]{1,0:T(8,128)(2,1)}, bf16[512,128]{1,0:T(8,128)(2,1)}) custom-call(s32[2]{0:T(128)S(1)} %get-tuple-element.38.place, s32[24]{0:T(128)S(1)} %get-tuple-element.39.far_groups, s32[8]{0:T(128)S(1)} %get-tuple-element.40.need, f32[1024,128]{1,0:T(8,128)S(1)} %near.4.partial, ...), custom_call_target="tpu_custom_call" | custom-call | tf_op jit(solution)/shard_map/cond/branch_0_fun/late/pallas_call | solution.py:423
  117.7 2.2 %collective-permute-start.7 = (bf16[1024,128]{1,0:T(8,128)(2,1)S(1)}, bf16[1024,128]{1,0:T(8,128)(2,1)S(1)}, u32[]{:S(2)}, u32[]{:S(2)}) collective-permute-start(bf16[1024,128]{1,0:T(8,128)(2,1)S(1)} %fusion.rows), channel_id=1, source_target_pairs={{0,2},{1,3},{2,0},{3,1},{4,6},{5,7},{6,4},{7,5},{8,10},{9,11},{10,... | collective-permute-start | bytes 786440 | tf_op jit(solution)/shard_map/cond/branch_0_fun/ppermute | solution.py:542
  123.2 2.6 %collective-permute-start.12 = (bf16[1040,128]{1,0:T(8,128)(2,1)S(1)}, bf16[1040,128]{1,0:T(8,128)(2,1)S(1)}, u32[]{:S(2)}, u32[]{:S(2)}) collective-permute-start(bf16[1040,128]{1,0:T(8,128)(2,1)S(1)} %prepare.4.refs_0_), channel_id=1, source_target_pairs={{0,24},{4,28},{8,16},{12,20},{16,8},{20,12},{24,0},{28,4},{1,25},{... | collective-permute-start | bytes 798728 | tf_op jit(solution)/shard_map/cond/branch_0_fun/ppermute | solution.py:542
  125.7 7.3 %collective-permute-done.7.x_ref.refs_2_.refs_1_ = bf16[1024,128]{1,0:T(8,128)(2,1)S(1)} collective-permute-done((bf16[1024,128]{1,0:T(8,128)(2,1)S(1)}, bf16[1024,128]{1,0:T(8,128)(2,1)S(1)}, u32[]{:S(2)}, u32[]{:S(2)}) %collective-permute-start.7) | collective-permute-done | bytes 262176 | tf_op jit(solution)/shard_map/cond/branch_0_fun/ppermute | solution.py:542
  134.3 3.2 %load.4 = (bf16[32,256,256]{2,1,0:T(8,128)(2,1)S(1)}, bf16[24,256,256]{2,1,0:T(8,128)(2,1)S(1)}) custom-call(bf16[32,256,256]{2,1,0:T(8,128)(2,1)} %get-tuple-element.43.refs_0_, bf16[24,256,256]{2,1,0:T(8,128)(2,1)} %get-tuple-element.44.refs_1_, bf16[1024,128]{1,0:T(8,128)(2,1)S(1)} %collective-permute-done.7.x_ref.refs_2_.refs_1_), custom_call_target="tpu_custom_call" | custom-call | bytes 14680064 | tf_op jit(solution)/shard_map/cond/branch_0_fun/load/pallas_call | solution.py:251
  137.6 3.5 %collective-permute-done.9.refs_3_.refs_4_ = bf16[1024,128]{1,0:T(8,128)(2,1)S(1)} collective-permute-done((bf16[1024,128]{1,0:T(8,128)(2,1)S(1)}, bf16[1024,128]{1,0:T(8,128)(2,1)S(1)}, u32[]{:S(2)}, u32[]{:S(2)}) %collective-permute-start.9) | collective-permute-done | bytes 262176 | tf_op jit(solution)/shard_map/cond/branch_0_fun/ppermute | solution.py:542
  143.5 2.3 %late.4 = (f32[1024,128]{1,0:T(8,128)S(1)}, bf16[1024,128]{1,0:T(8,128)(2,1)}, bf16[512,128]{1,0:T(8,128)(2,1)}, bf16[512,128]{1,0:T(8,128)(2,1)}) custom-call(s32[2]{0:T(128)S(1)} %get-tuple-element.38.place, s32[24]{0:T(128)S(1)} %get-tuple-element.39.far_groups, s32[8]{0:T(128)S(1)} %get-tuple-element.40.need, f32[1024,128]{1,0:T(8,128)S(1)} %near.5.partial, ...), custom_call_target="tpu_custom_call" | custom-call | tf_op jit(solution)/shard_map/cond/branch_0_fun/late/pallas_call | solution.py:423
  164.2 3.6 %factors.2 = (f32[128,128]{1,0:T(8,128)}, f32[1,128]{1,0:T(1,128)S(1)}, f32[128,128]{1,0:T(8,128)S(1)}, f32[1,128]{1,0:T(1,128)S(1)}, s32[2]{0:T(128)S(1)}) custom-call(s32[2]{0:T(128)S(1)} %get-tuple-element.38.place, f32[72,128]{1,0:T(8,128)S(1)} %add_add_fusion.mine, f32[72,128]{1,0:T(8,128)S(1)} %collective-permute-done.21.other), custom_call_target="tpu_custom_call" | custom-call | flops 125829120 | bytes 131072 | tf_op jit(solution)/shard_map/cond/branch_0_fun/factors/pallas_call | solution.py:159
  (117 shorter events, 75.8 us)
Async XLA Ops:
  0.0 16.3 %collective-permute-start.22 = (bf16[1024,128]{1,0:T(8,128)(2,1)}, bf16[1024,128]{1,0:T(8,128)(2,1)S(1)}, u32[]{:S(2)}, u32[]{:S(2)}) collective-permute-start(bf16[1024,128]{1,0:T(8,128)(2,1)} %rows.1), channel_id=1, source_target_pairs={{0,2},{1,3},{2,0},{3,1},{4,6},{5,7},{6,4},{7,5},{8,10},{9,11},{10,... | collective-permute-start | bytes 786440 | tf_op jit(solution)/shard_map/ppermute | solution.py:542
  4.0 12.4 %collective-permute-start.23 = (bf16[1024,128]{1,0:T(8,128)(2,1)}, bf16[1024,128]{1,0:T(8,128)(2,1)S(1)}, u32[]{:S(2)}, u32[]{:S(2)}) collective-permute-start(bf16[1024,128]{1,0:T(8,128)(2,1)} %rows.1), channel_id=1, source_target_pairs={{0,1},{1,0},{2,3},{3,2},{4,5},{5,4},{6,7},{7,6},{8,9},{9,8},{10,11... | collective-permute-start | bytes 786440 | tf_op jit(solution)/shard_map/ppermute | solution.py:542
  6.6 14.7 %collective-permute-start.25 = (bf16[1040,128]{1,0:T(8,128)(2,1)S(1)}, bf16[1040,128]{1,0:T(8,128)(2,1)S(1)}, u32[]{:S(2)}, u32[]{:S(2)}) collective-permute-start(bf16[1040,128]{1,0:T(8,128)(2,1)S(1)} %prepare.5.refs_0_), channel_id=1, source_target_pairs={{0,8},{4,12},{8,0},{12,4},{16,24},{20,28},{24,16},{28,20},{1,9},{5... | collective-permute-start | bytes 798728 | tf_op jit(solution)/shard_map/ppermute | solution.py:542
  8.2 13.1 %collective-permute-start.26 = (bf16[1040,128]{1,0:T(8,128)(2,1)S(1)}, bf16[1040,128]{1,0:T(8,128)(2,1)S(1)}, u32[]{:S(2)}, u32[]{:S(2)}) collective-permute-start(bf16[1040,128]{1,0:T(8,128)(2,1)S(1)} %prepare.5.refs_0_), channel_id=1, source_target_pairs={{0,16},{4,20},{8,24},{12,28},{16,0},{20,4},{24,8},{28,12},{1,17},{... | collective-permute-start | bytes 798728 | tf_op jit(solution)/shard_map/ppermute | solution.py:542
  9.7 11.6 %collective-permute-start.27 = (bf16[1040,128]{1,0:T(8,128)(2,1)S(1)}, bf16[1040,128]{1,0:T(8,128)(2,1)S(1)}, u32[]{:S(2)}, u32[]{:S(2)}) collective-permute-start(bf16[1040,128]{1,0:T(8,128)(2,1)S(1)} %prepare.5.refs_0_), channel_id=1, source_target_pairs={{0,24},{4,28},{8,16},{12,20},{16,8},{20,12},{24,0},{28,4},{1,25},{... | collective-permute-start | bytes 798728 | tf_op jit(solution)/shard_map/ppermute | solution.py:542
  16.5 7.3 %collective-permute-start.24 = (bf16[1024,128]{1,0:T(8,128)(2,1)S(1)}, bf16[1024,128]{1,0:T(8,128)(2,1)S(1)}, u32[]{:S(2)}, u32[]{:S(2)}) collective-permute-start(bf16[1024,128]{1,0:T(8,128)(2,1)S(1)} %relay.6), channel_id=1, source_target_pairs={{0,1},{1,0},{2,3},{3,2},{4,5},{5,4},{6,7},{7,6},{8,9},{9,8},{10,11... | collective-permute-start | bytes 786440 | tf_op jit(solution)/shard_map/ppermute | solution.py:542
  27.9 10.2 %collective-permute-start.30 = (bf16[512,128]{1,0:T(8,128)(2,1)S(1)}, bf16[512,128]{1,0:T(8,128)(2,1)S(1)}, u32[]{:S(2)}, u32[]{:S(2)}) collective-permute-start(bf16[512,128]{1,0:T(8,128)(2,1)S(1)} %get-tuple-element.86), channel_id=1, source_target_pairs={{0,2},{1,3},{2,0},{3,1},{4,6},{5,7},{6,4},{7,5},{8,10},{9,11},{10,... | collective-permute-start | bytes 393224 | tf_op jit(solution)/shard_map/ppermute | solution.py:542
  31.1 16.2 %collective-permute-start.32 = (bf16[1024,128]{1,0:T(8,128)(2,1)S(1)}, bf16[1024,128]{1,0:T(8,128)(2,1)S(1)}, u32[]{:S(2)}, u32[]{:S(2)}) collective-permute-start(bf16[1024,128]{1,0:T(8,128)(2,1)S(1)} %get-tuple-element.85.refs_0_.rounded), channel_id=1, source_target_pairs={{0,1},{1,0},{2,3},{3,2},{4,5},{5,4},{6,7},{7,6},{8,9},{9,8},{10,11... | collective-permute-start | bytes 786440 | tf_op jit(solution)/shard_map/ppermute | solution.py:542
  35.5 7.9 %collective-permute-start.36 = (bf16[512,128]{1,0:T(8,128)(2,1)S(1)}, bf16[512,128]{1,0:T(8,128)(2,1)S(1)}, u32[]{:S(2)}, u32[]{:S(2)}) collective-permute-start(bf16[512,128]{1,0:T(8,128)(2,1)S(1)} %get-tuple-element.91), channel_id=1, source_target_pairs={{0,16},{4,20},{8,24},{12,28},{16,0},{20,4},{24,8},{28,12},{1,17},{... | collective-permute-start | bytes 393224 | tf_op jit(solution)/shard_map/ppermute | solution.py:542
  38.1 9.1 %collective-permute-start.31 = (bf16[512,128]{1,0:T(8,128)(2,1)S(1)}, bf16[512,128]{1,0:T(8,128)(2,1)S(1)}, u32[]{:S(2)}, u32[]{:S(2)}) collective-permute-start(bf16[512,128]{1,0:T(8,128)(2,1)S(1)} %get-tuple-element.87), channel_id=1, source_target_pairs={{0,2},{1,3},{2,0},{3,1},{4,6},{5,7},{6,4},{7,5},{8,10},{9,11},{10,... | collective-permute-start | bytes 393224 | tf_op jit(solution)/shard_map/ppermute | solution.py:542
  39.7 7.6 %collective-permute-start.33 = (bf16[512,128]{1,0:T(8,128)(2,1)S(1)}, bf16[512,128]{1,0:T(8,128)(2,1)S(1)}, u32[]{:S(2)}, u32[]{:S(2)}) collective-permute-start(bf16[512,128]{1,0:T(8,128)(2,1)S(1)} %collective-permute-done.30.refs_1_), channel_id=1, source_target_pairs={{0,1},{1,0},{2,3},{3,2},{4,5},{5,4},{6,7},{7,6},{8,9},{9,8},{10,11... | collective-permute-start | bytes 393224 | tf_op jit(solution)/shard_map/ppermute | solution.py:542
  43.3 9.0 %collective-permute-start.38 = (bf16[1024,128]{1,0:T(8,128)(2,1)S(1)}, bf16[1024,128]{1,0:T(8,128)(2,1)S(1)}, u32[]{:S(2)}, u32[]{:S(2)}) collective-permute-start(bf16[1024,128]{1,0:T(8,128)(2,1)S(1)} %core_pack.1), channel_id=1, source_target_pairs={{0,4},{4,0},{8,12},{12,8},{16,20},{20,16},{24,28},{28,24},{1,5},{5... | collective-permute-start | bytes 786440 | tf_op jit(solution)/shard_map/ppermute | solution.py:542
  89.6 15.0 %collective-permute-start = (bf16[1024,128]{1,0:T(8,128)(2,1)S(1)}, bf16[1024,128]{1,0:T(8,128)(2,1)S(1)}, u32[]{:S(2)}, u32[]{:S(2)}) collective-permute-start(bf16[1024,128]{1,0:T(8,128)(2,1)S(1)} %get-tuple-element.42.rows), channel_id=1, source_target_pairs={{0,2},{1,3},{2,0},{3,1},{4,6},{5,7},{6,4},{7,5},{8,10},{9,11},{10,... | collective-permute-start | bytes 786440 | tf_op jit(solution)/shard_map/cond/branch_0_fun/ppermute | solution.py:542
  91.4 13.2 %collective-permute-start.1 = (bf16[1024,128]{1,0:T(8,128)(2,1)S(1)}, bf16[1024,128]{1,0:T(8,128)(2,1)S(1)}, u32[]{:S(2)}, u32[]{:S(2)}) collective-permute-start(bf16[1024,128]{1,0:T(8,128)(2,1)S(1)} %get-tuple-element.42.rows), channel_id=1, source_target_pairs={{0,1},{1,0},{2,3},{3,2},{4,5},{5,4},{6,7},{7,6},{8,9},{9,8},{10,11... | collective-permute-start | bytes 786440 | tf_op jit(solution)/shard_map/cond/branch_0_fun/ppermute | solution.py:542
  93.6 15.1 %collective-permute-start.3 = (bf16[1040,128]{1,0:T(8,128)(2,1)S(1)}, bf16[1040,128]{1,0:T(8,128)(2,1)S(1)}, u32[]{:S(2)}, u32[]{:S(2)}) collective-permute-start(bf16[1040,128]{1,0:T(8,128)(2,1)S(1)} %prepare.3.refs_0_), channel_id=1, source_target_pairs={{0,8},{4,12},{8,0},{12,4},{16,24},{20,28},{24,16},{28,20},{1,9},{5... | collective-permute-start | bytes 798728 | tf_op jit(solution)/shard_map/cond/branch_0_fun/ppermute | solution.py:542
  94.3 14.5 %collective-permute-start.4 = (bf16[1040,128]{1,0:T(8,128)(2,1)S(1)}, bf16[1040,128]{1,0:T(8,128)(2,1)S(1)}, u32[]{:S(2)}, u32[]{:S(2)}) collective-permute-start(bf16[1040,128]{1,0:T(8,128)(2,1)S(1)} %prepare.3.refs_0_), channel_id=1, source_target_pairs={{0,16},{4,20},{8,24},{12,28},{16,0},{20,4},{24,8},{28,12},{1,17},{... | collective-permute-start | bytes 798728 | tf_op jit(solution)/shard_map/cond/branch_0_fun/ppermute | solution.py:542
  94.8 14.0 %collective-permute-start.5 = (bf16[1040,128]{1,0:T(8,128)(2,1)S(1)}, bf16[1040,128]{1,0:T(8,128)(2,1)S(1)}, u32[]{:S(2)}, u32[]{:S(2)}) collective-permute-start(bf16[1040,128]{1,0:T(8,128)(2,1)S(1)} %prepare.3.refs_0_), channel_id=1, source_target_pairs={{0,24},{4,28},{8,16},{12,20},{16,8},{20,12},{24,0},{28,4},{1,25},{... | collective-permute-start | bytes 798728 | tf_op jit(solution)/shard_map/cond/branch_0_fun/ppermute | solution.py:542
  104.6 7.6 %collective-permute-start.2 = (bf16[1024,128]{1,0:T(8,128)(2,1)S(1)}, bf16[1024,128]{1,0:T(8,128)(2,1)S(1)}, u32[]{:S(2)}, u32[]{:S(2)}) collective-permute-start(bf16[1024,128]{1,0:T(8,128)(2,1)S(1)} %relay.4), channel_id=1, source_target_pairs={{0,1},{1,0},{2,3},{3,2},{4,5},{5,4},{6,7},{7,6},{8,9},{9,8},{10,11... | collective-permute-start | bytes 786440 | tf_op jit(solution)/shard_map/cond/branch_0_fun/ppermute | solution.py:542
  117.7 15.4 %collective-permute-start.7 = (bf16[1024,128]{1,0:T(8,128)(2,1)S(1)}, bf16[1024,128]{1,0:T(8,128)(2,1)S(1)}, u32[]{:S(2)}, u32[]{:S(2)}) collective-permute-start(bf16[1024,128]{1,0:T(8,128)(2,1)S(1)} %fusion.rows), channel_id=1, source_target_pairs={{0,2},{1,3},{2,0},{3,1},{4,6},{5,7},{6,4},{7,5},{8,10},{9,11},{10,... | collective-permute-start | bytes 786440 | tf_op jit(solution)/shard_map/cond/branch_0_fun/ppermute | solution.py:542
  119.9 13.3 %collective-permute-start.8 = (bf16[1024,128]{1,0:T(8,128)(2,1)S(1)}, bf16[1024,128]{1,0:T(8,128)(2,1)S(1)}, u32[]{:S(2)}, u32[]{:S(2)}) collective-permute-start(bf16[1024,128]{1,0:T(8,128)(2,1)S(1)} %fusion.rows), channel_id=1, source_target_pairs={{0,1},{1,0},{2,3},{3,2},{4,5},{5,4},{6,7},{7,6},{8,9},{9,8},{10,11... | collective-permute-start | bytes 786440 | tf_op jit(solution)/shard_map/cond/branch_0_fun/ppermute | solution.py:542
  122.2 15.3 %collective-permute-start.10 = (bf16[1040,128]{1,0:T(8,128)(2,1)S(1)}, bf16[1040,128]{1,0:T(8,128)(2,1)S(1)}, u32[]{:S(2)}, u32[]{:S(2)}) collective-permute-start(bf16[1040,128]{1,0:T(8,128)(2,1)S(1)} %prepare.4.refs_0_), channel_id=1, source_target_pairs={{0,8},{4,12},{8,0},{12,4},{16,24},{20,28},{24,16},{28,20},{1,9},{5... | collective-permute-start | bytes 798728 | tf_op jit(solution)/shard_map/cond/branch_0_fun/ppermute | solution.py:542
  122.6 14.9 %collective-permute-start.11 = (bf16[1040,128]{1,0:T(8,128)(2,1)S(1)}, bf16[1040,128]{1,0:T(8,128)(2,1)S(1)}, u32[]{:S(2)}, u32[]{:S(2)}) collective-permute-start(bf16[1040,128]{1,0:T(8,128)(2,1)S(1)} %prepare.4.refs_0_), channel_id=1, source_target_pairs={{0,16},{4,20},{8,24},{12,28},{16,0},{20,4},{24,8},{28,12},{1,17},{... | collective-permute-start | bytes 798728 | tf_op jit(solution)/shard_map/cond/branch_0_fun/ppermute | solution.py:542
  123.2 14.4 %collective-permute-start.12 = (bf16[1040,128]{1,0:T(8,128)(2,1)S(1)}, bf16[1040,128]{1,0:T(8,128)(2,1)S(1)}, u32[]{:S(2)}, u32[]{:S(2)}) collective-permute-start(bf16[1040,128]{1,0:T(8,128)(2,1)S(1)} %prepare.4.refs_0_), channel_id=1, source_target_pairs={{0,24},{4,28},{8,16},{12,20},{16,8},{20,12},{24,0},{28,4},{1,25},{... | collective-permute-start | bytes 798728 | tf_op jit(solution)/shard_map/cond/branch_0_fun/ppermute | solution.py:542
  133.2 7.9 %collective-permute-start.9 = (bf16[1024,128]{1,0:T(8,128)(2,1)S(1)}, bf16[1024,128]{1,0:T(8,128)(2,1)S(1)}, u32[]{:S(2)}, u32[]{:S(2)}) collective-permute-start(bf16[1024,128]{1,0:T(8,128)(2,1)S(1)} %relay.5), channel_id=1, source_target_pairs={{0,1},{1,0},{2,3},{3,2},{4,5},{5,4},{6,7},{7,6},{8,9},{9,8},{10,11... | collective-permute-start | bytes 786440 | tf_op jit(solution)/shard_map/cond/branch_0_fun/ppermute | solution.py:542
  (27 other events, 132.4 us)

commit v3 on v2

v3 whole, which is shorter than its diff:
```python
import functools

import jax
import jax.numpy as jnp
from jax import lax
from jax.experimental import pallas as pl
from jax.experimental.pallas import tpu as pltpu
from jax.sharding import PartitionSpec as P

AXES = ("grp", "blk")
HIGHEST = lax.Precision.HIGHEST
INFLATION_MAX = 1.15
CORRECTION_MAX = 4e-6
VMEM = pl.BlockSpec(memory_space=pltpu.VMEM)
SMEM = pl.BlockSpec(memory_space=pltpu.SMEM)
ANY = pl.BlockSpec(memory_space=pl.ANY)
F32 = jnp.float32
NEED_ROWS = 16
DIAGONAL_ROWS = 8
BF16 = jnp.bfloat16
NN = (((1,), (0,)), ((), ()))
NT = (((1,), (1,)), ((), ()))
TN = (((0,), (0,)), ((), ()))


def cost(flops, nbytes):
    return pl.CostEstimate(flops=int(flops), bytes_accessed=int(nbytes), transcendentals=0)


def vmem(nbytes):
    return pltpu.CompilerParams(vmem_limit_bytes=int(nbytes) + (8 << 20))


def parts(x):
    high = x.astype(BF16)
    return high, (x - high.astype(F32)).astype(BF16)


def dot1(a, b, dims=NN):
    return lax.dot_general(a.astype(BF16), b.astype(BF16), dims, preferred_element_type=F32)


def dot3(a, b, dims=NN):
    a_high, a_low = parts(a)
    b_high, b_low = parts(b)
    (across,), (down,) = dims[0]
    return dot1(jnp.concatenate([a_high, a_low, a_high], across), jnp.concatenate([b_high, b_high, b_low], down), dims)


def dot6(a, b, dims=NN):
    return lax.dot_general(a, b, dims, precision=HIGHEST, preferred_element_type=F32)


def normalised(gram):
    _, on_diag = masks(gram.shape[0])
    diag = jnp.where(on_diag, gram, 0.0)
    scale_row = lax.rsqrt(jnp.sum(diag, axis=0, keepdims=True))
    scale_col = lax.rsqrt(jnp.sum(diag, axis=1, keepdims=True))
    return scale_row, gram * scale_col * scale_row - on_diag.astype(F32)


def iterated(base):
    below, on_diag = masks(base.shape[0])
    eye = on_diag.astype(F32)
    weight = below.astype(F32) + 0.5 * eye
    first = weight * base
    moved = dot1(first, base)
    low = first + weight * (dot1(moved, first, NT) - moved) + dot1(weight * moved, first)
    moved = dot3(low, base)
    crossed = dot3(low + moved - base, low, NT)
    step = weight * (base - low - moved + crossed - low * eye)
    return low + step - dot1(step, low), jnp.sum(step * step)


def eliminated(base, work):
    n = base.shape[0]
    rows = lax.broadcasted_iota(jnp.int32, (n, n), 0)
    cols = lax.broadcasted_iota(jnp.int32, (n, n), 1)
    eye = (rows == cols).astype(F32)
    work[0] = eye
    work[1] = base + eye

    def eliminate(j, carry):
        left = work[1]
        pivot_row = work[1, pl.ds(j, 1), :]
        pivot = jnp.sum(jnp.where(cols[:1] == j, pivot_row, 0.0), axis=1, keepdims=True)
        column = jnp.sum(jnp.where(cols == j, left, 0.0), axis=1, keepdims=True)
        factor = jnp.where(rows[:, :1] > j, column / pivot, 0.0)
        right_row = work[0, pl.ds(j, 1), :]
        work[1] = left - factor * pivot_row
        work[0] = work[0] - factor * right_row
        work[0, pl.ds(j, 1), :] = right_row * lax.rsqrt(pivot)
        return carry

    lax.fori_loop(0, n, eliminate, 0)
    return eye - work[0]


def masks(n):
    rows = lax.broadcasted_iota(jnp.int32, (n, n), 0)
    cols = lax.broadcasted_iota(jnp.int32, (n, n), 1)
    return rows > cols, rows == cols


def halved(place, a, b, whole, mine, other):
    n = whole.shape[0]
    half = n // 2
    below, diagonal = masks(n)
    whole[...] = jnp.where(jnp.logical_or(below, diagonal), b, a)
    row = jnp.sum(jnp.where(diagonal, a, 0.0), axis=0, keepdims=True)
    here = pl.multiple_of((place[1] & 1) * half, half)
    for ref, start in ((mine, here), (other, half - here)):
        ref[:half, :] = whole[pl.ds(start, half), :]
        ref[half:, :] = jnp.broadcast_to(row, (DIAGONAL_ROWS, n))


def unhalved(place, mine, other, whole):
    n = whole.shape[0]
    half = n // 2
    here = pl.multiple_of((place[1] & 1) * half, half)
    whole[pl.ds(here, half), :] = mine[:half, :]
    whole[pl.ds(half - here, half), :] = other[:half, :]
    stored = whole[...]
    turned = stored.T
    below, diagonal = masks(n)
    a = jnp.where(diagonal, mine[half : half + 1, :], jnp.where(below, turned, stored))
    return a, jnp.where(jnp.logical_or(below, diagonal), stored, turned)


def scaled(x, scale, low, dot):
    x = x * scale
    return x - dot(x, low, NT)


def inflation_of(low):
    inverse = masks(low.shape[0])[1].astype(F32) - low
    return jnp.sum(inverse * inverse) / low.shape[0]


def both_factors(first, second, low_of, dot):
    _, on_diag = masks(first.shape[0])

    def as_column(row):
        return jnp.sum(jnp.where(on_diag, row, 0.0), axis=1, keepdims=True)

    scale, base = normalised(first)
    low = low_of(base)
    raw = second * scale * as_column(scale)
    raw = raw - dot(low, raw)
    raw = raw - dot(raw, low, NT)
    next_scale, base = normalised(raw)
    next_low = low_of(base)
    moved = as_column(next_scale) * low
    return low, scale, moved + next_low * next_scale - dot(next_low, moved), next_scale, next_low


def finish_kernel(total_rows, place, mine, other, product, out_ref, low_ref, scale_ref, fine_ref, whole, work, done, sems):
    first, second = [x / total_rows for x in unhalved(place, mine, other, whole)]
    step = product.shape[0] // sems.shape[0]
    sizes = []

    def quickly(base):
        low, size = iterated(base)
        sizes.append(size)
        return low

    def write(low, scale, both_low, next_scale, dot):
        low_ref[...] = low
        scale_ref[...] = scale
        copies = []
        for i in range(sems.shape[0]):
            here = pl.ds(i * step, step)
            x = product[here, :] * scale
            done[here, :] = x * next_scale - dot(x, both_low, NT)
            copies.append(pltpu.make_async_copy(done.at[here, :], out_ref.at[here, :], sems.at[i]))
            copies[-1].start()
        for copy in copies:
            copy.wait()

    *found, next_low = both_factors(first, second, quickly, dot3)
    write(*found, dot3)
    close = jnp.maximum(*sizes) <= CORRECTION_MAX
    fine = jnp.maximum(inflation_of(found[0]), inflation_of(next_low)) <= INFLATION_MAX
    fine_ref[0] = jnp.logical_and(close, fine).astype(jnp.int32)

    @pl.when(jnp.logical_not(close))
    def _():
        *found, _ = both_factors(first, second, lambda base: eliminated(base, work), dot6)
        write(*found, dot6)


def finish(place, halves, product, total_rows):
    n = product.shape[1]
    return pl.pallas_call(
        functools.partial(finish_kernel, total_rows),
        out_shape=(
            pltpu.HBM(product.shape, F32),
            jax.ShapeDtypeStruct((n, n), F32),
            jax.ShapeDtypeStruct((1, n), F32),
            jax.ShapeDtypeStruct((1,), jnp.int32),
        ),
        in_specs=[SMEM] + [VMEM] * 3,
        out_specs=(ANY, VMEM, VMEM, SMEM),
        scratch_shapes=[
            pltpu.VMEM((n, n), F32),
            pltpu.VMEM((2, n, n), F32),
            pltpu.VMEM(product.shape, F32),
            pltpu.SemaphoreType.DMA((4,)),
        ],
        cost_estimate=cost(60 * n**3 + 6 * product.size * n, 8 * product.size),
        compiler_params=vmem(8 * product.size),
        name="finish",
    )(place, *held(*halves, product))


def add_near(shape, place, near_cols, tiles, near, r, acc):
    blocks, sources, per_source, tile = shape
    for k, ref in near:
        first = (r * sources + (place[0] ^ k)) * per_source
        for n in range(per_source):
            start = pl.multiple_of(near_cols[first + n] * tile, tile)
            part = jnp.dot(tiles[first + n], ref[pl.ds(start, tile), :], preferred_element_type=F32)
            acc = part if acc is None else acc + part
    return acc


def load_kernel(n, *refs):
    ins, outs, sems = refs[:n], refs[-n - 1 : -1], refs[-1]
    copies = [pltpu.make_async_copy(ins[i], outs[i], sems.at[i]) for i in range(n)]
    for copy in copies:
        copy.start()
    for copy in copies:
        copy.wait()


def load(token, *arrays):
    n = len(arrays)
    return pl.pallas_call(
        functools.partial(load_kernel, n),
        out_shape=tuple(pltpu.VMEM(a.shape, a.dtype) for a in arrays),
        in_specs=[ANY] * (n + 1),
        out_specs=(VMEM,) * n,
        scratch_shapes=[pltpu.SemaphoreType.DMA((n,))],
        cost_estimate=cost(0, sum(a.size * 4 for a in arrays)),
        compiler_params=vmem(0),
        name="load",
    )(*outside(*arrays), token)


def outside(*arrays):
    return [pltpu.with_memory_space_constraint(a, pltpu.HBM) for a in arrays]


def held(*arrays):
    return [pltpu.with_memory_space_constraint(a, pltpu.VMEM) for a in arrays]


def relay_kernel(x_ref, *refs):
    refs[-1][...] = x_ref[...]


def relay(x, *tokens):
    return pl.pallas_call(
        relay_kernel,
        out_shape=pltpu.VMEM(x.shape, x.dtype),
        in_specs=[VMEM] + [ANY] * len(tokens),
        out_specs=VMEM,
        cost_estimate=cost(0, 0),
        compiler_params=vmem(0),
        name="relay",
    )(*held(x), *tokens)


def prepare_kernel(rows, need, out_ref):
    n, width = rows.shape
    out_ref[:n, :] = rows[...]
    lanes = lax.broadcasted_iota(jnp.int32, (NEED_ROWS, width), 1)
    needs = jnp.zeros((NEED_ROWS, width), F32)
    for h in range(need.shape[0]):
        needs = jnp.where(lanes == h, need[h].astype(F32), needs)
    out_ref[n:, :] = needs.astype(BF16)


def prepare(rows, need):
    n, width = rows.shape
    return pl.pallas_call(
        prepare_kernel,
        out_shape=pltpu.VMEM((n + NEED_ROWS, width), BF16),
        in_specs=[VMEM, SMEM],
        out_specs=VMEM,
        cost_estimate=cost(0, 0),
        compiler_params=vmem(4 * rows.size),
        name="prepare",
    )(rows, need)


def pack_kernel(tile, n, place, wanted, *refs):
    out_ref = refs[-1]
    size = tile + NEED_ROWS
    for i, ref in enumerate(refs[:n]):
        start = pl.multiple_of(jnp.maximum(wanted[place[1] ^ (2 * i)], 0) * tile, tile)
        out_ref[i * size : i * size + tile, :] = ref[pl.ds(start, tile), :]
        out_ref[i * size + tile : (i + 1) * size, :] = ref[ref.shape[0] - NEED_ROWS :, :]


def pack(tile, place, wanted, rows, tokens):
    return pl.pallas_call(
        functools.partial(pack_kernel, tile, len(rows)),
        out_shape=pltpu.VMEM((len(rows) * (tile + NEED_ROWS), rows[0].shape[1]), BF16),
        in_specs=[SMEM] * 2 + [VMEM] * len(rows) + [ANY] * len(tokens),
        out_specs=VMEM,
        cost_estimate=cost(0, 0),
        compiler_params=vmem(0),
        name="pack",
    )(place, wanted, *held(*rows), *tokens)


def core_pack_kernel(tile, own, *refs):
    out_ref = refs[-1]
    out_ref[:tile, :] = own[...]
    for i, ref in enumerate(refs[:-1], 1):
        out_ref[i * tile : (i + 1) * tile, :] = ref[tile:, :]


def core_pack(own, received):
    tile, width = own.shape
    n = 1 + len(received)
    return pl.pallas_call(
        functools.partial(core_pack_kernel, tile),
        out_shape=pltpu.VMEM((n * tile, width), BF16),
        in_specs=[VMEM] * n,
        out_specs=VMEM,
        cost_estimate=cost(0, 0),
        compiler_params=vmem(0),
        name="core_pack",
    )(*held(own, *received))


def early_kernel(shape, distances, n_far, place, near_cols, far_groups, *refs):
    blocks, _, _, tile = shape
    n = len(distances)
    near = list(zip(distances, refs[:n]))
    packed, far = refs[n], refs[n + 1 : n + n_far]
    tiles_near, tiles_far, out_ref, table = refs[n + n_far :]
    for i in range(len(far) + 1):
        table[place[1] ^ (2 * i + 1)] = packed[i * tile : (i + 1) * tile, :]
        if i:
            table[place[1] ^ (2 * i)] = far[i - 1][:tile, :]
    for r in range(blocks):
        here = pl.ds(r * tile, tile)
        acc = add_near(shape, place, near_cols, tiles_near, near, r, None)
        out_ref[here, :] = add_far(far_groups, tiles_far, table, r, blocks, acc)


def early(shape, groups, scalars, near, far, tiles_near, tiles_far):
    blocks, _, _, tile = shape
    distances, rows = zip(*near)
    width = rows[0].shape[1]
    return pl.pallas_call(
        functools.partial(early_kernel, shape, distances, len(far)),
        out_shape=pltpu.VMEM((blocks * tile, width), F32),
        in_specs=[SMEM] * 3 + [VMEM] * (len(rows) + len(far) + 2),
        out_specs=VMEM,
        scratch_shapes=[pltpu.VMEM((groups, tile, width), BF16)],
        cost_estimate=cost(0, 0),
        compiler_params=vmem(0),
        name="early",
    )(*scalars, *held(*rows, *far, tiles_near, tiles_far))


def near_kernel(shape, distances, place, near_cols, *refs):
    blocks, _, _, tile = shape
    n = len(distances)
    *before, tiles, out_ref = refs[n:]
    near = list(zip(distances, refs[:n]))
    for r in range(blocks):
        here = pl.ds(r * tile, tile)
        acc = before[0][here, :] if before else None
        out_ref[here, :] = add_near(shape, place, near_cols, tiles, near, r, acc)


def near_product(shape, scalars, near, tiles, *before):
    blocks, _, _, tile = shape
    distances, rows = zip(*near)
    return pl.pallas_call(
        functools.partial(near_kernel, shape, distances),
        out_shape=pltpu.VMEM((blocks * tile, rows[0].shape[1]), F32),
        in_specs=[SMEM] * 2 + [VMEM] * (len(rows) + len(before) + 1),
        out_specs=VMEM,
        cost_estimate=cost(0, 0),
        compiler_params=vmem(0),
        name="near",
    )(*scalars[:2], *held(*rows, *before, tiles))


def far_table(place, need, far, packed, table):
    tile = table.shape[1]
    size = tile + NEED_ROWS
    for i in range(len(far) + 1):
        h = place[1] ^ (2 * i)
        table[h ^ 1] = packed[i * size : i * size + tile, :]
        if i:
            start = pl.multiple_of(jnp.maximum(need[h], 0) * tile, tile)
            table[h] = far[i - 1][pl.ds(start, tile), :]


def add_far(far_groups, tiles, table, r, blocks, acc):
    each = tiles.shape[0] // blocks
    for t in range(r * each, (r + 1) * each):
        acc = acc + jnp.dot(tiles[t], table[far_groups[t]], preferred_element_type=F32)
    return acc


def gram_of(rows, tile):
    gram = None
    for start in range(0, rows.shape[0], tile):
        both = jnp.concatenate(parts(rows[pl.ds(start, tile), :]), axis=1)
        part = lax.dot_general(both, both, TN, preferred_element_type=F32)
        gram = part if gram is None else gram + part
    n = rows.shape[1]
    crossed = gram[:n, n:]
    return gram[:n, :n] + (crossed + crossed.T) + gram[n:, n:]


def late_kernel(shape, place, far_groups, need, partial, *refs):
    blocks, _, _, tile = shape
    *far, packed, tiles = refs[: need.shape[0] // 2 + 1]
    product_ref, rounded_ref, table = refs[need.shape[0] // 2 + 1 :]
    far_table(place, need, far, packed, table)
    for r in range(blocks):
        here = pl.ds(r * tile, tile)
        acc = add_far(far_groups, tiles, table, r, blocks, partial[here, :])
        product_ref[here, :] = acc
        rounded_ref[here, :] = acc.astype(BF16)


def late(shape, scalars, need, partial, far, tiles):
    n, width = partial.shape
    groups, tile = need.shape[0], shape[3]
    return pl.pallas_call(
        functools.partial(late_kernel, shape),
        out_shape=(pltpu.VMEM((n, width), F32), pltpu.VMEM((n, width), BF16)),
        in_specs=[SMEM] * 3 + [VMEM] * (len(far) + 2),
        out_specs=(VMEM,) * 2,
        scratch_shapes=[pltpu.VMEM((groups, tile, width), BF16)],
        cost_estimate=cost(0, 0),
        compiler_params=vmem(0),
        name="late",
    )(scalars[0], scalars[2], need, *held(partial, *far, tiles))


def gram_kernel(tile, product, rounded, out_ref, copy_ref):
    out_ref[...] = gram_of(product, tile)
    copy_ref[...] = rounded[...]


def gram(tile, product, rounded):
    width = product.shape[1]
    return pl.pallas_call(
        functools.partial(gram_kernel, tile),
        out_shape=(pltpu.VMEM((width, width), F32), pltpu.VMEM(rounded.shape, BF16)),
        in_specs=[VMEM] * 2,
        out_specs=(VMEM,) * 2,
        cost_estimate=cost(0, 0),
        compiler_params=vmem(0),
        name="gram",
    )(*held(product, rounded))


def halves_kernel(place, a, b, mine, other, whole):
    halved(place, a[...], b[...], whole, mine, other)


def halves_of(place, a, b):
    n = a.shape[0]
    half = pltpu.VMEM((n // 2 + DIAGONAL_ROWS, n), F32)
    return pl.pallas_call(
        halves_kernel,
        out_shape=(half, half),
        in_specs=[SMEM] + [VMEM] * 2,
        out_specs=(VMEM,) * 2,
        scratch_shapes=[pltpu.VMEM((n, n), F32)],
        compiler_params=vmem(0),
        name="halves",
    )(place, a, b)


def blocks_kernel(tile, n_far, place, rounded, *refs):
    *far, packed = refs[:n_far]
    own_ref, *outs = refs[n_far + 1 :]
    lane = lax.broadcasted_iota(jnp.int32, (1, rounded.shape[1]), 1) == place[1]
    size = tile + NEED_ROWS

    def wanted_block(k):
        ref, first = (packed, k // 2 * size + tile) if k % 2 else (far[k // 2 - 1], far[0].shape[0] - NEED_ROWS)
        needs = ref[first : first + NEED_ROWS, :].astype(F32)[:1]
        block = jnp.maximum(jnp.sum(jnp.where(lane, needs, 0.0)).astype(jnp.int32), 0)
        return rounded[pl.ds(pl.multiple_of(block * tile, tile), tile), :]

    own_ref[...] = wanted_block(1)
    for i, out_ref in enumerate(outs, 1):
        out_ref[:tile, :] = wanted_block(2 * i)
        out_ref[tile:, :] = wanted_block(2 * i + 1)


def blocks_for_others(tile, place, rounded, far, token):
    width = rounded.shape[1]
    pair = pltpu.VMEM((2 * tile, width), BF16)
    return pl.pallas_call(
        functools.partial(blocks_kernel, tile, len(far)),
        out_shape=(pltpu.VMEM((tile, width), BF16), *(pair,) * (len(far) - 1)),
        in_specs=[SMEM] + [VMEM] * (1 + len(far)) + [ANY],
        out_specs=(VMEM,) * len(far),
        cost_estimate=cost(0, 0),
        compiler_params=vmem(0),
        name="blocks",
    )(place, *held(rounded, *far), token)


def last_kernel(shape, distances, place, near_cols, partial, *refs):
    blocks, _, _, tile = shape
    n = len(distances)
    near = list(zip(distances, refs[:n]))
    past, tiles, product_ref, mine, other, whole = refs[n:]
    for r in range(blocks):
        here = pl.ds(r * tile, tile)
        product_ref[here, :] = add_near(shape, place, near_cols, tiles, near, r, partial[here, :])
    halved(place, past[...], gram_of(product_ref, tile), whole, mine, other)


def last(shape, scalars, partial, near, tiles, past):
    distances, rows = zip(*near)
    width = partial.shape[1]
    half = pltpu.VMEM((width // 2 + DIAGONAL_ROWS, width), F32)
    return pl.pallas_call(
        functools.partial(last_kernel, shape, distances),
        out_shape=(pltpu.VMEM(partial.shape, F32), half, half),
        in_specs=[SMEM] * 2 + [VMEM] * (len(rows) + 3),
        out_specs=(VMEM,) * 3,
        scratch_shapes=[pltpu.VMEM((width, width), F32)],
        cost_estimate=cost(0, 0),
        compiler_params=vmem(0),
        name="last",
    )(*scalars[:2], *held(partial, *rows, past, tiles))


def swap(x, axis, mask):
    size = lax.axis_size(axis)
    return lax.ppermute(x, axis, [(i, i ^ mask) for i in range(size)])


def near_rows(rows, again):
    step = lax.axis_size("blk") // 2
    here = [(0, rows), (step, swap(rows, "blk", step))]
    while step > 1:
        step //= 2
        direct = swap(again, "blk", step)
        here += [(step, direct)] + [(k | step, swap(relay(x, direct), "blk", step)) for k, x in here[1:]]
    return here


def bits(size, scale):
    return [scale << i for i in range(size.bit_length() - 1)]


def everywhere(mine, other):
    positions = lax.axis_size("blk")
    chips, places = bits(lax.axis_size("grp"), positions)[1:], bits(positions, 1)
    x = mine + swap(other, "grp", 1)
    while chips or places:
        a, b = chips[:1], places[:1]
        chips, places = chips[1:], places[1:]
        if a and b:
            x = (x + swap(x, AXES, a[0])) + (swap(x, AXES, b[0]) + swap(x, AXES, a[0] | b[0]))
        else:
            x = x + swap(x, AXES, (a + b)[0])
    return x, swap(x, "grp", 1)


def per_device(tiles_near, near_cols, tiles_far, far_groups, need_blocks, start_vectors):
    tile = tiles_near.shape[1]
    blocks = start_vectors.shape[0] // tile
    sources = lax.axis_size("blk")
    groups = lax.axis_size("grp")
    shape = (blocks, sources, tiles_near.shape[0] // (blocks * sources), tile)
    total_rows = start_vectors.shape[0] * sources * groups
    place = jnp.stack([lax.axis_index("blk"), lax.axis_index("grp")]).astype(jnp.int32)
    scalars = (place, near_cols.reshape(-1), far_groups.reshape(-1))
    need = need_blocks.reshape(-1)
    wanted = swap(need_blocks, "grp", 1).reshape(-1)
    split = 3 * sources // 4

    def begin(rows):
        below = prepare(rows, need)
        far = [swap(below, "grp", k) for k in range(2, groups, 2)]
        near = near_rows(rows, rows)
        near[0] = (0, below)
        tiles = load(near[1][1], tiles_near, tiles_far)
        partial = near_product(shape, scalars, near[:split], tiles[0])
        tokens = [partial, *(x for _, x in near[split:])]
        far.append(swap(pack(tile, place, wanted, [below, *far], tokens), "grp", 1))
        partial = near_product(shape, scalars, near[split:], tiles[0], partial)
        return tiles, far, late(shape, scalars, need, partial, far, tiles[1])

    tiles, far, (product, rounded) = begin(start_vectors)
    past, copied = gram(tile, product, rounded)
    own, *outs = blocks_for_others(tile, place, rounded, far, past)
    near = near_rows(rounded, copied)
    far = [swap(x, "grp", 2 * i) for i, x in enumerate(outs, 1)]
    far.insert(0, swap(core_pack(own, far), "grp", 1))
    partial = early(shape, groups, scalars, near[:split], far, *tiles)
    moved, *halves = last(shape, scalars, partial, near[split:], tiles[0], past)
    vectors, low, scale, fine = finish(place, everywhere(*halves), moved, total_rows)

    def plain(start, vectors, low, scale):
        _, _, (product, _) = begin(start)
        current = scaled(product, scale, low, dot6).astype(BF16)
        _, _, (product, rounded) = begin(current)
        unit = jnp.eye(product.shape[1], dtype=F32) * start.shape[0]
        halves = everywhere(*halves_of(place, unit, gram(tile, product, rounded)[0]))
        return finish(place, halves, product, total_rows)[0]

    return lax.cond(fine[0] > 0, lambda start, vectors, low, scale: vectors, plain, start_vectors, vectors, low, scale)


def solution(mesh):
    in_specs = (
        P(AXES, None, None),
        P(AXES, None),
        P(AXES, None, None),
        P(AXES, None),
        P(AXES, None),
        P(AXES, None),
    )
    return jax.shard_map(
        per_device, mesh=mesh, in_specs=in_specs, out_specs=P(AXES, None), check_vma=False
    )
```

time: 171 us -> 183 us (1.070)
  Pallas kernels: 53.8 us -> 70.3 us
  waiting for transfers between devices: 58.4 us -> 55.1 us
    pallas_call x10 -> x12, Pallas kernels: 32.8 us -> 50.2 us  [the longest x2 37.4 us: finish(): pl.pallas_call(functools.partial(finish_kernel, total_rows), out_shape=(p...]
    ppermute x47 -> x45, waiting for transfers between devices: 58.4 us -> 55.1 us  [swap(): return lax.ppermute(x, axis, [(i, i ^ mask) for i in range(size)])]
    ppermute x47 -> x45, starting transfers between devices: 56.4 us -> 55 us  [swap(): return lax.ppermute(x, axis, [(i, i ^ mask) for i in range(size)])]
  transfers between devices with their start and end apart: 47 -> 45, of which waited for: 29 -> 29; matrix products, arithmetic and copies ran while one was open for 0% -> 0% of each run, Pallas kernels for 12% -> 12%
where the time goes in v3:
time: 183 us
  Pallas kernels  70.3 us (38%)
  waiting for transfers between devices  55.1 us (30%)
  starting transfers between devices  55 us (30%)
    ppermute x45, waiting for transfers between devices, swap(): return lax.ppermute(x, axis, [(i, i ^ mask) for i in range(size)])  55.1 us
    ppermute x45, starting transfers between devices, swap(): return lax.ppermute(x, axis, [(i, i ^ mask) for i in range(size)])  55 us
    pallas_call x2, Pallas kernels, finish(): pl.pallas_call(functools.partial(finish_kernel, total_rows), out_shape=(p...  37.4 us
    pallas_call x3, Pallas kernels, load(): pl.pallas_call(functools.partial(load_kernel, n), out_shape=tuple((pltpu....  9.55 us
    pallas_call x6, Pallas kernels, near_product(): pl.pallas_call(functools.partial(near_kernel, shape, distances), out_shap...  7.51 us
    pallas_call x3, Pallas kernels, late(): pl.pallas_call(functools.partial(late_kernel, shape), out_shape=(pltpu.VM...  5.39 us
  transfers between devices with their start and end apart: 45, of which 29 were waited for; matrix products, arithmetic and copies ran while one was open for 0% of the time, Pallas kernels for 12%

profile of v3, /device:TPU:0, one launch (start us, length us, event | category | flops | bytes accessed | tf_op | source)
XLA Modules:
  0.0 182.9 jit_solution(7901197074508982229)
XLA Ops:
  0.0 4.0 %collective-permute-start.22 = (bf16[1024,128]{1,0:T(8,128)(2,1)}, bf16[1024,128]{1,0:T(8,128)(2,1)S(1)}, u32[]{:S(2)}, u32[]{:S(2)}) collective-permute-start(bf16[1024,128]{1,0:T(8,128)(2,1)} %rows.1), channel_id=1, source_target_pairs={{0,2},{1,3},{2,0},{3,1},{4,6},{5,7},{6,4},{7,5},{8,10},{9,11},{10,... | collective-permute-start | bytes 786440 | tf_op jit(solution)/shard_map/ppermute | solution.py:549
  10.2 6.1 %collective-permute-done.22.x_ref.refs_2_.refs_1_ = bf16[1024,128]{1,0:T(8,128)(2,1)S(1)} collective-permute-done((bf16[1024,128]{1,0:T(8,128)(2,1)}, bf16[1024,128]{1,0:T(8,128)(2,1)S(1)}, u32[]{:S(2)}, u32[]{:S(2)}) %collective-permute-start.22) | collective-permute-done | bytes 262176 | tf_op jit(solution)/shard_map/ppermute | solution.py:549
  18.1 3.2 %load.5 = (bf16[32,256,256]{2,1,0:T(8,128)(2,1)S(1)}, bf16[24,256,256]{2,1,0:T(8,128)(2,1)S(1)}) custom-call(bf16[32,256,256]{2,1,0:T(8,128)(2,1)} %refs_0_.1, bf16[24,256,256]{2,1,0:T(8,128)(2,1)} %refs_1_.1, bf16[1024,128]{1,0:T(8,128)(2,1)S(1)} %collective-permute-done.22.x_ref.refs_2_.refs_1_), custom_call_target="tpu_custom_call" | custom-call | bytes 14680064 | tf_op jit(solution)/shard_map/load/pallas_call | solution.py:238
  27.6 3.1 %collective-permute-start.30 = (bf16[1024,128]{1,0:T(8,128)(2,1)S(1)}, bf16[1024,128]{1,0:T(8,128)(2,1)S(1)}, u32[]{:S(2)}, u32[]{:S(2)}) collective-permute-start(bf16[1024,128]{1,0:T(8,128)(2,1)S(1)} %get-tuple-element.69.rounded.refs_0_), channel_id=1, source_target_pairs={{0,2},{1,3},{2,0},{3,1},{4,6},{5,7},{6,4},{7,5},{8,10},{9,11},{10,... | collective-permute-start | bytes 786440 | tf_op jit(solution)/shard_map/ppermute | solution.py:549
  39.0 3.9 %collective-permute-done.33.refs_1_.refs_5_ = bf16[512,128]{1,0:T(8,128)(2,1)S(1)} collective-permute-done((bf16[512,128]{1,0:T(8,128)(2,1)S(1)}, bf16[512,128]{1,0:T(8,128)(2,1)S(1)}, u32[]{:S(2)}, u32[]{:S(2)}) %collective-permute-start.33) | collective-permute-done | bytes 131104 | tf_op jit(solution)/shard_map/ppermute | solution.py:549
  44.8 2.3 %early.1.partial = f32[1024,128]{1,0:T(8,128)S(1)} custom-call(s32[2]{0:T(128)S(1)} %pad_add_fusion.place, s32[32]{0:T(128)S(1)} %bitcast.11, s32[24]{0:T(128)S(1)} %bitcast.18, bf16[1024,128]{1,0:T(8,128)(2,1)S(1)} %get-tuple-element.69.rounded.refs_0_, bf16[1024,128]{1,0:T(8,128)(2,1)S(1)} %collective-permute-done.30.refs_1_.x_ref, ...), custom_call_target="tpu_custom_call" | custom-call | tf_op jit(solution)/shard_map/early/pallas_call | solution.py:359
  47.1 4.7 %collective-permute-done.36.refs_0_ = bf16[1024,128]{1,0:T(8,128)(2,1)S(1)} collective-permute-done((bf16[1024,128]{1,0:T(8,128)(2,1)S(1)}, bf16[1024,128]{1,0:T(8,128)(2,1)S(1)}, u32[]{:S(2)}, u32[]{:S(2)}) %collective-permute-start.36) | collective-permute-done | bytes 262176 | tf_op jit(solution)/shard_map/ppermute | solution.py:549
  60.9 2.5 %collective-permute-start.42 = (f32[72,128]{1,0:T(8,128)S(1)}, f32[72,128]{1,0:T(8,128)S(1)}, u32[]{:S(2)}, u32[]{:S(2)}) collective-permute-start(f32[72,128]{1,0:T(8,128)S(1)} %add_add_fusion.3), channel_id=1, source_target_pairs={{0,2},{1,3},{2,0},{3,1},{4,6},{5,7},{6,4},{7,5},{8,10},{9,11},{10,... | collective-permute-start | bytes 110600 | tf_op jit(solution)/shard_map/ppermute | solution.py:549
  65.9 3.3 %collective-permute-done.43 = f32[72,128]{1,0:T(8,128)S(1)} collective-permute-done((f32[72,128]{1,0:T(8,128)S(1)}, f32[72,128]{1,0:T(8,128)S(1)}, u32[]{:S(2)}, u32[]{:S(2)}) %collective-permute-start.43) | collective-permute-done | bytes 36896 | tf_op jit(solution)/shard_map/ppermute | solution.py:549
  70.5 33.1 %finish.3 = (f32[1024,128]{1,0:T(8,128)}, f32[128,128]{1,0:T(8,128)S(1)}, f32[1,128]{1,0:T(1,128)S(1)}, s32[1]{0:T(128)}) custom-call(s32[2]{0:T(128)S(1)} %pad_add_fusion.place, f32[72,128]{1,0:T(8,128)S(1)} %add_add_fusion.2.mine, f32[72,128]{1,0:T(8,128)S(1)} %collective-permute-done.44.other, f32[1024,128]{1,0:T(8,128)S(1)} %get-tuple-element.79.product), custom_call_target="tpu_custom_call" | custom-call | flops 226492416 | bytes 1048576 | tf_op jit(solution)/shard_map/finish/pallas_call | solution.py:194
  104.3 78.4 %conditional.1 = (f32[1024,128]{1,0:T(8,128)}) conditional(s32[]{:T(128)} %bitcast.7, (bf16[1024,128]{1,0:T(8,128)(2,1)S(1)}, s32[8]{0:T(128)S(1)}, bf16[32,256,256]{2,1,0:T(8,128)(2,1)}, bf16[24,256,256]{2,1,0:T(8,128)(2,1)}, s32[2]{0:T(128)S(1)}, /*index=5*/s32[32]{0:T(128)S(1)}, s32[8]{0:T(128)S(1)}, s32[24]{0:T(128)S(1)}, f32[1,128]{1,0:T(1,128)S(1)}, ...), branch_computations={%region_0.0_spmd, %region_1.0_spmd} | conditional | flops 428309504 | bytes 47895928 | solution.py:623
  104.5 2.1 %collective-permute-start = (bf16[1024,128]{1,0:T(8,128)(2,1)S(1)}, bf16[1024,128]{1,0:T(8,128)(2,1)S(1)}, u32[]{:S(2)}, u32[]{:S(2)}) collective-permute-start(bf16[1024,128]{1,0:T(8,128)(2,1)S(1)} %get-tuple-element.33.rows), channel_id=1, source_target_pairs={{0,2},{1,3},{2,0},{3,1},{4,6},{5,7},{6,4},{7,5},{8,10},{9,11},{10,... | collective-permute-start | bytes 786440 | tf_op jit(solution)/shard_map/cond/branch_0_fun/ppermute | solution.py:549
  109.9 2.4 %collective-permute-start.5 = (bf16[1040,128]{1,0:T(8,128)(2,1)S(1)}, bf16[1040,128]{1,0:T(8,128)(2,1)S(1)}, u32[]{:S(2)}, u32[]{:S(2)}) collective-permute-start(bf16[1040,128]{1,0:T(8,128)(2,1)S(1)} %prepare.3.refs_0_), channel_id=1, source_target_pairs={{0,24},{4,28},{8,16},{12,20},{16,8},{20,12},{24,0},{28,4},{1,25},{... | collective-permute-start | bytes 798728 | tf_op jit(solution)/shard_map/cond/branch_0_fun/ppermute | solution.py:549
  112.4 7.0 %collective-permute-done.x_ref.refs_2_.refs_1_ = bf16[1024,128]{1,0:T(8,128)(2,1)S(1)} collective-permute-done((bf16[1024,128]{1,0:T(8,128)(2,1)S(1)}, bf16[1024,128]{1,0:T(8,128)(2,1)S(1)}, u32[]{:S(2)}, u32[]{:S(2)}) %collective-permute-start) | collective-permute-done | bytes 262176 | tf_op jit(solution)/shard_map/cond/branch_0_fun/ppermute | solution.py:549
  120.7 3.2 %load.3 = (bf16[32,256,256]{2,1,0:T(8,128)(2,1)S(1)}, bf16[24,256,256]{2,1,0:T(8,128)(2,1)S(1)}) custom-call(bf16[32,256,256]{2,1,0:T(8,128)(2,1)} %get-tuple-element.34.refs_0_, bf16[24,256,256]{2,1,0:T(8,128)(2,1)} %get-tuple-element.35.refs_1_, bf16[1024,128]{1,0:T(8,128)(2,1)S(1)} %collective-permute-done.x_ref.refs_2_.refs_1_), custom_call_target="tpu_custom_call" | custom-call | bytes 14680064 | tf_op jit(solution)/shard_map/cond/branch_0_fun/load/pallas_call | solution.py:238
  129.3 2.3 %late.3 = (f32[1024,128]{1,0:T(8,128)S(1)}, bf16[1024,128]{1,0:T(8,128)(2,1)}) custom-call(s32[2]{0:T(128)S(1)} %get-tuple-element.29.place, s32[24]{0:T(128)S(1)} %get-tuple-element.30.far_groups, s32[8]{0:T(128)S(1)} %get-tuple-element.31.need, f32[1024,128]{1,0:T(8,128)S(1)} %near.7.partial, bf16[1040,128]{1,0:T(8,128)(2,1)S(1)} %collective-permute-done.3.refs_1_.refs_0_, ...), custom_call_target="tpu_custom_call" | custom-call | tf_op jit(solution)/shard_map/cond/branch_0_fun/late/pallas_call | solution.py:440
  132.1 2.6 %collective-permute-start.7 = (bf16[1024,128]{1,0:T(8,128)(2,1)S(1)}, bf16[1024,128]{1,0:T(8,128)(2,1)S(1)}, u32[]{:S(2)}, u32[]{:S(2)}) collective-permute-start(bf16[1024,128]{1,0:T(8,128)(2,1)S(1)} %fusion.rows), channel_id=1, source_target_pairs={{0,2},{1,3},{2,0},{3,1},{4,6},{5,7},{6,4},{7,5},{8,10},{9,11},{10,... | collective-permute-start | bytes 786440 | tf_op jit(solution)/shard_map/cond/branch_0_fun/ppermute | solution.py:549
  138.0 2.6 %collective-permute-start.12 = (bf16[1040,128]{1,0:T(8,128)(2,1)S(1)}, bf16[1040,128]{1,0:T(8,128)(2,1)S(1)}, u32[]{:S(2)}, u32[]{:S(2)}) collective-permute-start(bf16[1040,128]{1,0:T(8,128)(2,1)S(1)} %prepare.4.refs_0_), channel_id=1, source_target_pairs={{0,24},{4,28},{8,16},{12,20},{16,8},{20,12},{24,0},{28,4},{1,25},{... | collective-permute-start | bytes 798728 | tf_op jit(solution)/shard_map/cond/branch_0_fun/ppermute | solution.py:549
  140.6 6.6 %collective-permute-done.7.x_ref.refs_2_.refs_1_ = bf16[1024,128]{1,0:T(8,128)(2,1)S(1)} collective-permute-done((bf16[1024,128]{1,0:T(8,128)(2,1)S(1)}, bf16[1024,128]{1,0:T(8,128)(2,1)S(1)}, u32[]{:S(2)}, u32[]{:S(2)}) %collective-permute-start.7) | collective-permute-done | bytes 262176 | tf_op jit(solution)/shard_map/cond/branch_0_fun/ppermute | solution.py:549
  148.8 3.2 %load.4 = (bf16[32,256,256]{2,1,0:T(8,128)(2,1)S(1)}, bf16[24,256,256]{2,1,0:T(8,128)(2,1)S(1)}) custom-call(bf16[32,256,256]{2,1,0:T(8,128)(2,1)} %get-tuple-element.34.refs_0_, bf16[24,256,256]{2,1,0:T(8,128)(2,1)} %get-tuple-element.35.refs_1_, bf16[1024,128]{1,0:T(8,128)(2,1)S(1)} %collective-permute-done.7.x_ref.refs_2_.refs_1_), custom_call_target="tpu_custom_call" | custom-call | bytes 14680064 | tf_op jit(solution)/shard_map/cond/branch_0_fun/load/pallas_call | solution.py:238
  165.4 2.4 %collective-permute-done.17 = f32[72,128]{1,0:T(8,128)S(1)} collective-permute-done((f32[72,128]{1,0:T(8,128)S(1)}, f32[72,128]{1,0:T(8,128)S(1)}, u32[]{:S(2)}, u32[]{:S(2)}) %collective-permute-start.17) | collective-permute-done | bytes 36896 | tf_op jit(solution)/shard_map/cond/branch_0_fun/ppermute | solution.py:549
  168.4 2.6 %collective-permute-start.19 = (f32[72,128]{1,0:T(8,128)S(1)}, f32[72,128]{1,0:T(8,128)S(1)}, u32[]{:S(2)}, u32[]{:S(2)}) collective-permute-start(f32[72,128]{1,0:T(8,128)S(1)} %add_add_fusion.1), channel_id=1, source_target_pairs={{0,2},{1,3},{2,0},{3,1},{4,6},{5,7},{6,4},{7,5},{8,10},{9,11},{10,... | collective-permute-start | bytes 110600 | tf_op jit(solution)/shard_map/cond/branch_0_fun/ppermute | solution.py:549
  174.5 2.4 %collective-permute-done.20 = f32[72,128]{1,0:T(8,128)S(1)} collective-permute-done((f32[72,128]{1,0:T(8,128)S(1)}, f32[72,128]{1,0:T(8,128)S(1)}, u32[]{:S(2)}, u32[]{:S(2)}) %collective-permute-start.20) | collective-permute-done | bytes 36896 | tf_op jit(solution)/shard_map/cond/branch_0_fun/ppermute | solution.py:549
  178.1 4.3 %finish.2 = (f32[1024,128]{1,0:T(8,128)}, f32[128,128]{1,0:T(8,128)}, f32[1,128]{1,0:T(1,128)}, s32[1]{0:T(128)}) custom-call(s32[2]{0:T(128)S(1)} %get-tuple-element.29.place, f32[72,128]{1,0:T(8,128)S(1)} %add_add_fusion.mine, f32[72,128]{1,0:T(8,128)S(1)} %collective-permute-done.21.other, f32[1024,128]{1,0:T(8,128)S(1)} %get-tuple-element.44.product), custom_call_target="tpu_custom_call" | custom-call | flops 226492416 | bytes 1048576 | tf_op jit(solution)/shard_map/cond/branch_0_fun/finish/pallas_call | solution.py:194
  (115 shorter events, 71.3 us)
Async XLA Ops:
  0.0 16.3 %collective-permute-start.22 = (bf16[1024,128]{1,0:T(8,128)(2,1)}, bf16[1024,128]{1,0:T(8,128)(2,1)S(1)}, u32[]{:S(2)}, u32[]{:S(2)}) collective-permute-start(bf16[1024,128]{1,0:T(8,128)(2,1)} %rows.1), channel_id=1, source_target_pairs={{0,2},{1,3},{2,0},{3,1},{4,6},{5,7},{6,4},{7,5},{8,10},{9,11},{10,... | collective-permute-start | bytes 786440 | tf_op jit(solution)/shard_map/ppermute | solution.py:549
  4.0 12.4 %collective-permute-start.23 = (bf16[1024,128]{1,0:T(8,128)(2,1)}, bf16[1024,128]{1,0:T(8,128)(2,1)S(1)}, u32[]{:S(2)}, u32[]{:S(2)}) collective-permute-start(bf16[1024,128]{1,0:T(8,128)(2,1)} %rows.1), channel_id=1, source_target_pairs={{0,1},{1,0},{2,3},{3,2},{4,5},{5,4},{6,7},{7,6},{8,9},{9,8},{10,11... | collective-permute-start | bytes 786440 | tf_op jit(solution)/shard_map/ppermute | solution.py:549
  6.6 16.2 %collective-permute-start.25 = (bf16[1040,128]{1,0:T(8,128)(2,1)S(1)}, bf16[1040,128]{1,0:T(8,128)(2,1)S(1)}, u32[]{:S(2)}, u32[]{:S(2)}) collective-permute-start(bf16[1040,128]{1,0:T(8,128)(2,1)S(1)} %prepare.5.refs_0_), channel_id=1, source_target_pairs={{0,8},{4,12},{8,0},{12,4},{16,24},{20,28},{24,16},{28,20},{1,9},{5... | collective-permute-start | bytes 798728 | tf_op jit(solution)/shard_map/ppermute | solution.py:549
  8.2 14.7 %collective-permute-start.26 = (bf16[1040,128]{1,0:T(8,128)(2,1)S(1)}, bf16[1040,128]{1,0:T(8,128)(2,1)S(1)}, u32[]{:S(2)}, u32[]{:S(2)}) collective-permute-start(bf16[1040,128]{1,0:T(8,128)(2,1)S(1)} %prepare.5.refs_0_), channel_id=1, source_target_pairs={{0,16},{4,20},{8,24},{12,28},{16,0},{20,4},{24,8},{28,12},{1,17},{... | collective-permute-start | bytes 798728 | tf_op jit(solution)/shard_map/ppermute | solution.py:549
  9.7 13.2 %collective-permute-start.27 = (bf16[1040,128]{1,0:T(8,128)(2,1)S(1)}, bf16[1040,128]{1,0:T(8,128)(2,1)S(1)}, u32[]{:S(2)}, u32[]{:S(2)}) collective-permute-start(bf16[1040,128]{1,0:T(8,128)(2,1)S(1)} %prepare.5.refs_0_), channel_id=1, source_target_pairs={{0,24},{4,28},{8,16},{12,20},{16,8},{20,12},{24,0},{28,4},{1,25},{... | collective-permute-start | bytes 798728 | tf_op jit(solution)/shard_map/ppermute | solution.py:549
  16.5 7.3 %collective-permute-start.24 = (bf16[1024,128]{1,0:T(8,128)(2,1)S(1)}, bf16[1024,128]{1,0:T(8,128)(2,1)S(1)}, u32[]{:S(2)}, u32[]{:S(2)}) collective-permute-start(bf16[1024,128]{1,0:T(8,128)(2,1)S(1)} %relay.6), channel_id=1, source_target_pairs={{0,1},{1,0},{2,3},{3,2},{4,5},{5,4},{6,7},{7,6},{8,9},{9,8},{10,11... | collective-permute-start | bytes 786440 | tf_op jit(solution)/shard_map/ppermute | solution.py:549
  27.6 15.5 %collective-permute-start.30 = (bf16[1024,128]{1,0:T(8,128)(2,1)S(1)}, bf16[1024,128]{1,0:T(8,128)(2,1)S(1)}, u32[]{:S(2)}, u32[]{:S(2)}) collective-permute-start(bf16[1024,128]{1,0:T(8,128)(2,1)S(1)} %get-tuple-element.69.rounded.refs_0_), channel_id=1, source_target_pairs={{0,2},{1,3},{2,0},{3,1},{4,6},{5,7},{6,4},{7,5},{8,10},{9,11},{10,... | collective-permute-start | bytes 786440 | tf_op jit(solution)/shard_map/ppermute | solution.py:549
  31.1 12.5 %collective-permute-start.31 = (bf16[1024,128]{1,0:T(8,128)(2,1)S(1)}, bf16[1024,128]{1,0:T(8,128)(2,1)S(1)}, u32[]{:S(2)}, u32[]{:S(2)}) collective-permute-start(bf16[1024,128]{1,0:T(8,128)(2,1)S(1)} %get-tuple-element.71), channel_id=1, source_target_pairs={{0,1},{1,0},{2,3},{3,2},{4,5},{5,4},{6,7},{7,6},{8,9},{9,8},{10,11... | collective-permute-start | bytes 786440 | tf_op jit(solution)/shard_map/ppermute | solution.py:549
  35.1 7.8 %collective-permute-start.33 = (bf16[512,128]{1,0:T(8,128)(2,1)S(1)}, bf16[512,128]{1,0:T(8,128)(2,1)S(1)}, u32[]{:S(2)}, u32[]{:S(2)}) collective-permute-start(bf16[512,128]{1,0:T(8,128)(2,1)S(1)} %get-tuple-element.75), channel_id=1, source_target_pairs={{0,16},{4,20},{8,24},{12,28},{16,0},{20,4},{24,8},{28,12},{1,17},{... | collective-permute-start | bytes 393224 | tf_op jit(solution)/shard_map/ppermute | solution.py:549
  36.7 6.3 %collective-permute-start.34 = (bf16[512,128]{1,0:T(8,128)(2,1)S(1)}, bf16[512,128]{1,0:T(8,128)(2,1)S(1)}, u32[]{:S(2)}, u32[]{:S(2)}) collective-permute-start(bf16[512,128]{1,0:T(8,128)(2,1)S(1)} %get-tuple-element.76), channel_id=1, source_target_pairs={{0,24},{4,28},{8,16},{12,20},{16,8},{20,12},{24,0},{28,4},{1,25},{... | collective-permute-start | bytes 393224 | tf_op jit(solution)/shard_map/ppermute | solution.py:549
  43.6 8.3 %collective-permute-start.36 = (bf16[1024,128]{1,0:T(8,128)(2,1)S(1)}, bf16[1024,128]{1,0:T(8,128)(2,1)S(1)}, u32[]{:S(2)}, u32[]{:S(2)}) collective-permute-start(bf16[1024,128]{1,0:T(8,128)(2,1)S(1)} %relay.7), channel_id=1, source_target_pairs={{0,1},{1,0},{2,3},{3,2},{4,5},{5,4},{6,7},{7,6},{8,9},{9,8},{10,11... | collective-permute-start | bytes 786440 | tf_op jit(solution)/shard_map/ppermute | solution.py:549
  104.5 15.0 %collective-permute-start = (bf16[1024,128]{1,0:T(8,128)(2,1)S(1)}, bf16[1024,128]{1,0:T(8,128)(2,1)S(1)}, u32[]{:S(2)}, u32[]{:S(2)}) collective-permute-start(bf16[1024,128]{1,0:T(8,128)(2,1)S(1)} %get-tuple-element.33.rows), channel_id=1, source_target_pairs={{0,2},{1,3},{2,0},{3,1},{4,6},{5,7},{6,4},{7,5},{8,10},{9,11},{10,... | collective-permute-start | bytes 786440 | tf_op jit(solution)/shard_map/cond/branch_0_fun/ppermute | solution.py:549
  106.6 12.8 %collective-permute-start.1 = (bf16[1024,128]{1,0:T(8,128)(2,1)S(1)}, bf16[1024,128]{1,0:T(8,128)(2,1)S(1)}, u32[]{:S(2)}, u32[]{:S(2)}) collective-permute-start(bf16[1024,128]{1,0:T(8,128)(2,1)S(1)} %get-tuple-element.33.rows), channel_id=1, source_target_pairs={{0,1},{1,0},{2,3},{3,2},{4,5},{5,4},{6,7},{7,6},{8,9},{9,8},{10,11... | collective-permute-start | bytes 786440 | tf_op jit(solution)/shard_map/cond/branch_0_fun/ppermute | solution.py:549
  108.8 16.6 %collective-permute-start.3 = (bf16[1040,128]{1,0:T(8,128)(2,1)S(1)}, bf16[1040,128]{1,0:T(8,128)(2,1)S(1)}, u32[]{:S(2)}, u32[]{:S(2)}) collective-permute-start(bf16[1040,128]{1,0:T(8,128)(2,1)S(1)} %prepare.3.refs_0_), channel_id=1, source_target_pairs={{0,8},{4,12},{8,0},{12,4},{16,24},{20,28},{24,16},{28,20},{1,9},{5... | collective-permute-start | bytes 798728 | tf_op jit(solution)/shard_map/cond/branch_0_fun/ppermute | solution.py:549
  109.4 16.0 %collective-permute-start.4 = (bf16[1040,128]{1,0:T(8,128)(2,1)S(1)}, bf16[1040,128]{1,0:T(8,128)(2,1)S(1)}, u32[]{:S(2)}, u32[]{:S(2)}) collective-permute-start(bf16[1040,128]{1,0:T(8,128)(2,1)S(1)} %prepare.3.refs_0_), channel_id=1, source_target_pairs={{0,16},{4,20},{8,24},{12,28},{16,0},{20,4},{24,8},{28,12},{1,17},{... | collective-permute-start | bytes 798728 | tf_op jit(solution)/shard_map/cond/branch_0_fun/ppermute | solution.py:549
  109.9 15.5 %collective-permute-start.5 = (bf16[1040,128]{1,0:T(8,128)(2,1)S(1)}, bf16[1040,128]{1,0:T(8,128)(2,1)S(1)}, u32[]{:S(2)}, u32[]{:S(2)}) collective-permute-start(bf16[1040,128]{1,0:T(8,128)(2,1)S(1)} %prepare.3.refs_0_), channel_id=1, source_target_pairs={{0,24},{4,28},{8,16},{12,20},{16,8},{20,12},{24,0},{28,4},{1,25},{... | collective-permute-start | bytes 798728 | tf_op jit(solution)/shard_map/cond/branch_0_fun/ppermute | solution.py:549
  119.4 7.6 %collective-permute-start.2 = (bf16[1024,128]{1,0:T(8,128)(2,1)S(1)}, bf16[1024,128]{1,0:T(8,128)(2,1)S(1)}, u32[]{:S(2)}, u32[]{:S(2)}) collective-permute-start(bf16[1024,128]{1,0:T(8,128)(2,1)S(1)} %relay.4), channel_id=1, source_target_pairs={{0,1},{1,0},{2,3},{3,2},{4,5},{5,4},{6,7},{7,6},{8,9},{9,8},{10,11... | collective-permute-start | bytes 786440 | tf_op jit(solution)/shard_map/cond/branch_0_fun/ppermute | solution.py:549
  132.1 15.0 %collective-permute-start.7 = (bf16[1024,128]{1,0:T(8,128)(2,1)S(1)}, bf16[1024,128]{1,0:T(8,128)(2,1)S(1)}, u32[]{:S(2)}, u32[]{:S(2)}) collective-permute-start(bf16[1024,128]{1,0:T(8,128)(2,1)S(1)} %fusion.rows), channel_id=1, source_target_pairs={{0,2},{1,3},{2,0},{3,1},{4,6},{5,7},{6,4},{7,5},{8,10},{9,11},{10,... | collective-permute-start | bytes 786440 | tf_op jit(solution)/shard_map/cond/branch_0_fun/ppermute | solution.py:549
  134.7 12.5 %collective-permute-start.8 = (bf16[1024,128]{1,0:T(8,128)(2,1)S(1)}, bf16[1024,128]{1,0:T(8,128)(2,1)S(1)}, u32[]{:S(2)}, u32[]{:S(2)}) collective-permute-start(bf16[1024,128]{1,0:T(8,128)(2,1)S(1)} %fusion.rows), channel_id=1, source_target_pairs={{0,1},{1,0},{2,3},{3,2},{4,5},{5,4},{6,7},{7,6},{8,9},{9,8},{10,11... | collective-permute-start | bytes 786440 | tf_op jit(solution)/shard_map/cond/branch_0_fun/ppermute | solution.py:549
  137.0 16.5 %collective-permute-start.10 = (bf16[1040,128]{1,0:T(8,128)(2,1)S(1)}, bf16[1040,128]{1,0:T(8,128)(2,1)S(1)}, u32[]{:S(2)}, u32[]{:S(2)}) collective-permute-start(bf16[1040,128]{1,0:T(8,128)(2,1)S(1)} %prepare.4.refs_0_), channel_id=1, source_target_pairs={{0,8},{4,12},{8,0},{12,4},{16,24},{20,28},{24,16},{28,20},{1,9},{5... | collective-permute-start | bytes 798728 | tf_op jit(solution)/shard_map/cond/branch_0_fun/ppermute | solution.py:549
  137.4 16.1 %collective-permute-start.11 = (bf16[1040,128]{1,0:T(8,128)(2,1)S(1)}, bf16[1040,128]{1,0:T(8,128)(2,1)S(1)}, u32[]{:S(2)}, u32[]{:S(2)}) collective-permute-start(bf16[1040,128]{1,0:T(8,128)(2,1)S(1)} %prepare.4.refs_0_), channel_id=1, source_target_pairs={{0,16},{4,20},{8,24},{12,28},{16,0},{20,4},{24,8},{28,12},{1,17},{... | collective-permute-start | bytes 798728 | tf_op jit(solution)/shard_map/cond/branch_0_fun/ppermute | solution.py:549
  138.0 15.5 %collective-permute-start.12 = (bf16[1040,128]{1,0:T(8,128)(2,1)S(1)}, bf16[1040,128]{1,0:T(8,128)(2,1)S(1)}, u32[]{:S(2)}, u32[]{:S(2)}) collective-permute-start(bf16[1040,128]{1,0:T(8,128)(2,1)S(1)} %prepare.4.refs_0_), channel_id=1, source_target_pairs={{0,24},{4,28},{8,16},{12,20},{16,8},{20,12},{24,0},{28,4},{1,25},{... | collective-permute-start | bytes 798728 | tf_op jit(solution)/shard_map/cond/branch_0_fun/ppermute | solution.py:549
  147.3 7.5 %collective-permute-start.9 = (bf16[1024,128]{1,0:T(8,128)(2,1)S(1)}, bf16[1024,128]{1,0:T(8,128)(2,1)S(1)}, u32[]{:S(2)}, u32[]{:S(2)}) collective-permute-start(bf16[1024,128]{1,0:T(8,128)(2,1)S(1)} %relay.5), channel_id=1, source_target_pairs={{0,1},{1,0},{2,3},{3,2},{4,5},{5,4},{6,7},{7,6},{8,9},{9,8},{10,11... | collective-permute-start | bytes 786440 | tf_op jit(solution)/shard_map/cond/branch_0_fun/ppermute | solution.py:549
  168.4 6.1 %collective-permute-start.19 = (f32[72,128]{1,0:T(8,128)S(1)}, f32[72,128]{1,0:T(8,128)S(1)}, u32[]{:S(2)}, u32[]{:S(2)}) collective-permute-start(f32[72,128]{1,0:T(8,128)S(1)} %add_add_fusion.1), channel_id=1, source_target_pairs={{0,2},{1,3},{2,0},{3,1},{4,6},{5,7},{6,4},{7,5},{8,10},{9,11},{10,... | collective-permute-start | bytes 110600 | tf_op jit(solution)/shard_map/cond/branch_0_fun/ppermute | solution.py:549
  (25 other events, 151.6 us)

commit v4 on v3

--- a/solution.py
+++ b/solution.py
@@ -114,10 +114,10 @@
         ref[half:, :] = jnp.broadcast_to(row, (DIAGONAL_ROWS, n))
 
 
-def unhalved(place, mine, other, whole):
+def unhalved(core, mine, other, whole):
     n = whole.shape[0]
     half = n // 2
-    here = pl.multiple_of((place[1] & 1) * half, half)
+    here = pl.multiple_of(core * half, half)
     whole[pl.ds(here, half), :] = mine[:half, :]
     whole[pl.ds(half - here, half), :] = other[:half, :]
     stored = whole[...]
@@ -154,9 +154,8 @@
     return low, scale, moved + next_low * next_scale - dot(next_low, moved), next_scale, next_low
 
 
-def finish_kernel(total_rows, place, mine, other, product, out_ref, low_ref, scale_ref, fine_ref, whole, work, done, sems):
-    first, second = [x / total_rows for x in unhalved(place, mine, other, whole)]
-    step = product.shape[0] // sems.shape[0]
+def factors_kernel(total_rows, mine, other, low_ref, scale_ref, both_low_ref, both_scale_ref, fine_ref, whole, work):
+    first, second = [x / total_rows for x in unhalved(lax.axis_index("grp") & 1, mine, other, whole)]
     sizes = []
 
     def quickly(base):
@@ -164,53 +163,65 @@
         sizes.append(size)
         return low
 
-    def write(low, scale, both_low, next_scale, dot):
-        low_ref[...] = low
-        scale_ref[...] = scale
-        copies = []
-        for i in range(sems.shape[0]):
-            here = pl.ds(i * step, step)
-            x = product[here, :] * scale
-            done[here, :] = x * next_scale - dot(x, both_low, NT)
-            copies.append(pltpu.make_async_copy(done.at[here, :], out_ref.at[here, :], sems.at[i]))
-            copies[-1].start()
-        for copy in copies:
-            copy.wait()
-
     *found, next_low = both_factors(first, second, quickly, dot3)
-    write(*found, dot3)
+    refs = (low_ref, scale_ref, both_low_ref, both_scale_ref)
+    for ref, value in zip(refs, found):
+        ref[...] = value
     close = jnp.maximum(*sizes) <= CORRECTION_MAX
     fine = jnp.maximum(inflation_of(found[0]), inflation_of(next_low)) <= INFLATION_MAX
     fine_ref[0] = jnp.logical_and(close, fine).astype(jnp.int32)
 
     @pl.when(jnp.logical_not(close))
     def _():
-        *found, _ = both_factors(first, second, lambda base: eliminated(base, work), dot6)
-        write(*found, dot6)
-
-
-def finish(place, halves, product, total_rows):
-    n = product.shape[1]
-    return pl.pallas_call(
-        functools.partial(finish_kernel, total_rows),
-        out_shape=(
-            pltpu.HBM(product.shape, F32),
-            jax.ShapeDtypeStruct((n, n), F32),
-            jax.ShapeDtypeStruct((1, n), F32),
-            jax.ShapeDtypeStruct((1,), jnp.int32),
-        ),
-        in_specs=[SMEM] + [VMEM] * 3,
-        out_specs=(ANY, VMEM, VMEM, SMEM),
-        scratch_shapes=[
-            pltpu.VMEM((n, n), F32),
-            pltpu.VMEM((2, n, n), F32),
-            pltpu.VMEM(product.shape, F32),
-            pltpu.SemaphoreType.DMA((4,)),
-        ],
-        cost_estimate=cost(60 * n**3 + 6 * product.size * n, 8 * product.size),
-        compiler_params=vmem(8 * product.size),
+        for ref, value in zip(refs, both_factors(first, second, lambda base: eliminated(base, work), dot6)):
+            ref[...] = value
+
+
+def factors(halves, total_rows):
+    n = halves[0].shape[1]
+    square, row = jax.ShapeDtypeStruct((n, n), F32), jax.ShapeDtypeStruct((1, n), F32)
+    return pl.pallas_call(
+        functools.partial(factors_kernel, total_rows),
+        out_shape=(square, row, square, row, pltpu.SMEM((1,), jnp.int32)),
+        in_specs=[VMEM] * 2,
+        out_specs=(VMEM, VMEM, VMEM, VMEM, SMEM),
+        scratch_shapes=[pltpu.VMEM((n, n), F32), pltpu.VMEM((2, n, n), F32)],
+        cost_estimate=cost(60 * n**3, 8 * n * n),
+        compiler_params=vmem(0),
+        name="factors",
+    )(*held(*halves))
+
+
+def finish_kernel(dot, product, scale, low, next_scale, out_ref, done, sems):
+    step = product.shape[0] // sems.shape[0]
+    copies = []
+    for i in range(sems.shape[0]):
+        here = pl.ds(i * step, step)
+        x = product[here, :] * scale[...]
+        done[here, :] = x * next_scale[...] - dot(x, low[...], NT)
+        copies.append(pltpu.make_async_copy(done.at[here, :], out_ref.at[here, :], sems.at[i]))
+        copies[-1].start()
+    for copy in copies:
+        copy.wait()
+
+
+def finish(dot, product, scale, low, next_scale):
+    return pl.pallas_call(
+        functools.partial(finish_kernel, dot),
+        out_shape=pltpu.HBM(product.shape, F32),
+        in_specs=[VMEM] * 4,
+        out_specs=ANY,
+        scratch_shapes=[pltpu.VMEM(product.shape, F32), pltpu.SemaphoreType.DMA((4,))],
+        cost_estimate=cost(6 * product.size * product.shape[1], 8 * product.size),
+        compiler_params=vmem(4 * product.size),
         name="finish",
-    )(place, *held(*halves, product))
+    )(*held(product, scale, low, next_scale))
+
+
+def entries(row):
+    lane = lax.broadcasted_iota(jnp.int32, row.shape, 1)
+    values = row[...]
+    return lambda i: jnp.sum(jnp.where(lane == i, values, 0))
 
 
 def add_near(shape, place, near_cols, tiles, near, r, acc):
@@ -218,7 +229,7 @@
     for k, ref in near:
         first = (r * sources + (place[0] ^ k)) * per_source
         for n in range(per_source):
-            start = pl.multiple_of(near_cols[first + n] * tile, tile)
+            start = pl.multiple_of(near_cols(first + n) * tile, tile)
             part = jnp.dot(tiles[first + n], ref[pl.ds(start, tile), :], preferred_element_type=F32)
             acc = part if acc is None else acc + part
     return acc
@@ -294,25 +305,29 @@
     )(rows, need)
 
 
-def pack_kernel(tile, n, place, wanted, *refs):
+def pack_kernel(tile, n, wanted, *refs):
     out_ref = refs[-1]
+    own = lax.axis_index("grp")
+    lane = lax.broadcasted_iota(jnp.int32, wanted.shape, 1)
+    needs = wanted[...]
     size = tile + NEED_ROWS
     for i, ref in enumerate(refs[:n]):
-        start = pl.multiple_of(jnp.maximum(wanted[place[1] ^ (2 * i)], 0) * tile, tile)
+        block = jnp.sum(jnp.where(lane == (own ^ (2 * i)), needs, 0))
+        start = pl.multiple_of(jnp.maximum(block, 0) * tile, tile)
         out_ref[i * size : i * size + tile, :] = ref[pl.ds(start, tile), :]
         out_ref[i * size + tile : (i + 1) * size, :] = ref[ref.shape[0] - NEED_ROWS :, :]
 
 
-def pack(tile, place, wanted, rows, tokens):
+def pack(tile, wanted, rows, tokens):
     return pl.pallas_call(
         functools.partial(pack_kernel, tile, len(rows)),
         out_shape=pltpu.VMEM((len(rows) * (tile + NEED_ROWS), rows[0].shape[1]), BF16),
-        in_specs=[SMEM] * 2 + [VMEM] * len(rows) + [ANY] * len(tokens),
+        in_specs=[VMEM] * (1 + len(rows)) + [ANY] * len(tokens),
         out_specs=VMEM,
         cost_estimate=cost(0, 0),
         compiler_params=vmem(0),
         name="pack",
-    )(place, wanted, *held(*rows), *tokens)
+    )(wanted, *held(*rows), *tokens)
 
 
 def core_pack_kernel(tile, own, *refs):
@@ -336,7 +351,13 @@
     )(*held(own, *received))
 
 
-def early_kernel(shape, distances, n_far, place, near_cols, far_groups, *refs):
+def flat_rows(scalars):
+    return [x.reshape(-1) for x in scalars]
+
+
+def early_kernel(shape, distances, n_far, near_cols, far_groups, *refs):
+    place = lax.axis_index("blk"), lax.axis_index("grp")
+    near_cols, far_groups = near_cols.__getitem__, far_groups.__getitem__
     blocks, _, _, tile = shape
     n = len(distances)
     near = list(zip(distances, refs[:n]))
@@ -359,16 +380,18 @@
     return pl.pallas_call(
         functools.partial(early_kernel, shape, distances, len(far)),
         out_shape=pltpu.VMEM((blocks * tile, width), F32),
-        in_specs=[SMEM] * 3 + [VMEM] * (len(rows) + len(far) + 2),
+        in_specs=[SMEM] * 2 + [VMEM] * (len(rows) + len(far) + 2),
         out_specs=VMEM,
         scratch_shapes=[pltpu.VMEM((groups, tile, width), BF16)],
         cost_estimate=cost(0, 0),
         compiler_params=vmem(0),
         name="early",
-    )(*scalars, *held(*rows, *far, tiles_near, tiles_far))
-
-
-def near_kernel(shape, distances, place, near_cols, *refs):
+    )(*flat_rows(scalars), *held(*rows, *far, tiles_near, tiles_far))
+
+
+def near_kernel(shape, distances, near_cols, *refs):
+    place = lax.axis_index("blk"), lax.axis_index("grp")
+    near_cols = near_cols.__getitem__
     blocks, _, _, tile = shape
     n = len(distances)
     *before, tiles, out_ref = refs[n:]
@@ -385,12 +408,12 @@
     return pl.pallas_call(
         functools.partial(near_kernel, shape, distances),
         out_shape=pltpu.VMEM((blocks * tile, rows[0].shape[1]), F32),
-        in_specs=[SMEM] * 2 + [VMEM] * (len(rows) + len(before) + 1),
+        in_specs=[SMEM] + [VMEM] * (len(rows) + len(before) + 1),
         out_specs=VMEM,
         cost_estimate=cost(0, 0),
         compiler_params=vmem(0),
         name="near",
-    )(*scalars[:2], *held(*rows, *before, tiles))
+    )(*flat_rows(scalars[:1]), *held(*rows, *before, tiles))
 
 
 def far_table(place, need, far, packed, table):
@@ -400,14 +423,14 @@
         h = place[1] ^ (2 * i)
         table[h ^ 1] = packed[i * size : i * size + tile, :]
         if i:
-            start = pl.multiple_of(jnp.maximum(need[h], 0) * tile, tile)
+            start = pl.multiple_of(jnp.maximum(need(h), 0) * tile, tile)
             table[h] = far[i - 1][pl.ds(start, tile), :]
 
 
 def add_far(far_groups, tiles, table, r, blocks, acc):
     each = tiles.shape[0] // blocks
     for t in range(r * each, (r + 1) * each):
-        acc = acc + jnp.dot(tiles[t], table[far_groups[t]], preferred_element_type=F32)
+        acc = acc + jnp.dot(tiles[t], table[far_groups(t)], preferred_element_type=F32)
     return acc
 
 
@@ -422,10 +445,13 @@
     return gram[:n, :n] + (crossed + crossed.T) + gram[n:, n:]
 
 
-def late_kernel(shape, place, far_groups, need, partial, *refs):
+def late_kernel(shape, far_groups, need, partial, *refs):
+    place = lax.axis_index("blk"), lax.axis_index("grp")
+    groups = need.shape[1]
+    far_groups, need = entries(far_groups), entries(need)
     blocks, _, _, tile = shape
-    *far, packed, tiles = refs[: need.shape[0] // 2 + 1]
-    product_ref, rounded_ref, table = refs[need.shape[0] // 2 + 1 :]
+    *far, packed, tiles = refs[: groups // 2 + 1]
+    product_ref, rounded_ref, table = refs[groups // 2 + 1 :]
     far_table(place, need, far, packed, table)
     for r in range(blocks):
         here = pl.ds(r * tile, tile)
@@ -436,17 +462,17 @@
 
 def late(shape, scalars, need, partial, far, tiles):
     n, width = partial.shape
-    groups, tile = need.shape[0], shape[3]
+    groups, tile = need.shape[1], shape[3]
     return pl.pallas_call(
         functools.partial(late_kernel, shape),
         out_shape=(pltpu.VMEM((n, width), F32), pltpu.VMEM((n, width), BF16)),
-        in_specs=[SMEM] * 3 + [VMEM] * (len(far) + 2),
+        in_specs=[VMEM] * (len(far) + 4),
         out_specs=(VMEM,) * 2,
         scratch_shapes=[pltpu.VMEM((groups, tile, width), BF16)],
         cost_estimate=cost(0, 0),
         compiler_params=vmem(0),
         name="late",
-    )(scalars[0], scalars[2], need, *held(partial, *far, tiles))
+    )(scalars[1], need, *held(partial, *far, tiles))
 
 
 def gram_kernel(tile, product, rounded, out_ref, copy_ref):
@@ -467,25 +493,27 @@
     )(*held(product, rounded))
 
 
-def halves_kernel(place, a, b, mine, other, whole):
+def halves_kernel(a, b, mine, other, whole):
+    place = lax.axis_index("blk"), lax.axis_index("grp")
     halved(place, a[...], b[...], whole, mine, other)
 
 
-def halves_of(place, a, b):
+def halves_of(a, b):
     n = a.shape[0]
     half = pltpu.VMEM((n // 2 + DIAGONAL_ROWS, n), F32)
     return pl.pallas_call(
         halves_kernel,
         out_shape=(half, half),
-        in_specs=[SMEM] + [VMEM] * 2,
+        in_specs=[VMEM] * 2,
         out_specs=(VMEM,) * 2,
         scratch_shapes=[pltpu.VMEM((n, n), F32)],
         compiler_params=vmem(0),
         name="halves",
-    )(place, a, b)
-
-
-def blocks_kernel(tile, n_far, place, rounded, *refs):
+    )(a, b)
+
+
+def blocks_kernel(tile, n_far, rounded, *refs):
+    place = lax.axis_index("blk"), lax.axis_index("grp")
     *far, packed = refs[:n_far]
     own_ref, *outs = refs[n_far + 1 :]
     lane = lax.broadcasted_iota(jnp.int32, (1, rounded.shape[1]), 1) == place[1]
@@ -503,21 +531,23 @@
         out_ref[tile:, :] = wanted_block(2 * i + 1)
 
 
-def blocks_for_others(tile, place, rounded, far, token):
+def blocks_for_others(tile, rounded, far, token):
     width = rounded.shape[1]
     pair = pltpu.VMEM((2 * tile, width), BF16)
     return pl.pallas_call(
         functools.partial(blocks_kernel, tile, len(far)),
         out_shape=(pltpu.VMEM((tile, width), BF16), *(pair,) * (len(far) - 1)),
-        in_specs=[SMEM] + [VMEM] * (1 + len(far)) + [ANY],
+        in_specs=[VMEM] * (1 + len(far)) + [ANY],
         out_specs=(VMEM,) * len(far),
         cost_estimate=cost(0, 0),
         compiler_params=vmem(0),
         name="blocks",
-    )(place, *held(rounded, *far), token)
-
-
-def last_kernel(shape, distances, place, near_cols, partial, *refs):
+    )(*held(rounded, *far), token)
+
+
+def last_kernel(shape, distances, near_cols, partial, *refs):
+    place = lax.axis_index("blk"), lax.axis_index("grp")
+    near_cols = entries(near_cols)
     blocks, _, _, tile = shape
     n = len(distances)
     near = list(zip(distances, refs[:n]))
@@ -535,13 +565,13 @@
     return pl.pallas_call(
         functools.partial(last_kernel, shape, distances),
         out_shape=(pltpu.VMEM(partial.shape, F32), half, half),
-        in_specs=[SMEM] * 2 + [VMEM] * (len(rows) + 3),
+        in_specs=[VMEM] * (len(rows) + 4),
         out_specs=(VMEM,) * 3,
         scratch_shapes=[pltpu.VMEM((width, width), F32)],
         cost_estimate=cost(0, 0),
         compiler_params=vmem(0),
         name="last",
-    )(*scalars[:2], *held(partial, *rows, past, tiles))
+    )(scalars[0], *held(partial, *rows, past, tiles))
 
 
 def swap(x, axis, mask):
@@ -584,43 +614,44 @@
     groups = lax.axis_size("grp")
     shape = (blocks, sources, tiles_near.shape[0] // (blocks * sources), tile)
     total_rows = start_vectors.shape[0] * sources * groups
-    place = jnp.stack([lax.axis_index("blk"), lax.axis_index("grp")]).astype(jnp.int32)
-    scalars = (place, near_cols.reshape(-1), far_groups.reshape(-1))
-    need = need_blocks.reshape(-1)
-    wanted = swap(need_blocks, "grp", 1).reshape(-1)
+    scalars = (near_cols, far_groups)
+    wanted = swap(need_blocks, "grp", 1)
     split = 3 * sources // 4
 
     def begin(rows):
-        below = prepare(rows, need)
+        below = prepare(rows, need_blocks.reshape(-1))
         far = [swap(below, "grp", k) for k in range(2, groups, 2)]
         near = near_rows(rows, rows)
         near[0] = (0, below)
         tiles = load(near[1][1], tiles_near, tiles_far)
         partial = near_product(shape, scalars, near[:split], tiles[0])
         tokens = [partial, *(x for _, x in near[split:])]
-        far.append(swap(pack(tile, place, wanted, [below, *far], tokens), "grp", 1))
+        far.append(swap(pack(tile, wanted, [below, *far], tokens), "grp", 1))
         partial = near_product(shape, scalars, near[split:], tiles[0], partial)
-        return tiles, far, late(shape, scalars, need, partial, far, tiles[1])
+        return tiles, far, late(shape, scalars, need_blocks, partial, far, tiles[1])
 
     tiles, far, (product, rounded) = begin(start_vectors)
     past, copied = gram(tile, product, rounded)
-    own, *outs = blocks_for_others(tile, place, rounded, far, past)
+    own, *outs = blocks_for_others(tile, rounded, far, past)
     near = near_rows(rounded, copied)
     far = [swap(x, "grp", 2 * i) for i, x in enumerate(outs, 1)]
     far.insert(0, swap(core_pack(own, far), "grp", 1))
     partial = early(shape, groups, scalars, near[:split], far, *tiles)
     moved, *halves = last(shape, scalars, partial, near[split:], tiles[0], past)
-    vectors, low, scale, fine = finish(place, everywhere(*halves), moved, total_rows)
+    low, scale, both_low, next_scale, fine = factors(everywhere(*halves), total_rows)
+    vectors = finish(dot3, moved, scale, both_low, next_scale)
 
     def plain(start, vectors, low, scale):
         _, _, (product, _) = begin(start)
         current = scaled(product, scale, low, dot6).astype(BF16)
         _, _, (product, rounded) = begin(current)
         unit = jnp.eye(product.shape[1], dtype=F32) * start.shape[0]
-        halves = everywhere(*halves_of(place, unit, gram(tile, product, rounded)[0]))
-        return finish(place, halves, product, total_rows)[0]
-
-    return lax.cond(fine[0] > 0, lambda start, vectors, low, scale: vectors, plain, start_vectors, vectors, low, scale)
+        halves = everywhere(*halves_of(unit, gram(tile, product, rounded)[0]))
+        _, scale, both_low, next_scale, _ = factors(halves, total_rows)
+        return finish(dot6, product, scale, both_low, next_scale)
+
+    branches = [plain, lambda start, vectors, low, scale: vectors]
+    return lax.switch(fine[0], branches, start_vectors, vectors, low, scale)
 
 
 def solution(mesh):

time: 183 us -> 176 us (0.962)
  Pallas kernels: 70.3 us -> 63.5 us
    pallas_call x3 -> x5, Pallas kernels: 38 us -> 34.6 us  [the longest x2 32.2 us: factors(): pl.pallas_call(functools.partial(factors_kernel, total_rows), out_shape=(...]
  transfers between devices with their start and end apart: 45 -> 45, of which waited for: 29 -> 30; matrix products, arithmetic and copies ran while one was open for 0% -> 0% of each run, Pallas kernels for 12% -> 13%
where the time goes in v4:
time: 176 us
  Pallas kernels  63.5 us (36%)
  waiting for transfers between devices  55.7 us (32%)
  starting transfers between devices  55 us (31%)
    ppermute x45, waiting for transfers between devices, swap(): return lax.ppermute(x, axis, [(i, i ^ mask) for i in range(size)])  55.7 us
    ppermute x45, starting transfers between devices, swap(): return lax.ppermute(x, axis, [(i, i ^ mask) for i in range(size)])  55 us
    pallas_call x2, Pallas kernels, factors(): pl.pallas_call(functools.partial(factors_kernel, total_rows), out_shape=(...  32.2 us
    pallas_call x3, Pallas kernels, load(): pl.pallas_call(functools.partial(load_kernel, n), out_shape=tuple((pltpu....  9.55 us
    pallas_call x6, Pallas kernels, near_product(): pl.pallas_call(functools.partial(near_kernel, shape, distances), out_shap...  7.53 us
    pallas_call x3, Pallas kernels, late(): pl.pallas_call(functools.partial(late_kernel, shape), out_shape=(pltpu.VM...  4.13 us
  transfers between devices with their start and end apart: 45, of which 30 were waited for; matrix products, arithmetic and copies ran while one was open for 0% of the time, Pallas kernels for 13%

profile of v4, /device:TPU:0, one launch (start us, length us, event | category | flops | bytes accessed | tf_op | source)
XLA Modules:
  0.0 175.9 jit_solution(17337607400742608682)
XLA Ops:
  0.0 4.0 %collective-permute-start.22 = (bf16[1024,128]{1,0:T(8,128)(2,1)}, bf16[1024,128]{1,0:T(8,128)(2,1)S(1)}, u32[]{:S(2)}, u32[]{:S(2)}) collective-permute-start(bf16[1024,128]{1,0:T(8,128)(2,1)} %rows.1), channel_id=1, source_target_pairs={{0,2},{1,3},{2,0},{3,1},{4,6},{5,7},{6,4},{7,5},{8,10},{9,11},{10,... | collective-permute-start | bytes 786440 | tf_op jit(solution)/shard_map/ppermute | solution.py:579
  10.2 6.1 %collective-permute-done.22.x_ref.refs_2_.refs_1_ = bf16[1024,128]{1,0:T(8,128)(2,1)S(1)} collective-permute-done((bf16[1024,128]{1,0:T(8,128)(2,1)}, bf16[1024,128]{1,0:T(8,128)(2,1)S(1)}, u32[]{:S(2)}, u32[]{:S(2)}) %collective-permute-start.22) | collective-permute-done | bytes 262176 | tf_op jit(solution)/shard_map/ppermute | solution.py:579
  18.0 3.2 %load.5 = (bf16[32,256,256]{2,1,0:T(8,128)(2,1)S(1)}, bf16[24,256,256]{2,1,0:T(8,128)(2,1)S(1)}) custom-call(bf16[32,256,256]{2,1,0:T(8,128)(2,1)} %refs_0_.1, bf16[24,256,256]{2,1,0:T(8,128)(2,1)} %refs_1_.1, bf16[1024,128]{1,0:T(8,128)(2,1)S(1)} %collective-permute-done.22.x_ref.refs_2_.refs_1_), custom_call_target="tpu_custom_call" | custom-call | bytes 14680064 | tf_op jit(solution)/shard_map/load/pallas_call | solution.py:249
  26.7 3.1 %collective-permute-start.30 = (bf16[1024,128]{1,0:T(8,128)(2,1)S(1)}, bf16[1024,128]{1,0:T(8,128)(2,1)S(1)}, u32[]{:S(2)}, u32[]{:S(2)}) collective-permute-start(bf16[1024,128]{1,0:T(8,128)(2,1)S(1)} %get-tuple-element.69.rounded.refs_0_), channel_id=1, source_target_pairs={{0,2},{1,3},{2,0},{3,1},{4,6},{5,7},{6,4},{7,5},{8,10},{9,11},{10,... | collective-permute-start | bytes 786440 | tf_op jit(solution)/shard_map/ppermute | solution.py:579
  37.7 3.9 %collective-permute-done.33.refs_1_.refs_5_ = bf16[512,128]{1,0:T(8,128)(2,1)S(1)} collective-permute-done((bf16[512,128]{1,0:T(8,128)(2,1)S(1)}, bf16[512,128]{1,0:T(8,128)(2,1)S(1)}, u32[]{:S(2)}, u32[]{:S(2)}) %collective-permute-start.33) | collective-permute-done | bytes 131104 | tf_op jit(solution)/shard_map/ppermute | solution.py:579
  43.9 2.3 %early.1.partial = f32[1024,128]{1,0:T(8,128)S(1)} custom-call(s32[32]{0:T(128)S(1)} %bitcast.11, s32[24]{0:T(128)S(1)} %bitcast.19, bf16[1024,128]{1,0:T(8,128)(2,1)S(1)} %get-tuple-element.69.rounded.refs_0_, bf16[1024,128]{1,0:T(8,128)(2,1)S(1)} %collective-permute-done.30.refs_1_.x_ref, bf16[1024,128]{1,0:T(8,128)(2,1)S(1)} %collective-permute-done.31.refs_2_.refs_0_, ...), custom_call_target="tpu_custom_call" | custom-call | tf_op jit(solution)/shard_map/early/pallas_call | solution.py:380
  46.3 4.1 %collective-permute-done.36.refs_0_ = bf16[1024,128]{1,0:T(8,128)(2,1)S(1)} collective-permute-done((bf16[1024,128]{1,0:T(8,128)(2,1)S(1)}, bf16[1024,128]{1,0:T(8,128)(2,1)S(1)}, u32[]{:S(2)}, u32[]{:S(2)}) %collective-permute-start.36) | collective-permute-done | bytes 262176 | tf_op jit(solution)/shard_map/ppermute | solution.py:579
  56.7 1.9 %collective-permute-done.40 = f32[72,128]{1,0:T(8,128)S(1)} collective-permute-done((f32[72,128]{1,0:T(8,128)S(1)}, f32[72,128]{1,0:T(8,128)S(1)}, u32[]{:S(2)}, u32[]{:S(2)}) %collective-permute-start.40) | collective-permute-done | bytes 36896 | tf_op jit(solution)/shard_map/ppermute | solution.py:579
  59.3 2.9 %collective-permute-start.42 = (f32[72,128]{1,0:T(8,128)S(1)}, f32[72,128]{1,0:T(8,128)S(1)}, u32[]{:S(2)}, u32[]{:S(2)}) collective-permute-start(f32[72,128]{1,0:T(8,128)S(1)} %add_add_fusion.3), channel_id=1, source_target_pairs={{0,2},{1,3},{2,0},{3,1},{4,6},{5,7},{6,4},{7,5},{8,10},{9,11},{10,... | collective-permute-start | bytes 110600 | tf_op jit(solution)/shard_map/ppermute | solution.py:579
  64.2 3.7 %collective-permute-done.43 = f32[72,128]{1,0:T(8,128)S(1)} collective-permute-done((f32[72,128]{1,0:T(8,128)S(1)}, f32[72,128]{1,0:T(8,128)S(1)}, u32[]{:S(2)}, u32[]{:S(2)}) %collective-permute-start.43) | collective-permute-done | bytes 36896 | tf_op jit(solution)/shard_map/ppermute | solution.py:579
  69.2 29.6 %factors.3 = (f32[128,128]{1,0:T(8,128)S(1)}, f32[1,128]{1,0:T(1,128)S(1)}, f32[128,128]{1,0:T(8,128)S(1)}, f32[1,128]{1,0:T(1,128)S(1)}, s32[1]{0:T(128)S(4)}) custom-call(f32[72,128]{1,0:T(8,128)S(1)} %add_add_fusion.2.mine, f32[72,128]{1,0:T(8,128)S(1)} %collective-permute-done.44.other), custom_call_target="tpu_custom_call" | custom-call | flops 125829120 | bytes 131072 | tf_op jit(solution)/shard_map/factors/pallas_call | solution.py:183
  99.9 75.8 %conditional.1 = (f32[1024,128]{1,0:T(8,128)}) conditional(s32[]{:T(128)} %bitcast.6, (s32[1,32]{1,0:T(1,128)S(1)}, bf16[1024,128]{1,0:T(8,128)(2,1)S(1)}, s32[1,8]{1,0:T(1,128)S(1)}, bf16[32,256,256]{2,1,0:T(8,128)(2,1)}, bf16[24,256,256]{2,1,0:T(8,128)(2,1)}, /*index=5*/s32[1,8]{1,0:T(1,128)S(1)}, s32[1,24]{1,0:T(1,128)S(1)}, ...), branch_computations={%region_0.0_spmd, %region_1.0_spmd} | conditional | flops 428309504 | bytes 48027000 | solution.py:654
  100.1 2.2 %collective-permute-start = (bf16[1024,128]{1,0:T(8,128)(2,1)S(1)}, bf16[1024,128]{1,0:T(8,128)(2,1)S(1)}, u32[]{:S(2)}, u32[]{:S(2)}) collective-permute-start(bf16[1024,128]{1,0:T(8,128)(2,1)S(1)} %get-tuple-element.30.rows), channel_id=1, source_target_pairs={{0,2},{1,3},{2,0},{3,1},{4,6},{5,7},{6,4},{7,5},{8,10},{9,11},{10,... | collective-permute-start | bytes 786440 | tf_op jit(solution)/shard_map/cond/branch_0_fun/ppermute | solution.py:579
  105.6 2.4 %collective-permute-start.5 = (bf16[1040,128]{1,0:T(8,128)(2,1)S(1)}, bf16[1040,128]{1,0:T(8,128)(2,1)S(1)}, u32[]{:S(2)}, u32[]{:S(2)}) collective-permute-start(bf16[1040,128]{1,0:T(8,128)(2,1)S(1)} %prepare.3.refs_0_), channel_id=1, source_target_pairs={{0,24},{4,28},{8,16},{12,20},{16,8},{20,12},{24,0},{28,4},{1,25},{... | collective-permute-start | bytes 798728 | tf_op jit(solution)/shard_map/cond/branch_0_fun/ppermute | solution.py:579
  108.0 7.0 %collective-permute-done.x_ref.refs_2_.refs_1_ = bf16[1024,128]{1,0:T(8,128)(2,1)S(1)} collective-permute-done((bf16[1024,128]{1,0:T(8,128)(2,1)S(1)}, bf16[1024,128]{1,0:T(8,128)(2,1)S(1)}, u32[]{:S(2)}, u32[]{:S(2)}) %collective-permute-start) | collective-permute-done | bytes 262176 | tf_op jit(solution)/shard_map/cond/branch_0_fun/ppermute | solution.py:579
  116.4 3.2 %load.3 = (bf16[32,256,256]{2,1,0:T(8,128)(2,1)S(1)}, bf16[24,256,256]{2,1,0:T(8,128)(2,1)S(1)}) custom-call(bf16[32,256,256]{2,1,0:T(8,128)(2,1)} %get-tuple-element.31.refs_0_, bf16[24,256,256]{2,1,0:T(8,128)(2,1)} %get-tuple-element.32.refs_1_, bf16[1024,128]{1,0:T(8,128)(2,1)S(1)} %collective-permute-done.x_ref.refs_2_.refs_1_), custom_call_target="tpu_custom_call" | custom-call | bytes 14680064 | tf_op jit(solution)/shard_map/cond/branch_0_fun/load/pallas_call | solution.py:249
  126.9 2.6 %collective-permute-start.7 = (bf16[1024,128]{1,0:T(8,128)(2,1)S(1)}, bf16[1024,128]{1,0:T(8,128)(2,1)S(1)}, u32[]{:S(2)}, u32[]{:S(2)}) collective-permute-start(bf16[1024,128]{1,0:T(8,128)(2,1)S(1)} %fusion.rows), channel_id=1, source_target_pairs={{0,2},{1,3},{2,0},{3,1},{4,6},{5,7},{6,4},{7,5},{8,10},{9,11},{10,... | collective-permute-start | bytes 786440 | tf_op jit(solution)/shard_map/cond/branch_0_fun/ppermute | solution.py:579
  132.8 2.6 %collective-permute-start.12 = (bf16[1040,128]{1,0:T(8,128)(2,1)S(1)}, bf16[1040,128]{1,0:T(8,128)(2,1)S(1)}, u32[]{:S(2)}, u32[]{:S(2)}) collective-permute-start(bf16[1040,128]{1,0:T(8,128)(2,1)S(1)} %prepare.4.refs_0_), channel_id=1, source_target_pairs={{0,24},{4,28},{8,16},{12,20},{16,8},{20,12},{24,0},{28,4},{1,25},{... | collective-permute-start | bytes 798728 | tf_op jit(solution)/shard_map/cond/branch_0_fun/ppermute | solution.py:579
  135.4 6.6 %collective-permute-done.7.x_ref.refs_2_.refs_1_ = bf16[1024,128]{1,0:T(8,128)(2,1)S(1)} collective-permute-done((bf16[1024,128]{1,0:T(8,128)(2,1)S(1)}, bf16[1024,128]{1,0:T(8,128)(2,1)S(1)}, u32[]{:S(2)}, u32[]{:S(2)}) %collective-permute-start.7) | collective-permute-done | bytes 262176 | tf_op jit(solution)/shard_map/cond/branch_0_fun/ppermute | solution.py:579
  143.6 3.2 %load.4 = (bf16[32,256,256]{2,1,0:T(8,128)(2,1)S(1)}, bf16[24,256,256]{2,1,0:T(8,128)(2,1)S(1)}) custom-call(bf16[32,256,256]{2,1,0:T(8,128)(2,1)} %get-tuple-element.31.refs_0_, bf16[24,256,256]{2,1,0:T(8,128)(2,1)} %get-tuple-element.32.refs_1_, bf16[1024,128]{1,0:T(8,128)(2,1)S(1)} %collective-permute-done.7.x_ref.refs_2_.refs_1_), custom_call_target="tpu_custom_call" | custom-call | bytes 14680064 | tf_op jit(solution)/shard_map/cond/branch_0_fun/load/pallas_call | solution.py:249
  158.9 2.4 %collective-permute-done.17 = f32[72,128]{1,0:T(8,128)S(1)} collective-permute-done((f32[72,128]{1,0:T(8,128)S(1)}, f32[72,128]{1,0:T(8,128)S(1)}, u32[]{:S(2)}, u32[]{:S(2)}) %collective-permute-start.17) | collective-permute-done | bytes 36896 | tf_op jit(solution)/shard_map/cond/branch_0_fun/ppermute | solution.py:579
  161.8 2.6 %collective-permute-start.19 = (f32[72,128]{1,0:T(8,128)S(1)}, f32[72,128]{1,0:T(8,128)S(1)}, u32[]{:S(2)}, u32[]{:S(2)}) collective-permute-start(f32[72,128]{1,0:T(8,128)S(1)} %add_add_fusion.1), channel_id=1, source_target_pairs={{0,2},{1,3},{2,0},{3,1},{4,6},{5,7},{6,4},{7,5},{8,10},{9,11},{10,... | collective-permute-start | bytes 110600 | tf_op jit(solution)/shard_map/cond/branch_0_fun/ppermute | solution.py:579
  167.9 2.4 %collective-permute-done.20 = f32[72,128]{1,0:T(8,128)S(1)} collective-permute-done((f32[72,128]{1,0:T(8,128)S(1)}, f32[72,128]{1,0:T(8,128)S(1)}, u32[]{:S(2)}, u32[]{:S(2)}) %collective-permute-start.20) | collective-permute-done | bytes 36896 | tf_op jit(solution)/shard_map/cond/branch_0_fun/ppermute | solution.py:579
  171.5 2.6 %factors.2 = (f32[128,128]{1,0:T(8,128)}, f32[1,128]{1,0:T(1,128)S(1)}, f32[128,128]{1,0:T(8,128)S(1)}, f32[1,128]{1,0:T(1,128)S(1)}, s32[1]{0:T(128)S(4)}) custom-call(f32[72,128]{1,0:T(8,128)S(1)} %add_add_fusion.mine, f32[72,128]{1,0:T(8,128)S(1)} %collective-permute-done.21.other), custom_call_target="tpu_custom_call" | custom-call | flops 125829120 | bytes 131072 | tf_op jit(solution)/shard_map/cond/branch_0_fun/factors/pallas_call | solution.py:183
  (116 shorter events, 70.3 us)
Async XLA Ops:
  0.0 16.3 %collective-permute-start.22 = (bf16[1024,128]{1,0:T(8,128)(2,1)}, bf16[1024,128]{1,0:T(8,128)(2,1)S(1)}, u32[]{:S(2)}, u32[]{:S(2)}) collective-permute-start(bf16[1024,128]{1,0:T(8,128)(2,1)} %rows.1), channel_id=1, source_target_pairs={{0,2},{1,3},{2,0},{3,1},{4,6},{5,7},{6,4},{7,5},{8,10},{9,11},{10,... | collective-permute-start | bytes 786440 | tf_op jit(solution)/shard_map/ppermute | solution.py:579
  4.0 12.4 %collective-permute-start.23 = (bf16[1024,128]{1,0:T(8,128)(2,1)}, bf16[1024,128]{1,0:T(8,128)(2,1)S(1)}, u32[]{:S(2)}, u32[]{:S(2)}) collective-permute-start(bf16[1024,128]{1,0:T(8,128)(2,1)} %rows.1), channel_id=1, source_target_pairs={{0,1},{1,0},{2,3},{3,2},{4,5},{5,4},{6,7},{7,6},{8,9},{9,8},{10,11... | collective-permute-start | bytes 786440 | tf_op jit(solution)/shard_map/ppermute | solution.py:579
  6.6 16.2 %collective-permute-start.25 = (bf16[1040,128]{1,0:T(8,128)(2,1)S(1)}, bf16[1040,128]{1,0:T(8,128)(2,1)S(1)}, u32[]{:S(2)}, u32[]{:S(2)}) collective-permute-start(bf16[1040,128]{1,0:T(8,128)(2,1)S(1)} %prepare.5.refs_0_), channel_id=1, source_target_pairs={{0,8},{4,12},{8,0},{12,4},{16,24},{20,28},{24,16},{28,20},{1,9},{5... | collective-permute-start | bytes 798728 | tf_op jit(solution)/shard_map/ppermute | solution.py:579
  8.2 14.6 %collective-permute-start.26 = (bf16[1040,128]{1,0:T(8,128)(2,1)S(1)}, bf16[1040,128]{1,0:T(8,128)(2,1)S(1)}, u32[]{:S(2)}, u32[]{:S(2)}) collective-permute-start(bf16[1040,128]{1,0:T(8,128)(2,1)S(1)} %prepare.5.refs_0_), channel_id=1, source_target_pairs={{0,16},{4,20},{8,24},{12,28},{16,0},{20,4},{24,8},{28,12},{1,17},{... | collective-permute-start | bytes 798728 | tf_op jit(solution)/shard_map/ppermute | solution.py:579
  9.7 13.1 %collective-permute-start.27 = (bf16[1040,128]{1,0:T(8,128)(2,1)S(1)}, bf16[1040,128]{1,0:T(8,128)(2,1)S(1)}, u32[]{:S(2)}, u32[]{:S(2)}) collective-permute-start(bf16[1040,128]{1,0:T(8,128)(2,1)S(1)} %prepare.5.refs_0_), channel_id=1, source_target_pairs={{0,24},{4,28},{8,16},{12,20},{16,8},{20,12},{24,0},{28,4},{1,25},{... | collective-permute-start | bytes 798728 | tf_op jit(solution)/shard_map/ppermute | solution.py:579
  16.5 7.3 %collective-permute-start.24 = (bf16[1024,128]{1,0:T(8,128)(2,1)S(1)}, bf16[1024,128]{1,0:T(8,128)(2,1)S(1)}, u32[]{:S(2)}, u32[]{:S(2)}) collective-permute-start(bf16[1024,128]{1,0:T(8,128)(2,1)S(1)} %relay.6), channel_id=1, source_target_pairs={{0,1},{1,0},{2,3},{3,2},{4,5},{5,4},{6,7},{7,6},{8,9},{9,8},{10,11... | collective-permute-start | bytes 786440 | tf_op jit(solution)/shard_map/ppermute | solution.py:579
  26.7 15.4 %collective-permute-start.30 = (bf16[1024,128]{1,0:T(8,128)(2,1)S(1)}, bf16[1024,128]{1,0:T(8,128)(2,1)S(1)}, u32[]{:S(2)}, u32[]{:S(2)}) collective-permute-start(bf16[1024,128]{1,0:T(8,128)(2,1)S(1)} %get-tuple-element.69.rounded.refs_0_), channel_id=1, source_target_pairs={{0,2},{1,3},{2,0},{3,1},{4,6},{5,7},{6,4},{7,5},{8,10},{9,11},{10,... | collective-permute-start | bytes 786440 | tf_op jit(solution)/shard_map/ppermute | solution.py:579
  30.2 12.5 %collective-permute-start.31 = (bf16[1024,128]{1,0:T(8,128)(2,1)S(1)}, bf16[1024,128]{1,0:T(8,128)(2,1)S(1)}, u32[]{:S(2)}, u32[]{:S(2)}) collective-permute-start(bf16[1024,128]{1,0:T(8,128)(2,1)S(1)} %get-tuple-element.71), channel_id=1, source_target_pairs={{0,1},{1,0},{2,3},{3,2},{4,5},{5,4},{6,7},{7,6},{8,9},{9,8},{10,11... | collective-permute-start | bytes 786440 | tf_op jit(solution)/shard_map/ppermute | solution.py:579
  33.8 7.8 %collective-permute-start.33 = (bf16[512,128]{1,0:T(8,128)(2,1)S(1)}, bf16[512,128]{1,0:T(8,128)(2,1)S(1)}, u32[]{:S(2)}, u32[]{:S(2)}) collective-permute-start(bf16[512,128]{1,0:T(8,128)(2,1)S(1)} %get-tuple-element.75), channel_id=1, source_target_pairs={{0,16},{4,20},{8,24},{12,28},{16,0},{20,4},{24,8},{28,12},{1,17},{... | collective-permute-start | bytes 393224 | tf_op jit(solution)/shard_map/ppermute | solution.py:579
  35.3 6.3 %collective-permute-start.34 = (bf16[512,128]{1,0:T(8,128)(2,1)S(1)}, bf16[512,128]{1,0:T(8,128)(2,1)S(1)}, u32[]{:S(2)}, u32[]{:S(2)}) collective-permute-start(bf16[512,128]{1,0:T(8,128)(2,1)S(1)} %get-tuple-element.76), channel_id=1, source_target_pairs={{0,24},{4,28},{8,16},{12,20},{16,8},{20,12},{24,0},{28,4},{1,25},{... | collective-permute-start | bytes 393224 | tf_op jit(solution)/shard_map/ppermute | solution.py:579
  42.7 7.7 %collective-permute-start.36 = (bf16[1024,128]{1,0:T(8,128)(2,1)S(1)}, bf16[1024,128]{1,0:T(8,128)(2,1)S(1)}, u32[]{:S(2)}, u32[]{:S(2)}) collective-permute-start(bf16[1024,128]{1,0:T(8,128)(2,1)S(1)} %relay.7), channel_id=1, source_target_pairs={{0,1},{1,0},{2,3},{3,2},{4,5},{5,4},{6,7},{7,6},{8,9},{9,8},{10,11... | collective-permute-start | bytes 786440 | tf_op jit(solution)/shard_map/ppermute | solution.py:579
  100.1 15.0 %collective-permute-start = (bf16[1024,128]{1,0:T(8,128)(2,1)S(1)}, bf16[1024,128]{1,0:T(8,128)(2,1)S(1)}, u32[]{:S(2)}, u32[]{:S(2)}) collective-permute-start(bf16[1024,128]{1,0:T(8,128)(2,1)S(1)} %get-tuple-element.30.rows), channel_id=1, source_target_pairs={{0,2},{1,3},{2,0},{3,1},{4,6},{5,7},{6,4},{7,5},{8,10},{9,11},{10,... | collective-permute-start | bytes 786440 | tf_op jit(solution)/shard_map/cond/branch_0_fun/ppermute | solution.py:579
  102.3 12.8 %collective-permute-start.1 = (bf16[1024,128]{1,0:T(8,128)(2,1)S(1)}, bf16[1024,128]{1,0:T(8,128)(2,1)S(1)}, u32[]{:S(2)}, u32[]{:S(2)}) collective-permute-start(bf16[1024,128]{1,0:T(8,128)(2,1)S(1)} %get-tuple-element.30.rows), channel_id=1, source_target_pairs={{0,1},{1,0},{2,3},{3,2},{4,5},{5,4},{6,7},{7,6},{8,9},{9,8},{10,11... | collective-permute-start | bytes 786440 | tf_op jit(solution)/shard_map/cond/branch_0_fun/ppermute | solution.py:579
  104.5 16.6 %collective-permute-start.3 = (bf16[1040,128]{1,0:T(8,128)(2,1)S(1)}, bf16[1040,128]{1,0:T(8,128)(2,1)S(1)}, u32[]{:S(2)}, u32[]{:S(2)}) collective-permute-start(bf16[1040,128]{1,0:T(8,128)(2,1)S(1)} %prepare.3.refs_0_), channel_id=1, source_target_pairs={{0,8},{4,12},{8,0},{12,4},{16,24},{20,28},{24,16},{28,20},{1,9},{5... | collective-permute-start | bytes 798728 | tf_op jit(solution)/shard_map/cond/branch_0_fun/ppermute | solution.py:579
  105.1 16.0 %collective-permute-start.4 = (bf16[1040,128]{1,0:T(8,128)(2,1)S(1)}, bf16[1040,128]{1,0:T(8,128)(2,1)S(1)}, u32[]{:S(2)}, u32[]{:S(2)}) collective-permute-start(bf16[1040,128]{1,0:T(8,128)(2,1)S(1)} %prepare.3.refs_0_), channel_id=1, source_target_pairs={{0,16},{4,20},{8,24},{12,28},{16,0},{20,4},{24,8},{28,12},{1,17},{... | collective-permute-start | bytes 798728 | tf_op jit(solution)/shard_map/cond/branch_0_fun/ppermute | solution.py:579
  105.6 15.5 %collective-permute-start.5 = (bf16[1040,128]{1,0:T(8,128)(2,1)S(1)}, bf16[1040,128]{1,0:T(8,128)(2,1)S(1)}, u32[]{:S(2)}, u32[]{:S(2)}) collective-permute-start(bf16[1040,128]{1,0:T(8,128)(2,1)S(1)} %prepare.3.refs_0_), channel_id=1, source_target_pairs={{0,24},{4,28},{8,16},{12,20},{16,8},{20,12},{24,0},{28,4},{1,25},{... | collective-permute-start | bytes 798728 | tf_op jit(solution)/shard_map/cond/branch_0_fun/ppermute | solution.py:579
  115.1 7.6 %collective-permute-start.2 = (bf16[1024,128]{1,0:T(8,128)(2,1)S(1)}, bf16[1024,128]{1,0:T(8,128)(2,1)S(1)}, u32[]{:S(2)}, u32[]{:S(2)}) collective-permute-start(bf16[1024,128]{1,0:T(8,128)(2,1)S(1)} %relay.4), channel_id=1, source_target_pairs={{0,1},{1,0},{2,3},{3,2},{4,5},{5,4},{6,7},{7,6},{8,9},{9,8},{10,11... | collective-permute-start | bytes 786440 | tf_op jit(solution)/shard_map/cond/branch_0_fun/ppermute | solution.py:579
  126.9 15.0 %collective-permute-start.7 = (bf16[1024,128]{1,0:T(8,128)(2,1)S(1)}, bf16[1024,128]{1,0:T(8,128)(2,1)S(1)}, u32[]{:S(2)}, u32[]{:S(2)}) collective-permute-start(bf16[1024,128]{1,0:T(8,128)(2,1)S(1)} %fusion.rows), channel_id=1, source_target_pairs={{0,2},{1,3},{2,0},{3,1},{4,6},{5,7},{6,4},{7,5},{8,10},{9,11},{10,... | collective-permute-start | bytes 786440 | tf_op jit(solution)/shard_map/cond/branch_0_fun/ppermute | solution.py:579
  129.5 12.5 %collective-permute-start.8 = (bf16[1024,128]{1,0:T(8,128)(2,1)S(1)}, bf16[1024,128]{1,0:T(8,128)(2,1)S(1)}, u32[]{:S(2)}, u32[]{:S(2)}) collective-permute-start(bf16[1024,128]{1,0:T(8,128)(2,1)S(1)} %fusion.rows), channel_id=1, source_target_pairs={{0,1},{1,0},{2,3},{3,2},{4,5},{5,4},{6,7},{7,6},{8,9},{9,8},{10,11... | collective-permute-start | bytes 786440 | tf_op jit(solution)/shard_map/cond/branch_0_fun/ppermute | solution.py:579
  131.8 16.5 %collective-permute-start.10 = (bf16[1040,128]{1,0:T(8,128)(2,1)S(1)}, bf16[1040,128]{1,0:T(8,128)(2,1)S(1)}, u32[]{:S(2)}, u32[]{:S(2)}) collective-permute-start(bf16[1040,128]{1,0:T(8,128)(2,1)S(1)} %prepare.4.refs_0_), channel_id=1, source_target_pairs={{0,8},{4,12},{8,0},{12,4},{16,24},{20,28},{24,16},{28,20},{1,9},{5... | collective-permute-start | bytes 798728 | tf_op jit(solution)/shard_map/cond/branch_0_fun/ppermute | solution.py:579
  132.3 16.1 %collective-permute-start.11 = (bf16[1040,128]{1,0:T(8,128)(2,1)S(1)}, bf16[1040,128]{1,0:T(8,128)(2,1)S(1)}, u32[]{:S(2)}, u32[]{:S(2)}) collective-permute-start(bf16[1040,128]{1,0:T(8,128)(2,1)S(1)} %prepare.4.refs_0_), channel_id=1, source_target_pairs={{0,16},{4,20},{8,24},{12,28},{16,0},{20,4},{24,8},{28,12},{1,17},{... | collective-permute-start | bytes 798728 | tf_op jit(solution)/shard_map/cond/branch_0_fun/ppermute | solution.py:579
  132.8 15.6 %collective-permute-start.12 = (bf16[1040,128]{1,0:T(8,128)(2,1)S(1)}, bf16[1040,128]{1,0:T(8,128)(2,1)S(1)}, u32[]{:S(2)}, u32[]{:S(2)}) collective-permute-start(bf16[1040,128]{1,0:T(8,128)(2,1)S(1)} %prepare.4.refs_0_), channel_id=1, source_target_pairs={{0,24},{4,28},{8,16},{12,20},{16,8},{20,12},{24,0},{28,4},{1,25},{... | collective-permute-start | bytes 798728 | tf_op jit(solution)/shard_map/cond/branch_0_fun/ppermute | solution.py:579
  142.1 7.5 %collective-permute-start.9 = (bf16[1024,128]{1,0:T(8,128)(2,1)S(1)}, bf16[1024,128]{1,0:T(8,128)(2,1)S(1)}, u32[]{:S(2)}, u32[]{:S(2)}) collective-permute-start(bf16[1024,128]{1,0:T(8,128)(2,1)S(1)} %relay.5), channel_id=1, source_target_pairs={{0,1},{1,0},{2,3},{3,2},{4,5},{5,4},{6,7},{7,6},{8,9},{9,8},{10,11... | collective-permute-start | bytes 786440 | tf_op jit(solution)/shard_map/cond/branch_0_fun/ppermute | solution.py:579
  161.8 6.1 %collective-permute-start.19 = (f32[72,128]{1,0:T(8,128)S(1)}, f32[72,128]{1,0:T(8,128)S(1)}, u32[]{:S(2)}, u32[]{:S(2)}) collective-permute-start(f32[72,128]{1,0:T(8,128)S(1)} %add_add_fusion.1), channel_id=1, source_target_pairs={{0,2},{1,3},{2,0},{3,1},{4,6},{5,7},{6,4},{7,5},{8,10},{9,11},{10,... | collective-permute-start | bytes 110600 | tf_op jit(solution)/shard_map/cond/branch_0_fun/ppermute | solution.py:579
  (25 other events, 147.6 us)

commit v5 on v4

--- a/solution.py
+++ b/solution.py
@@ -330,25 +330,25 @@
     )(wanted, *held(*rows), *tokens)
 
 
-def core_pack_kernel(tile, own, *refs):
+def core_pack_kernel(tile, n, own, *refs):
     out_ref = refs[-1]
     out_ref[:tile, :] = own[...]
-    for i, ref in enumerate(refs[:-1], 1):
+    for i, ref in enumerate(refs[:n], 1):
         out_ref[i * tile : (i + 1) * tile, :] = ref[tile:, :]
 
 
-def core_pack(own, received):
+def core_pack(own, received, token):
     tile, width = own.shape
     n = 1 + len(received)
     return pl.pallas_call(
-        functools.partial(core_pack_kernel, tile),
+        functools.partial(core_pack_kernel, tile, n - 1),
         out_shape=pltpu.VMEM((n * tile, width), BF16),
-        in_specs=[VMEM] * n,
+        in_specs=[VMEM] * n + [ANY],
         out_specs=VMEM,
         cost_estimate=cost(0, 0),
         compiler_params=vmem(0),
         name="core_pack",
-    )(*held(own, *received))
+    )(*held(own, *received), token)
 
 
 def flat_rows(scalars):
@@ -475,22 +475,21 @@
     )(scalars[1], need, *held(partial, *far, tiles))
 
 
-def gram_kernel(tile, product, rounded, out_ref, copy_ref):
+def gram_kernel(tile, product, out_ref):
     out_ref[...] = gram_of(product, tile)
-    copy_ref[...] = rounded[...]
-
-
-def gram(tile, product, rounded):
+
+
+def gram(tile, product):
     width = product.shape[1]
     return pl.pallas_call(
         functools.partial(gram_kernel, tile),
-        out_shape=(pltpu.VMEM((width, width), F32), pltpu.VMEM(rounded.shape, BF16)),
-        in_specs=[VMEM] * 2,
-        out_specs=(VMEM,) * 2,
+        out_shape=pltpu.VMEM((width, width), F32),
+        in_specs=[VMEM],
+        out_specs=VMEM,
         cost_estimate=cost(0, 0),
         compiler_params=vmem(0),
         name="gram",
-    )(*held(product, rounded))
+    )(*held(product))
 
 
 def halves_kernel(a, b, mine, other, whole):
@@ -631,11 +630,11 @@
         return tiles, far, late(shape, scalars, need_blocks, partial, far, tiles[1])
 
     tiles, far, (product, rounded) = begin(start_vectors)
-    past, copied = gram(tile, product, rounded)
+    past = gram(tile, product)
     own, *outs = blocks_for_others(tile, rounded, far, past)
-    near = near_rows(rounded, copied)
+    near = near_rows(rounded, rounded)
     far = [swap(x, "grp", 2 * i) for i, x in enumerate(outs, 1)]
-    far.insert(0, swap(core_pack(own, far), "grp", 1))
+    far.insert(0, swap(core_pack(own, far, near[1][1]), "grp", 1))
     partial = early(shape, groups, scalars, near[:split], far, *tiles)
     moved, *halves = last(shape, scalars, partial, near[split:], tiles[0], past)
     low, scale, both_low, next_scale, fine = factors(everywhere(*halves), total_rows)
@@ -644,9 +643,9 @@
     def plain(start, vectors, low, scale):
         _, _, (product, _) = begin(start)
         current = scaled(product, scale, low, dot6).astype(BF16)
-        _, _, (product, rounded) = begin(current)
+        _, _, (product, _) = begin(current)
         unit = jnp.eye(product.shape[1], dtype=F32) * start.shape[0]
-        halves = everywhere(*halves_of(unit, gram(tile, product, rounded)[0]))
+        halves = everywhere(*halves_of(unit, gram(tile, product)))
         _, scale, both_low, next_scale, _ = factors(halves, total_rows)
         return finish(dot6, product, scale, both_low, next_scale)
 

time: 176 us -> 177 us (level)
  transfers between devices with their start and end apart: 45 -> 45, of which waited for: 30 -> 29; matrix products, arithmetic and copies ran while one was open for 0% -> 0% of each run, Pallas kernels for 13% -> 13%
where the time goes in v5:
time: 177 us; the launch traced here: 176 us
  Pallas kernels  63.5 us (36%)
  waiting for transfers between devices  56.4 us (32%)
  starting transfers between devices  54.9 us (31%)
    ppermute x45, waiting for transfers between devices, swap(): return lax.ppermute(x, axis, [(i, i ^ mask) for i in range(size)])  56.4 us
    ppermute x45, starting transfers between devices, swap(): return lax.ppermute(x, axis, [(i, i ^ mask) for i in range(size)])  54.9 us
    pallas_call x2, Pallas kernels, factors(): pl.pallas_call(functools.partial(factors_kernel, total_rows), out_shape=(...  32.2 us
    pallas_call x3, Pallas kernels, load(): pl.pallas_call(functools.partial(load_kernel, n), out_shape=tuple((pltpu....  9.55 us
    pallas_call x6, Pallas kernels, near_product(): pl.pallas_call(functools.partial(near_kernel, shape, distances), out_shap...  7.53 us
    pallas_call x3, Pallas kernels, late(): pl.pallas_call(functools.partial(late_kernel, shape), out_shape=(pltpu.VM...  4.84 us
  transfers between devices with their start and end apart: 45, of which 29 were waited for; matrix products, arithmetic and copies ran while one was open for 0% of the time, Pallas kernels for 13%

profile of v5, /device:TPU:0, one launch (start us, length us, event | category | flops | bytes accessed | tf_op | source)
XLA Modules:
  0.0 176.5 jit_solution(8393459608254373849)
XLA Ops:
  0.0 4.0 %collective-permute-start.22 = (bf16[1024,128]{1,0:T(8,128)(2,1)}, bf16[1024,128]{1,0:T(8,128)(2,1)S(1)}, u32[]{:S(2)}, u32[]{:S(2)}) collective-permute-start(bf16[1024,128]{1,0:T(8,128)(2,1)} %rows.1), channel_id=1, source_target_pairs={{0,2},{1,3},{2,0},{3,1},{4,6},{5,7},{6,4},{7,5},{8,10},{9,11},{10,... | collective-permute-start | bytes 786440 | tf_op jit(solution)/shard_map/ppermute | solution.py:578
  10.2 6.1 %collective-permute-done.22.x_ref.refs_2_.refs_1_ = bf16[1024,128]{1,0:T(8,128)(2,1)S(1)} collective-permute-done((bf16[1024,128]{1,0:T(8,128)(2,1)}, bf16[1024,128]{1,0:T(8,128)(2,1)S(1)}, u32[]{:S(2)}, u32[]{:S(2)}) %collective-permute-start.22) | collective-permute-done | bytes 262176 | tf_op jit(solution)/shard_map/ppermute | solution.py:578
  18.0 3.2 %load.5 = (bf16[32,256,256]{2,1,0:T(8,128)(2,1)S(1)}, bf16[24,256,256]{2,1,0:T(8,128)(2,1)S(1)}) custom-call(bf16[32,256,256]{2,1,0:T(8,128)(2,1)} %refs_0_.1, bf16[24,256,256]{2,1,0:T(8,128)(2,1)} %refs_1_.1, bf16[1024,128]{1,0:T(8,128)(2,1)S(1)} %collective-permute-done.22.x_ref.refs_2_.refs_1_), custom_call_target="tpu_custom_call" | custom-call | bytes 14680064 | tf_op jit(solution)/shard_map/load/pallas_call | solution.py:249
  26.7 3.1 %collective-permute-start.30 = (bf16[1024,128]{1,0:T(8,128)(2,1)S(1)}, bf16[1024,128]{1,0:T(8,128)(2,1)S(1)}, u32[]{:S(2)}, u32[]{:S(2)}) collective-permute-start(bf16[1024,128]{1,0:T(8,128)(2,1)S(1)} %get-tuple-element.65.rounded.refs_0_), channel_id=1, source_target_pairs={{0,2},{1,3},{2,0},{3,1},{4,6},{5,7},{6,4},{7,5},{8,10},{9,11},{10,... | collective-permute-start | bytes 786440 | tf_op jit(solution)/shard_map/ppermute | solution.py:578
  37.6 3.9 %collective-permute-done.33.refs_1_.refs_5_ = bf16[512,128]{1,0:T(8,128)(2,1)S(1)} collective-permute-done((bf16[512,128]{1,0:T(8,128)(2,1)S(1)}, bf16[512,128]{1,0:T(8,128)(2,1)S(1)}, u32[]{:S(2)}, u32[]{:S(2)}) %collective-permute-start.33) | collective-permute-done | bytes 131104 | tf_op jit(solution)/shard_map/ppermute | solution.py:578
  43.9 2.4 %early.1.partial = f32[1024,128]{1,0:T(8,128)S(1)} custom-call(s32[32]{0:T(128)S(1)} %bitcast.11, s32[24]{0:T(128)S(1)} %bitcast.19, bf16[1024,128]{1,0:T(8,128)(2,1)S(1)} %get-tuple-element.65.rounded.refs_0_, bf16[1024,128]{1,0:T(8,128)(2,1)S(1)} %collective-permute-done.30.refs_3_.refs_1_.x_ref, ...), custom_call_target="tpu_custom_call" | custom-call | tf_op jit(solution)/shard_map/early/pallas_call | solution.py:380
  46.3 4.8 %collective-permute-done.36.refs_0_ = bf16[1024,128]{1,0:T(8,128)(2,1)S(1)} collective-permute-done((bf16[1024,128]{1,0:T(8,128)(2,1)S(1)}, bf16[1024,128]{1,0:T(8,128)(2,1)S(1)}, u32[]{:S(2)}, u32[]{:S(2)}) %collective-permute-start.36) | collective-permute-done | bytes 262176 | tf_op jit(solution)/shard_map/ppermute | solution.py:578
  54.0 2.3 %collective-permute-start.40 = (f32[72,128]{1,0:T(8,128)S(1)}, f32[72,128]{1,0:T(8,128)S(1)}, u32[]{:S(2)}, u32[]{:S(2)}) collective-permute-start(f32[72,128]{1,0:T(8,128)S(1)} %add.42), channel_id=1, source_target_pairs={{0,9},{1,8},{2,11},{3,10},{4,13},{5,12},{6,15},{7,14},{8,1},{9,0},... | collective-permute-start | bytes 110600 | tf_op jit(solution)/shard_map/ppermute | solution.py:578
  60.3 2.4 %collective-permute-start.42 = (f32[72,128]{1,0:T(8,128)S(1)}, f32[72,128]{1,0:T(8,128)S(1)}, u32[]{:S(2)}, u32[]{:S(2)}) collective-permute-start(f32[72,128]{1,0:T(8,128)S(1)} %add_add_fusion.3), channel_id=1, source_target_pairs={{0,2},{1,3},{2,0},{3,1},{4,6},{5,7},{6,4},{7,5},{8,10},{9,11},{10,... | collective-permute-start | bytes 110600 | tf_op jit(solution)/shard_map/ppermute | solution.py:578
  65.2 3.3 %collective-permute-done.43 = f32[72,128]{1,0:T(8,128)S(1)} collective-permute-done((f32[72,128]{1,0:T(8,128)S(1)}, f32[72,128]{1,0:T(8,128)S(1)}, u32[]{:S(2)}, u32[]{:S(2)}) %collective-permute-start.43) | collective-permute-done | bytes 36896 | tf_op jit(solution)/shard_map/ppermute | solution.py:578
  69.9 29.6 %factors.3 = (f32[128,128]{1,0:T(8,128)S(1)}, f32[1,128]{1,0:T(1,128)S(1)}, f32[128,128]{1,0:T(8,128)S(1)}, f32[1,128]{1,0:T(1,128)S(1)}, s32[1]{0:T(128)S(4)}) custom-call(f32[72,128]{1,0:T(8,128)S(1)} %add_add_fusion.2.mine, f32[72,128]{1,0:T(8,128)S(1)} %collective-permute-done.44.other), custom_call_target="tpu_custom_call" | custom-call | flops 125829120 | bytes 131072 | tf_op jit(solution)/shard_map/factors/pallas_call | solution.py:183
  100.6 75.7 %conditional.1 = (f32[1024,128]{1,0:T(8,128)}) conditional(s32[]{:T(128)} %bitcast.6, (s32[1,32]{1,0:T(1,128)S(1)}, bf16[1024,128]{1,0:T(8,128)(2,1)S(1)}, s32[1,8]{1,0:T(1,128)S(1)}, bf16[32,256,256]{2,1,0:T(8,128)(2,1)}, bf16[24,256,256]{2,1,0:T(8,128)(2,1)}, /*index=5*/s32[1,8]{1,0:T(1,128)S(1)}, s32[1,24]{1,0:T(1,128)S(1)}, ...), branch_computations={%region_0.0_spmd, %region_1.0_spmd} | conditional | flops 428309504 | bytes 48027000 | solution.py:653
  100.8 2.0 %collective-permute-start = (bf16[1024,128]{1,0:T(8,128)(2,1)S(1)}, bf16[1024,128]{1,0:T(8,128)(2,1)S(1)}, u32[]{:S(2)}, u32[]{:S(2)}) collective-permute-start(bf16[1024,128]{1,0:T(8,128)(2,1)S(1)} %get-tuple-element.30.rows), channel_id=1, source_target_pairs={{0,2},{1,3},{2,0},{3,1},{4,6},{5,7},{6,4},{7,5},{8,10},{9,11},{10,... | collective-permute-start | bytes 786440 | tf_op jit(solution)/shard_map/cond/branch_0_fun/ppermute | solution.py:578
  106.2 2.4 %collective-permute-start.5 = (bf16[1040,128]{1,0:T(8,128)(2,1)S(1)}, bf16[1040,128]{1,0:T(8,128)(2,1)S(1)}, u32[]{:S(2)}, u32[]{:S(2)}) collective-permute-start(bf16[1040,128]{1,0:T(8,128)(2,1)S(1)} %prepare.3.refs_0_), channel_id=1, source_target_pairs={{0,24},{4,28},{8,16},{12,20},{16,8},{20,12},{24,0},{28,4},{1,25},{... | collective-permute-start | bytes 798728 | tf_op jit(solution)/shard_map/cond/branch_0_fun/ppermute | solution.py:578
  108.6 7.2 %collective-permute-done.x_ref.refs_2_.refs_1_ = bf16[1024,128]{1,0:T(8,128)(2,1)S(1)} collective-permute-done((bf16[1024,128]{1,0:T(8,128)(2,1)S(1)}, bf16[1024,128]{1,0:T(8,128)(2,1)S(1)}, u32[]{:S(2)}, u32[]{:S(2)}) %collective-permute-start) | collective-permute-done | bytes 262176 | tf_op jit(solution)/shard_map/cond/branch_0_fun/ppermute | solution.py:578
  116.9 3.2 %load.3 = (bf16[32,256,256]{2,1,0:T(8,128)(2,1)S(1)}, bf16[24,256,256]{2,1,0:T(8,128)(2,1)S(1)}) custom-call(bf16[32,256,256]{2,1,0:T(8,128)(2,1)} %get-tuple-element.31.refs_0_, bf16[24,256,256]{2,1,0:T(8,128)(2,1)} %get-tuple-element.32.refs_1_, bf16[1024,128]{1,0:T(8,128)(2,1)S(1)} %collective-permute-done.x_ref.refs_2_.refs_1_), custom_call_target="tpu_custom_call" | custom-call | bytes 14680064 | tf_op jit(solution)/shard_map/cond/branch_0_fun/load/pallas_call | solution.py:249
  127.6 2.5 %collective-permute-start.7 = (bf16[1024,128]{1,0:T(8,128)(2,1)S(1)}, bf16[1024,128]{1,0:T(8,128)(2,1)S(1)}, u32[]{:S(2)}, u32[]{:S(2)}) collective-permute-start(bf16[1024,128]{1,0:T(8,128)(2,1)S(1)} %fusion.rows), channel_id=1, source_target_pairs={{0,2},{1,3},{2,0},{3,1},{4,6},{5,7},{6,4},{7,5},{8,10},{9,11},{10,... | collective-permute-start | bytes 786440 | tf_op jit(solution)/shard_map/cond/branch_0_fun/ppermute | solution.py:578
  133.4 2.6 %collective-permute-start.12 = (bf16[1040,128]{1,0:T(8,128)(2,1)S(1)}, bf16[1040,128]{1,0:T(8,128)(2,1)S(1)}, u32[]{:S(2)}, u32[]{:S(2)}) collective-permute-start(bf16[1040,128]{1,0:T(8,128)(2,1)S(1)} %prepare.4.refs_0_), channel_id=1, source_target_pairs={{0,24},{4,28},{8,16},{12,20},{16,8},{20,12},{24,0},{28,4},{1,25},{... | collective-permute-start | bytes 798728 | tf_op jit(solution)/shard_map/cond/branch_0_fun/ppermute | solution.py:578
  135.9 6.7 %collective-permute-done.7.x_ref.refs_2_.refs_1_ = bf16[1024,128]{1,0:T(8,128)(2,1)S(1)} collective-permute-done((bf16[1024,128]{1,0:T(8,128)(2,1)S(1)}, bf16[1024,128]{1,0:T(8,128)(2,1)S(1)}, u32[]{:S(2)}, u32[]{:S(2)}) %collective-permute-start.7) | collective-permute-done | bytes 262176 | tf_op jit(solution)/shard_map/cond/branch_0_fun/ppermute | solution.py:578
  144.2 3.2 %load.4 = (bf16[32,256,256]{2,1,0:T(8,128)(2,1)S(1)}, bf16[24,256,256]{2,1,0:T(8,128)(2,1)S(1)}) custom-call(bf16[32,256,256]{2,1,0:T(8,128)(2,1)} %get-tuple-element.31.refs_0_, bf16[24,256,256]{2,1,0:T(8,128)(2,1)} %get-tuple-element.32.refs_1_, bf16[1024,128]{1,0:T(8,128)(2,1)S(1)} %collective-permute-done.7.x_ref.refs_2_.refs_1_), custom_call_target="tpu_custom_call" | custom-call | bytes 14680064 | tf_op jit(solution)/shard_map/cond/branch_0_fun/load/pallas_call | solution.py:249
  159.7 2.2 %collective-permute-done.17 = f32[72,128]{1,0:T(8,128)S(1)} collective-permute-done((f32[72,128]{1,0:T(8,128)S(1)}, f32[72,128]{1,0:T(8,128)S(1)}, u32[]{:S(2)}, u32[]{:S(2)}) %collective-permute-start.17) | collective-permute-done | bytes 36896 | tf_op jit(solution)/shard_map/cond/branch_0_fun/ppermute | solution.py:578
  162.4 2.6 %collective-permute-start.19 = (f32[72,128]{1,0:T(8,128)S(1)}, f32[72,128]{1,0:T(8,128)S(1)}, u32[]{:S(2)}, u32[]{:S(2)}) collective-permute-start(f32[72,128]{1,0:T(8,128)S(1)} %add_add_fusion.1), channel_id=1, source_target_pairs={{0,2},{1,3},{2,0},{3,1},{4,6},{5,7},{6,4},{7,5},{8,10},{9,11},{10,... | collective-permute-start | bytes 110600 | tf_op jit(solution)/shard_map/cond/branch_0_fun/ppermute | solution.py:578
  168.5 2.4 %collective-permute-done.20 = f32[72,128]{1,0:T(8,128)S(1)} collective-permute-done((f32[72,128]{1,0:T(8,128)S(1)}, f32[72,128]{1,0:T(8,128)S(1)}, u32[]{:S(2)}, u32[]{:S(2)}) %collective-permute-start.20) | collective-permute-done | bytes 36896 | tf_op jit(solution)/shard_map/cond/branch_0_fun/ppermute | solution.py:578
  172.1 2.6 %factors.2 = (f32[128,128]{1,0:T(8,128)}, f32[1,128]{1,0:T(1,128)S(1)}, f32[128,128]{1,0:T(8,128)S(1)}, f32[1,128]{1,0:T(1,128)S(1)}, s32[1]{0:T(128)S(4)}) custom-call(f32[72,128]{1,0:T(8,128)S(1)} %add_add_fusion.mine, f32[72,128]{1,0:T(8,128)S(1)} %collective-permute-done.21.other), custom_call_target="tpu_custom_call" | custom-call | flops 125829120 | bytes 131072 | tf_op jit(solution)/shard_map/cond/branch_0_fun/factors/pallas_call | solution.py:183
  (116 shorter events, 70.9 us)
Async XLA Ops:
  0.0 16.3 %collective-permute-start.22 = (bf16[1024,128]{1,0:T(8,128)(2,1)}, bf16[1024,128]{1,0:T(8,128)(2,1)S(1)}, u32[]{:S(2)}, u32[]{:S(2)}) collective-permute-start(bf16[1024,128]{1,0:T(8,128)(2,1)} %rows.1), channel_id=1, source_target_pairs={{0,2},{1,3},{2,0},{3,1},{4,6},{5,7},{6,4},{7,5},{8,10},{9,11},{10,... | collective-permute-start | bytes 786440 | tf_op jit(solution)/shard_map/ppermute | solution.py:578
  4.0 12.4 %collective-permute-start.23 = (bf16[1024,128]{1,0:T(8,128)(2,1)}, bf16[1024,128]{1,0:T(8,128)(2,1)S(1)}, u32[]{:S(2)}, u32[]{:S(2)}) collective-permute-start(bf16[1024,128]{1,0:T(8,128)(2,1)} %rows.1), channel_id=1, source_target_pairs={{0,1},{1,0},{2,3},{3,2},{4,5},{5,4},{6,7},{7,6},{8,9},{9,8},{10,11... | collective-permute-start | bytes 786440 | tf_op jit(solution)/shard_map/ppermute | solution.py:578
  6.6 16.2 %collective-permute-start.25 = (bf16[1040,128]{1,0:T(8,128)(2,1)S(1)}, bf16[1040,128]{1,0:T(8,128)(2,1)S(1)}, u32[]{:S(2)}, u32[]{:S(2)}) collective-permute-start(bf16[1040,128]{1,0:T(8,128)(2,1)S(1)} %prepare.5.refs_0_), channel_id=1, source_target_pairs={{0,8},{4,12},{8,0},{12,4},{16,24},{20,28},{24,16},{28,20},{1,9},{5... | collective-permute-start | bytes 798728 | tf_op jit(solution)/shard_map/ppermute | solution.py:578
  8.2 14.6 %collective-permute-start.26 = (bf16[1040,128]{1,0:T(8,128)(2,1)S(1)}, bf16[1040,128]{1,0:T(8,128)(2,1)S(1)}, u32[]{:S(2)}, u32[]{:S(2)}) collective-permute-start(bf16[1040,128]{1,0:T(8,128)(2,1)S(1)} %prepare.5.refs_0_), channel_id=1, source_target_pairs={{0,16},{4,20},{8,24},{12,28},{16,0},{20,4},{24,8},{28,12},{1,17},{... | collective-permute-start | bytes 798728 | tf_op jit(solution)/shard_map/ppermute | solution.py:578
  9.7 13.1 %collective-permute-start.27 = (bf16[1040,128]{1,0:T(8,128)(2,1)S(1)}, bf16[1040,128]{1,0:T(8,128)(2,1)S(1)}, u32[]{:S(2)}, u32[]{:S(2)}) collective-permute-start(bf16[1040,128]{1,0:T(8,128)(2,1)S(1)} %prepare.5.refs_0_), channel_id=1, source_target_pairs={{0,24},{4,28},{8,16},{12,20},{16,8},{20,12},{24,0},{28,4},{1,25},{... | collective-permute-start | bytes 798728 | tf_op jit(solution)/shard_map/ppermute | solution.py:578
  16.5 7.3 %collective-permute-start.24 = (bf16[1024,128]{1,0:T(8,128)(2,1)S(1)}, bf16[1024,128]{1,0:T(8,128)(2,1)S(1)}, u32[]{:S(2)}, u32[]{:S(2)}) collective-permute-start(bf16[1024,128]{1,0:T(8,128)(2,1)S(1)} %relay.6), channel_id=1, source_target_pairs={{0,1},{1,0},{2,3},{3,2},{4,5},{5,4},{6,7},{7,6},{8,9},{9,8},{10,11... | collective-permute-start | bytes 786440 | tf_op jit(solution)/shard_map/ppermute | solution.py:578
  26.7 15.4 %collective-permute-start.30 = (bf16[1024,128]{1,0:T(8,128)(2,1)S(1)}, bf16[1024,128]{1,0:T(8,128)(2,1)S(1)}, u32[]{:S(2)}, u32[]{:S(2)}) collective-permute-start(bf16[1024,128]{1,0:T(8,128)(2,1)S(1)} %get-tuple-element.65.rounded.refs_0_), channel_id=1, source_target_pairs={{0,2},{1,3},{2,0},{3,1},{4,6},{5,7},{6,4},{7,5},{8,10},{9,11},{10,... | collective-permute-start | bytes 786440 | tf_op jit(solution)/shard_map/ppermute | solution.py:578
  29.8 12.4 %collective-permute-start.31 = (bf16[1024,128]{1,0:T(8,128)(2,1)S(1)}, bf16[1024,128]{1,0:T(8,128)(2,1)S(1)}, u32[]{:S(2)}, u32[]{:S(2)}) collective-permute-start(bf16[1024,128]{1,0:T(8,128)(2,1)S(1)} %get-tuple-element.65.rounded.refs_0_), channel_id=1, source_target_pairs={{0,1},{1,0},{2,3},{3,2},{4,5},{5,4},{6,7},{7,6},{8,9},{9,8},{10,11... | collective-permute-start | bytes 786440 | tf_op jit(solution)/shard_map/ppermute | solution.py:578
  33.7 7.8 %collective-permute-start.33 = (bf16[512,128]{1,0:T(8,128)(2,1)S(1)}, bf16[512,128]{1,0:T(8,128)(2,1)S(1)}, u32[]{:S(2)}, u32[]{:S(2)}) collective-permute-start(bf16[512,128]{1,0:T(8,128)(2,1)S(1)} %get-tuple-element.69), channel_id=1, source_target_pairs={{0,16},{4,20},{8,24},{12,28},{16,0},{20,4},{24,8},{28,12},{1,17},{... | collective-permute-start | bytes 393224 | tf_op jit(solution)/shard_map/ppermute | solution.py:578
  35.2 6.3 %collective-permute-start.34 = (bf16[512,128]{1,0:T(8,128)(2,1)S(1)}, bf16[512,128]{1,0:T(8,128)(2,1)S(1)}, u32[]{:S(2)}, u32[]{:S(2)}) collective-permute-start(bf16[512,128]{1,0:T(8,128)(2,1)S(1)} %get-tuple-element.70), channel_id=1, source_target_pairs={{0,24},{4,28},{8,16},{12,20},{16,8},{20,12},{24,0},{28,4},{1,25},{... | collective-permute-start | bytes 393224 | tf_op jit(solution)/shard_map/ppermute | solution.py:578
  42.3 8.8 %collective-permute-start.36 = (bf16[1024,128]{1,0:T(8,128)(2,1)S(1)}, bf16[1024,128]{1,0:T(8,128)(2,1)S(1)}, u32[]{:S(2)}, u32[]{:S(2)}) collective-permute-start(bf16[1024,128]{1,0:T(8,128)(2,1)S(1)} %relay.7), channel_id=1, source_target_pairs={{0,1},{1,0},{2,3},{3,2},{4,5},{5,4},{6,7},{7,6},{8,9},{9,8},{10,11... | collective-permute-start | bytes 786440 | tf_op jit(solution)/shard_map/ppermute | solution.py:578
  100.8 14.9 %collective-permute-start = (bf16[1024,128]{1,0:T(8,128)(2,1)S(1)}, bf16[1024,128]{1,0:T(8,128)(2,1)S(1)}, u32[]{:S(2)}, u32[]{:S(2)}) collective-permute-start(bf16[1024,128]{1,0:T(8,128)(2,1)S(1)} %get-tuple-element.30.rows), channel_id=1, source_target_pairs={{0,2},{1,3},{2,0},{3,1},{4,6},{5,7},{6,4},{7,5},{8,10},{9,11},{10,... | collective-permute-start | bytes 786440 | tf_op jit(solution)/shard_map/cond/branch_0_fun/ppermute | solution.py:578
  102.8 12.9 %collective-permute-start.1 = (bf16[1024,128]{1,0:T(8,128)(2,1)S(1)}, bf16[1024,128]{1,0:T(8,128)(2,1)S(1)}, u32[]{:S(2)}, u32[]{:S(2)}) collective-permute-start(bf16[1024,128]{1,0:T(8,128)(2,1)S(1)} %get-tuple-element.30.rows), channel_id=1, source_target_pairs={{0,1},{1,0},{2,3},{3,2},{4,5},{5,4},{6,7},{7,6},{8,9},{9,8},{10,11... | collective-permute-start | bytes 786440 | tf_op jit(solution)/shard_map/cond/branch_0_fun/ppermute | solution.py:578
  105.0 16.6 %collective-permute-start.3 = (bf16[1040,128]{1,0:T(8,128)(2,1)S(1)}, bf16[1040,128]{1,0:T(8,128)(2,1)S(1)}, u32[]{:S(2)}, u32[]{:S(2)}) collective-permute-start(bf16[1040,128]{1,0:T(8,128)(2,1)S(1)} %prepare.3.refs_0_), channel_id=1, source_target_pairs={{0,8},{4,12},{8,0},{12,4},{16,24},{20,28},{24,16},{28,20},{1,9},{5... | collective-permute-start | bytes 798728 | tf_op jit(solution)/shard_map/cond/branch_0_fun/ppermute | solution.py:578
  105.6 16.0 %collective-permute-start.4 = (bf16[1040,128]{1,0:T(8,128)(2,1)S(1)}, bf16[1040,128]{1,0:T(8,128)(2,1)S(1)}, u32[]{:S(2)}, u32[]{:S(2)}) collective-permute-start(bf16[1040,128]{1,0:T(8,128)(2,1)S(1)} %prepare.3.refs_0_), channel_id=1, source_target_pairs={{0,16},{4,20},{8,24},{12,28},{16,0},{20,4},{24,8},{28,12},{1,17},{... | collective-permute-start | bytes 798728 | tf_op jit(solution)/shard_map/cond/branch_0_fun/ppermute | solution.py:578
  106.2 15.5 %collective-permute-start.5 = (bf16[1040,128]{1,0:T(8,128)(2,1)S(1)}, bf16[1040,128]{1,0:T(8,128)(2,1)S(1)}, u32[]{:S(2)}, u32[]{:S(2)}) collective-permute-start(bf16[1040,128]{1,0:T(8,128)(2,1)S(1)} %prepare.3.refs_0_), channel_id=1, source_target_pairs={{0,24},{4,28},{8,16},{12,20},{16,8},{20,12},{24,0},{28,4},{1,25},{... | collective-permute-start | bytes 798728 | tf_op jit(solution)/shard_map/cond/branch_0_fun/ppermute | solution.py:578
  115.8 7.6 %collective-permute-start.2 = (bf16[1024,128]{1,0:T(8,128)(2,1)S(1)}, bf16[1024,128]{1,0:T(8,128)(2,1)S(1)}, u32[]{:S(2)}, u32[]{:S(2)}) collective-permute-start(bf16[1024,128]{1,0:T(8,128)(2,1)S(1)} %relay.4), channel_id=1, source_target_pairs={{0,1},{1,0},{2,3},{3,2},{4,5},{5,4},{6,7},{7,6},{8,9},{9,8},{10,11... | collective-permute-start | bytes 786440 | tf_op jit(solution)/shard_map/cond/branch_0_fun/ppermute | solution.py:578
  127.6 15.0 %collective-permute-start.7 = (bf16[1024,128]{1,0:T(8,128)(2,1)S(1)}, bf16[1024,128]{1,0:T(8,128)(2,1)S(1)}, u32[]{:S(2)}, u32[]{:S(2)}) collective-permute-start(bf16[1024,128]{1,0:T(8,128)(2,1)S(1)} %fusion.rows), channel_id=1, source_target_pairs={{0,2},{1,3},{2,0},{3,1},{4,6},{5,7},{6,4},{7,5},{8,10},{9,11},{10,... | collective-permute-start | bytes 786440 | tf_op jit(solution)/shard_map/cond/branch_0_fun/ppermute | solution.py:578
  130.1 12.7 %collective-permute-start.8 = (bf16[1024,128]{1,0:T(8,128)(2,1)S(1)}, bf16[1024,128]{1,0:T(8,128)(2,1)S(1)}, u32[]{:S(2)}, u32[]{:S(2)}) collective-permute-start(bf16[1024,128]{1,0:T(8,128)(2,1)S(1)} %fusion.rows), channel_id=1, source_target_pairs={{0,1},{1,0},{2,3},{3,2},{4,5},{5,4},{6,7},{7,6},{8,9},{9,8},{10,11... | collective-permute-start | bytes 786440 | tf_op jit(solution)/shard_map/cond/branch_0_fun/ppermute | solution.py:578
  132.4 16.5 %collective-permute-start.10 = (bf16[1040,128]{1,0:T(8,128)(2,1)S(1)}, bf16[1040,128]{1,0:T(8,128)(2,1)S(1)}, u32[]{:S(2)}, u32[]{:S(2)}) collective-permute-start(bf16[1040,128]{1,0:T(8,128)(2,1)S(1)} %prepare.4.refs_0_), channel_id=1, source_target_pairs={{0,8},{4,12},{8,0},{12,4},{16,24},{20,28},{24,16},{28,20},{1,9},{5... | collective-permute-start | bytes 798728 | tf_op jit(solution)/shard_map/cond/branch_0_fun/ppermute | solution.py:578
  132.8 16.1 %collective-permute-start.11 = (bf16[1040,128]{1,0:T(8,128)(2,1)S(1)}, bf16[1040,128]{1,0:T(8,128)(2,1)S(1)}, u32[]{:S(2)}, u32[]{:S(2)}) collective-permute-start(bf16[1040,128]{1,0:T(8,128)(2,1)S(1)} %prepare.4.refs_0_), channel_id=1, source_target_pairs={{0,16},{4,20},{8,24},{12,28},{16,0},{20,4},{24,8},{28,12},{1,17},{... | collective-permute-start | bytes 798728 | tf_op jit(solution)/shard_map/cond/branch_0_fun/ppermute | solution.py:578
  133.4 15.5 %collective-permute-start.12 = (bf16[1040,128]{1,0:T(8,128)(2,1)S(1)}, bf16[1040,128]{1,0:T(8,128)(2,1)S(1)}, u32[]{:S(2)}, u32[]{:S(2)}) collective-permute-start(bf16[1040,128]{1,0:T(8,128)(2,1)S(1)} %prepare.4.refs_0_), channel_id=1, source_target_pairs={{0,24},{4,28},{8,16},{12,20},{16,8},{20,12},{24,0},{28,4},{1,25},{... | collective-permute-start | bytes 798728 | tf_op jit(solution)/shard_map/cond/branch_0_fun/ppermute | solution.py:578
  142.8 7.5 %collective-permute-start.9 = (bf16[1024,128]{1,0:T(8,128)(2,1)S(1)}, bf16[1024,128]{1,0:T(8,128)(2,1)S(1)}, u32[]{:S(2)}, u32[]{:S(2)}) collective-permute-start(bf16[1024,128]{1,0:T(8,128)(2,1)S(1)} %relay.5), channel_id=1, source_target_pairs={{0,1},{1,0},{2,3},{3,2},{4,5},{5,4},{6,7},{7,6},{8,9},{9,8},{10,11... | collective-permute-start | bytes 786440 | tf_op jit(solution)/shard_map/cond/branch_0_fun/ppermute | solution.py:578
  162.4 6.1 %collective-permute-start.19 = (f32[72,128]{1,0:T(8,128)S(1)}, f32[72,128]{1,0:T(8,128)S(1)}, u32[]{:S(2)}, u32[]{:S(2)}) collective-permute-start(f32[72,128]{1,0:T(8,128)S(1)} %add_add_fusion.1), channel_id=1, source_target_pairs={{0,2},{1,3},{2,0},{3,1},{4,6},{5,7},{6,4},{7,5},{8,10},{9,11},{10,... | collective-permute-start | bytes 110600 | tf_op jit(solution)/shard_map/cond/branch_0_fun/ppermute | solution.py:578
  (25 other events, 147.6 us)
